TPU v7x, 128 devices: a whole 4x4x4 slice. The times are simulated.
128 devices in a mesh: fsdp: 16 (over z_hi, y, core), mp: 8 (over x, z_lo).
Axes of the slice: x: 4, y: 4, z: 4 (z_hi: 2, z_lo: 2; z = z_hi * 2 + z_lo), core: 2. Of those that a mesh axis runs over, the one named last changes fastest.
Arguments:
- tokens: bfloat16 [512, 16384], P('mp', 'fsdp'), may hold values from -6 to 6
- frozen_weights: bfloat16 [3, 26624, 16384], P(None, ('fsdp', 'mp')), may hold values from -0.046875 to 0.046875
- hidden_adapter_factor: bfloat16 [3, 26624, 64], P(None, ('fsdp', 'mp')), may hold values from -0.75 to 0.75
- feature_adapter_factor: bfloat16 [3, 64, 16384], P(None, None, ('fsdp', 'mp')), may hold values from -0.046875 to 0.046875
Outputs:
- block_out: bfloat16 [512, 16384], P('mp', 'fsdp')
All inputs are finite; a program needn't handle non-finite values.
Results may differ from a plain program's by a relative error of at most 0.038.
Values may be sent and summed in bfloat16 or wider, within the bound.
No kernel may reach another device: no remote copies, remote signals or barrier semaphores. Data moves between devices by JAX's collectives and lax.ppermute only.
A program may use at most 192 MiB of HBM per device.

v0:
```python
import jax
import jax.numpy as jnp
from jax import lax
from jax.sharding import PartitionSpec as P


def apply_adapter_update(weights, left_factor, right_factor):
    weight_update = jnp.einsum(
        "kfr,krd->kfd", left_factor, right_factor, preferred_element_type=jnp.float32
    )
    return (weights.astype(jnp.float32) + weight_update).astype(jnp.bfloat16)


def feature_product(input_tokens, weight_block):
    return lax.dot_general(
        input_tokens, weight_block, (((1,), (1,)), ((), ())), preferred_element_type=jnp.float32
    )


def per_device(tokens, frozen_weights, hidden_adapter_factor, feature_adapter_factor):
    feature_factor_full = lax.all_gather(feature_adapter_factor, ("fsdp", "mp"), axis=2, tiled=True)
    outgoing_block = apply_adapter_update(
        frozen_weights, hidden_adapter_factor, feature_factor_full
    )
    relaid = lax.all_to_all(outgoing_block, "fsdp", split_axis=2, concat_axis=1, tiled=True)
    whole_tok = lax.all_gather(tokens, "mp", axis=0, tiled=True)
    gate_part = feature_product(whole_tok, relaid[0])
    up_part = feature_product(whole_tok, relaid[1])
    gate_total, up_total = (
        lax.psum(gate_part.astype(jnp.bfloat16), "fsdp").astype(jnp.float32),
        lax.psum(up_part.astype(jnp.bfloat16), "fsdp").astype(jnp.float32),
    )
    hidden = (jax.nn.silu(gate_total) * up_total).astype(jnp.bfloat16)
    down_weight_block = relaid[2]
    return lax.psum_scatter(
        jnp.dot(hidden, down_weight_block, preferred_element_type=jnp.float32).astype(jnp.bfloat16),
        "mp",
        scatter_dimension=0,
        tiled=True,
    )


def solution(mesh):
    in_specs = (
        P("mp", "fsdp"),
        P(None, ("fsdp", "mp"), None),
        P(None, ("fsdp", "mp"), None),
        P(None, None, ("fsdp", "mp")),
    )
    out_specs = P("mp", "fsdp")
    return jax.shard_map(
        per_device, mesh=mesh, in_specs=in_specs, out_specs=out_specs, check_vma=False
    )
```

profile of v0, /device:TPU:38, one launch (start us, length us, event | category | flops | bytes accessed | tf_op | source)
XLA Modules:
  0.0 1070.3 jit_solution(16702357880315752007)
XLA Ops:
  7.4 0.0 copy-start
  7.4 0.0 all-gather.3.cloned.1.call-start
  7.4 0.7 all-gather.3.cloned.1.call-update
  8.1 269.2 %all-gather.3.cloned.1.call-done = bf16[3,64,16384]{2,1,0:T(8,128)(2,1)} async-done(((bf16[3,64,128]{2,1,0:T(8,128)(2,1)}), bf16[3,64,16384]{2,1,0:T(8,128)(2,1)}) %all-gather.3.cloned.1.call-update) | async-done | bytes 6291472 | tf_op jit(solution)/shard_map/all_gather | solution.py:21
  277.3 0.0 copy-done
  277.3 18.7 %add_convert_fusion = bf16[3,208,16384]{2,1,0:T(8,128)(2,1)} fusion(bf16[3,208,16384]{2,1,0:T(8,128)(2,1)} %param.5, bf16[3,208,64]{1,2,0:T(8,128)(2,1)S(1)} %copy-done, bf16[3,64,16384]{2,1,0:T(8,128)(2,1)} %all-gather.3.cloned.1.call-done), kind=kOutput, calls=%fused_computation | convolution fusion | flops 1339293696 | bytes 47265792 | tf_op jit(solution)/shard_map/kfr,krd->kfd/dot_general | solution.py:8
  296.0 47.6 %copy.7 = bf16[3,208,16384]{1,0,2:T(4,128)(2,1)} copy(bf16[3,208,16384]{2,1,0:T(8,128)(2,1)} %add_convert_fusion) | data formatting | bytes 40894464 | tf_op jit(solution)/shard_map/convert_element_type | solution.py:11
  343.6 5.9 all-to-all-start
  349.5 0.0 all-gather.5.cloned.1.call-start
  349.6 0.5 all-gather.5.cloned.1.call-update
  350.1 0.0 all-reduce.3.cloned.1.call-start
  350.1 431.2 %all-to-all-done = bf16[3,208,16384]{1,0,2:T(4,128)(2,1)} async-done(((bf16[3,208,16384]{1,0,2:T(4,128)(2,1)}), bf16[3,208,16384]{1,0,2:T(4,128)(2,1)}, u32[]{:S(2)}, u32[]{:S(2)}) %all-to-all-start) | async-done | bytes 20447264 | tf_op jit(solution)/shard_map/all_to_all | solution.py:25
  781.3 35.4 %copy.12 = bf16[3,208,16,1024]{3,2,1,0:T(8,128)(2,1)} copy(bf16[3,208,16,1024]{1,0,3,2:T(4,128)(2,1)} %bitcast) | data formatting | bytes 40894464 | tf_op jit(solution)/shard_map/all_to_all | solution.py:25
  816.7 10.4 fusion.13
  827.1 6.6 copy.9
  833.7 6.7 copy.10
  840.4 0.0 all-gather.5.cloned.1.call-done
  840.4 0.0 copy-start.2
  840.4 0.0 copy-start.3
  840.4 8.8 fusion.5
  849.3 0.0 copy-done.2
  849.3 0.0 copy-done.3
  849.3 5.5 fusion.6
  854.8 0.0 all-reduce.3.cloned.1.call-update
  854.8 0.0 reduce-scatter.2.cloned.1.call-start
  854.9 9.6 copy.11
  864.5 149.8 %all-reduce.3.cloned.1.call-done = (bf16[512,3328]{0,1:T(8,128)(2,1)}, bf16[512,3328]{0,1:T(8,128)(2,1)}) async-done(((bf16[512,3328]{0,1:T(8,128)(2,1)}, bf16[512,3328]{0,1:T(8,128)(2,1)}), (bf16[512,3328]{0,1:T(8,128)(2,1)}, bf16[512,3328]{0,1:T(8,128)(2,1)})) %all-reduce.3.cloned.1.call-update) | async-done | bytes 6815760 | tf_op jit(solution)/shard_map/psum | solution.py:31
  1014.3 0.0 copy-start.1
  1014.3 9.8 fusion.9
  1024.2 0.0 reduce-scatter.2.cloned.1.call-update
  1024.2 38.5 %reduce-scatter.2.cloned.1.call-done = bf16[64,1024]{1,0:T(8,128)(2,1)} async-done(((bf16[512,1024]{1,0:T(8,128)(2,1)}), bf16[64,1024]{1,0:T(8,128)(2,1)}) %reduce-scatter.2.cloned.1.call-update) | async-done | bytes 131088 | tf_op jit(solution)/shard_map/reduce_scatter | solution.py:35
  1062.7 0.0 copy-done.1
Async XLA Ops:
  7.4 269.9 %copy-start = (bf16[3,208,64]{1,2,0:T(8,128)(2,1)S(1)}, bf16[3,208,64]{1,2,0:T(8,128)(2,1)}, u32[]{:S(2)}) copy-start(bf16[3,208,64]{1,2,0:T(8,128)(2,1)} %param.6) | copy-start | bytes 239620
  7.4 269.9 %all-gather.3.cloned.1.call-start = ((), (), s32[]{:S(2)}) async-start(), calls=%async_computation.2 | async-start | bytes 6340608 | tf_op jit(solution)/shard_map/all_gather | solution.py:21
  343.6 437.7 %all-to-all-start = ((bf16[3,208,16384]{1,0,2:T(4,128)(2,1)}), bf16[3,208,16384]{1,0,2:T(4,128)(2,1)}, u32[]{:S(2)}, u32[]{:S(2)}) async-start(bf16[3,208,16384]{1,0,2:T(4,128)(2,1)} %copy.7), calls=%async_computation | async-start | bytes 67108864 | tf_op jit(solution)/shard_map/all_to_all | solution.py:25
  349.5 490.9 %all-gather.5.cloned.1.call-start = ((), (), s32[]{:S(2)}) async-start(), calls=%async_computation.3 | async-start | bytes 1179648 | tf_op jit(solution)/shard_map/all_gather | solution.py:26
  350.1 664.2 %all-reduce.3.cloned.1.call-start = ((), (), s32[]{:S(2)}) async-start(), calls=%async_computation.5 | async-start | bytes 13631488 | tf_op jit(solution)/shard_map/psum | solution.py:31
  840.4 8.8 copy-start.2
  840.4 8.8 copy-start.3
  854.8 207.9 %reduce-scatter.2.cloned.1.call-start = ((), (), s32[]{:S(2)}) async-start(), calls=%async_computation.4 | async-start | bytes 1179648 | tf_op jit(solution)/shard_map/reduce_scatter | solution.py:35
  1014.3 48.4 %copy-start.1 = (bf16[3,208,64]{1,2,0:T(8,128)(2,1)S(1)}, bf16[3,208,64]{1,2,0:T(8,128)(2,1)}, u32[]{:S(2)}) copy-start(bf16[3,208,64]{1,2,0:T(8,128)(2,1)} %param.6) | copy-start | bytes 239620
Sparse Core Ops, SparseCore 0:
  9.8 267.4 all-gather.2
Sparse Core Ops, SparseCore 1:
  351.6 126.6 all-gather.4
  854.9 159.4 all-reduce.2
  1024.3 38.4 reduce-scatter.1
where the time goes:
time: 1080 us; the launch traced here: 1070 us
  waiting for transfers between devices  890 us (82%)
  local copies, waits for them, and re-layouts  116 us (11%)
  matrix products  42.8 us (4%)
  between operations  15 us (1%)
    all_to_all x1, waiting for transfers between devices, per_device(): lax.all_to_all(outgoing_block, 'fsdp', split_axis=2, concat_axis=1, tiled...  431 us
    all_gather x1, waiting for transfers between devices, per_device(): lax.all_gather(feature_adapter_factor, ('fsdp', 'mp'), axis=2, tiled=True)  269 us
    psum x1, waiting for transfers between devices, per_device(): lax.psum(up_part.astype(jnp.bfloat16), 'fsdp').astype(jnp.float32)  150 us
    convert_element_type x1, local copies, waits for them, and re-layouts, apply_adapter_update(): return (weights.astype(jnp.float32) + weight_update).astype(jnp.bfloat16)  47.6 us
    reduce_scatter x1, waiting for transfers between devices, per_device(): lax.psum_scatter(jnp.dot(hidden, down_weight_block, preferred_element_typ...  38.5 us
    all_to_all x1, local copies, waits for them, and re-layouts, per_device(): lax.all_to_all(outgoing_block, 'fsdp', split_axis=2, concat_axis=1, tiled...  35.4 us
  transfers between devices with their start and end apart: 5, of which 4 were waited for; matrix products, arithmetic and copies ran while one was open for 6% of the time, Pallas kernels for 0%

commit v1 on v0

v1 whole, which is shorter than its diff:
```python
import jax
import jax.numpy as jnp
from jax import lax
from jax.experimental import pallas as pl
from jax.experimental.pallas import tpu as pltpu
from jax.sharding import Mesh, PartitionSpec as P

NAMES = ("zh", "y", "c", "x", "zl")
SIZES = (2, 4, 2, 4, 2)
ROWS = 208
TOK = 512
GROUP = 64
BLOCK = 1024
NB = 8
RANK = 64
WIDE = BLOCK + 128
PART = WIDE // 3
ORDERS = ((1, 2, 0), (2, 0, 1), (0, 1, 2))
VMEM = 60 * 1024 * 1024


def pairs(move):
    out = []
    for i in range(128):
        zh, y, c, x, zl = i // 64, i // 16 % 4, i // 8 % 2, i // 2 % 4, i % 2
        x, y, z, c = move(x, y, 2 * zh + zl, c)
        out.append((i, (((z // 2 * 4 + y) * 2 + c) * 4 + x) * 2 + z % 2))
    return out


def axis_pairs(axis, first):
    def move(x, y, z, c):
        q = [x, y, z]
        q[axis] ^= 1 if (c == 0) == first else 3
        return (*q, c)

    return pairs(move)


FIRST = [axis_pairs(a, True) for a in range(3)]
SECOND = [axis_pairs(a, False) for a in range(3)]
CORES = pairs(lambda x, y, z, c: (x, y, z, 1 - c))


def send(value, table):
    return lax.ppermute(value, NAMES, table)


def gather_part(value, order):
    value = value[None]
    for stage, axis in enumerate(order):
        mine = jnp.stack([value, send(value, FIRST[axis])])
        theirs = send(mine, SECOND[axis])
        if stage < 2:
            value = jnp.concatenate([mine, theirs]).reshape(-1, *value.shape[1:])
    return mine, theirs


def scatter_part(keep, away, order):
    for stage, axis in enumerate(order[::-1]):
        if stage > 0:
            keep, away = total.reshape(2, 2, -1, GROUP, PART)
        pair = keep + send(away, SECOND[axis])
        total = pair[0] + send(pair[1], FIRST[axis])
    return total.reshape(GROUP, PART)


def coordinate(place, k, core):
    return place ^ jnp.where(core == 0, (0, 1, 3, 2)[k], (0, 3, 1, 2)[k])


def relative(place, there, core):
    e = place ^ there
    zero = jnp.where(e == 1, 1, jnp.where(e == 3, 2, jnp.where(e == 2, 3, 0)))
    one = jnp.where(e == 3, 1, jnp.where(e == 1, 2, jnp.where(e == 2, 3, 0)))
    return jnp.where(core == 0, zero, one)


def split_kernel(place, w, out):
    out[...] = w[0]


def split(place, weights, k):
    return pl.pallas_call(
        split_kernel,
        out_shape=jax.ShapeDtypeStruct((ROWS, NB * BLOCK), jnp.bfloat16),
        grid_spec=pltpu.PrefetchScalarGridSpec(
            num_scalar_prefetch=1,
            grid=(NB,),
            in_specs=[pl.BlockSpec((1, ROWS, BLOCK), lambda j, s: (k, 0, 2 * j + 1 - s[0]))],
            out_specs=pl.BlockSpec((ROWS, BLOCK), lambda j, s: (0, j)),
        ),
        compiler_params=pltpu.CompilerParams(vmem_limit_bytes=VMEM),
        name="split",
    )(place, weights)


def dot_t(a, b):
    return lax.dot_general(a, b, (((1,), (1,)), ((), ())), preferred_element_type=jnp.float32)


def up_kernel(place, w, wg, wu, a_mine, a_other, *refs):
    blocks, (out, xs, acc, tacc, sems) = refs[:6], refs[6:]
    j = pl.program_id(0)
    core = place[0]

    @pl.when(j == 0)
    def _():
        at = [[coordinate(place[1 + a], k, core) for k in range(4)] for a in range(3)]
        for third in range(4):
            for second in range(4):
                for first in range(4):
                    for part, order in enumerate(ORDERS):
                        q = [None] * 3
                        q[order[0]], q[order[1]], q[order[2]] = (
                            at[order[0]][first], at[order[1]][second], at[order[2]][third],
                        )
                        x, y, z = q
                        block = (z // 2) * 4 + y
                        group = x * 2 + (z & 1)
                        pltpu.make_async_copy(
                            blocks[2 * part + third // 2].at[third % 2, second * 4 + first],
                            xs.at[
                                block,
                                pl.ds(pl.multiple_of(group * GROUP, GROUP), GROUP),
                                pl.ds(part * PART, PART),
                            ],
                            sems.at[block],
                        ).start()
        acc[...] = jnp.zeros_like(acc)
        tacc[...] = jnp.zeros_like(tacc)

    pltpu.make_async_copy(xs.at[j], xs.at[j], sems.at[j]).wait()
    x = xs[j, :, :BLOCK]
    acc[0] += dot_t(x, w[0])
    acc[1] += dot_t(x, w[1])
    acc[2] += dot_t(x, wg[...])
    acc[3] += dot_t(x, wu[...])
    tacc[...] += xs[j, :, BLOCK:].astype(jnp.float32)

    @pl.when(j == NB - 1)
    def _():
        t = tacc[...].astype(jnp.bfloat16)
        for side, a in enumerate((a_mine, a_other)):
            for k in range(2):
                low = dot_t(t[:, k * RANK : (k + 1) * RANK], a[k])
                out[side, k] = (acc[2 * side + k] + low).astype(jnp.bfloat16)


def up(place, weights, wg, wu, a_mine, a_other, blocks):
    any_spec = pl.BlockSpec(memory_space=pl.ANY)
    a_spec = pl.BlockSpec((3, ROWS, RANK), lambda j, s: (0, 0, 0))
    return pl.pallas_call(
        up_kernel,
        out_shape=jax.ShapeDtypeStruct((2, 2, TOK, ROWS), jnp.bfloat16),
        grid_spec=pltpu.PrefetchScalarGridSpec(
            num_scalar_prefetch=1,
            grid=(NB,),
            in_specs=[
                pl.BlockSpec((2, ROWS, BLOCK), lambda j, s: (0, 0, 2 * j + s[0])),
                pl.BlockSpec((ROWS, BLOCK), lambda j, s: (0, j)),
                pl.BlockSpec((ROWS, BLOCK), lambda j, s: (0, j)),
                a_spec,
                a_spec,
                *[any_spec] * 6,
            ],
            out_specs=pl.BlockSpec((2, 2, TOK, ROWS), lambda j, s: (0, 0, 0, 0)),
            scratch_shapes=[
                pltpu.VMEM((NB, TOK, WIDE), jnp.bfloat16),
                pltpu.VMEM((4, TOK, ROWS), jnp.float32),
                pltpu.VMEM((TOK, 128), jnp.float32),
                pltpu.SemaphoreType.DMA((NB,)),
            ],
        ),
        compiler_params=pltpu.CompilerParams(vmem_limit_bytes=VMEM),
        name="up",
    )(place, weights, wg, wu, a_mine, a_other, *blocks)


def down_kernel(place, mine, other, w, wd, a_mine, a_other, *refs):
    outs, (hidden, ob, sems) = refs[:6], refs[6:]
    j = pl.program_id(0)
    slot = lax.rem(j, 2)
    core = place[0]

    def drain(s):
        pltpu.make_async_copy(ob.at[s], ob.at[s], sems.at[s]).wait()

    @pl.when(j == 0)
    def _():
        for side in range(2):
            f32 = jnp.float32
            gate = mine[side, 0].astype(f32) + other[1 - side, 0].astype(f32)
            upper = mine[side, 1].astype(f32) + other[1 - side, 1].astype(f32)
            hidden[side] = (gate / (1.0 + jnp.exp(-gate)) * upper).astype(jnp.bfloat16)
        low = jnp.dot(hidden[0], a_mine[2], preferred_element_type=jnp.float32)
        low += jnp.dot(hidden[1], a_other[2], preferred_element_type=jnp.float32)
        for s in range(2):
            ob[s, :, BLOCK:] = jnp.concatenate([low, jnp.zeros_like(low)], axis=1).astype(jnp.bfloat16)

    @pl.when(j >= 2)
    def _():
        drain(slot)

    value = jnp.dot(hidden[0], w[0], preferred_element_type=jnp.float32)
    value += jnp.dot(hidden[1], wd[...], preferred_element_type=jnp.float32)
    ob[slot, :, :BLOCK] = value.astype(jnp.bfloat16)

    zh, y = j // 4, lax.rem(j, 4)
    rel_y = relative(place[2], y, core)
    for group in range(8):
        x, zl = group // 2, group % 2
        rel = (relative(place[1], x, core), rel_y, relative(place[3], 2 * zh + zl, core))
        for part, order in enumerate(ORDERS):
            first, second, third = (rel[a] for a in order)
            source = ob.at[slot, pl.ds(group * GROUP, GROUP), pl.ds(part * PART, PART)]
            for half in range(2):

                @pl.when(third // 2 == half)
                def _():
                    pltpu.make_async_copy(
                        source,
                        outs[2 * part + half].at[third % 2, second * 4 + first],
                        sems.at[slot],
                    ).start()

    @pl.when(j == NB - 1)
    def _():
        drain(0)
        drain(1)


def down(place, mine, other, weights, wd, a_mine, a_other):
    part_spec = pl.BlockSpec((2, 2, TOK, ROWS), lambda j, s: (0, 0, 0, 0))
    a_spec = pl.BlockSpec((3, ROWS, RANK), lambda j, s: (0, 0, 0))
    return pl.pallas_call(
        down_kernel,
        out_shape=[jax.ShapeDtypeStruct((2, 16, GROUP, PART), jnp.bfloat16)] * 6,
        grid_spec=pltpu.PrefetchScalarGridSpec(
            num_scalar_prefetch=1,
            grid=(NB,),
            in_specs=[
                part_spec,
                part_spec,
                pl.BlockSpec((1, ROWS, BLOCK), lambda j, s: (2, 0, 2 * j + s[0])),
                pl.BlockSpec((ROWS, BLOCK), lambda j, s: (0, j)),
                a_spec,
                a_spec,
            ],
            out_specs=[pl.BlockSpec(memory_space=pl.ANY)] * 6,
            scratch_shapes=[
                pltpu.VMEM((2, TOK, ROWS), jnp.bfloat16),
                pltpu.VMEM((2, TOK, WIDE), jnp.bfloat16),
                pltpu.SemaphoreType.DMA((2,)),
            ],
        ),
        compiler_params=pltpu.CompilerParams(vmem_limit_bytes=VMEM),
        name="down",
    )(place, mine, other, weights, wd, a_mine, a_other)


def group_features(factor, x, zl):
    flat = factor.reshape(3 * RANK, 128)
    across = []
    for step in range(4):
        got = flat if step == 0 else send(
            flat, pairs(lambda x, y, z, c: ((x + step) % 4, y, z, c))
        )
        across.append(got)
    wide = jnp.concatenate(across, axis=0)
    other = send(wide, pairs(lambda x, y, z, c: (x, y, z ^ 1, c)))
    out = jnp.zeros((3 * RANK, BLOCK), factor.dtype)
    for step in range(4):
        column = ((x - step) % 4) * 2
        rows = slice(step * 3 * RANK, (step + 1) * 3 * RANK)
        out = lax.dynamic_update_slice(out, wide[rows], (0, (column + zl) * 128))
        out = lax.dynamic_update_slice(out, other[rows], (0, (column + 1 - zl) * 128))
    return out


def per_device(tokens, frozen_weights, hidden_adapter_factor, feature_adapter_factor):
    zh, y, core, x, zl = (lax.axis_index(n) for n in NAMES)
    place = jnp.stack([core, x, y, 2 * zh + zl]).astype(jnp.int32)
    factor = group_features(feature_adapter_factor, x, zl)
    low = dot_t(tokens, factor[: 2 * RANK]).astype(jnp.bfloat16)
    parts = (
        tokens[:, :PART],
        tokens[:, PART : 2 * PART],
        jnp.concatenate([tokens[:, 2 * PART :], low], axis=1),
    )
    others = [send(split(place, frozen_weights, k), CORES) for k in range(3)]
    a_other = send(hidden_adapter_factor, CORES)
    blocks = [b for p, o in zip(parts, ORDERS) for b in gather_part(p, o)]
    mine = up(place, frozen_weights, others[0], others[1], hidden_adapter_factor, a_other, blocks)
    theirs = send(mine, CORES)
    sums = down(place, mine, theirs, frozen_weights, others[2], hidden_adapter_factor, a_other)
    left, middle, right = (
        scatter_part(sums[2 * p], sums[2 * p + 1], ORDERS[p]) for p in range(3)
    )
    last = BLOCK - 2 * PART
    plain = jnp.concatenate([left, middle, right[:, :last]], axis=1).astype(jnp.float32)
    extra = jnp.dot(
        right[:, last : last + RANK], factor[2 * RANK :], preferred_element_type=jnp.float32
    )
    return (plain + extra).astype(jnp.bfloat16)


def solution(mesh):
    fine = Mesh(mesh.devices.reshape(SIZES), NAMES)
    units = ("zh", "y", "c", "x", "zl")
    return jax.shard_map(
        per_device,
        mesh=fine,
        in_specs=(
            P(("x", "zl"), ("zh", "y", "c")),
            P(None, units, None),
            P(None, units, None),
            P(None, None, units),
        ),
        out_specs=P(("x", "zl"), ("zh", "y", "c")),
        check_vma=False,
    )
```

time: 1080 us -> 231 us (0.21)
  waiting for transfers between devices: 890 us -> 94.7 us
  local copies, waits for them, and re-layouts: 116 us -> 9.61 us
  starting transfers between devices: 6.07 us -> 59.8 us
  Pallas kernels: 0 us -> 51.7 us
  matrix products: 42.8 us -> 1.94 us
  between operations: 15 us -> 0.72 us
    all_to_all x1 -> x0, waiting for transfers between devices: 431 us -> none  [per_device(): lax.all_to_all(outgoing_block, 'fsdp', split_axis=2, concat_axis=1, tiled...]
    all_gather x2 -> x0, waiting for transfers between devices: 269 us -> none  [the longest x1 269 us: per_device(): lax.all_gather(feature_adapter_factor, ('fsdp', 'mp'), axis=2, tiled=True)]
    psum x1 -> x0, waiting for transfers between devices: 150 us -> none  [per_device(): lax.psum(up_part.astype(jnp.bfloat16), 'fsdp').astype(jnp.float32)]
    ppermute x0 -> x45, waiting for transfers between devices: none -> 94.7 us  [send(): return lax.ppermute(value, NAMES, table)]
    ppermute x0 -> x45, starting transfers between devices: none -> 59.8 us  [send(): return lax.ppermute(value, NAMES, table)]
    pallas_call x0 -> x5, Pallas kernels: none -> 51.7 us  [the longest x3 20.9 us: split(): pl.pallas_call(split_kernel, out_shape=jax.ShapeDtypeStruct((ROWS, NB * B...]
    convert_element_type x1 -> x0, local copies, waits for them, and re-layouts: 47.6 us -> none  [apply_adapter_update(): return (weights.astype(jnp.float32) + weight_update).astype(jnp.bfloat16)]
    dot_general x4 -> x2, matrix products: 42.8 us -> 1.94 us  [the longest x1 1.73 us: per_device(): jnp.dot(right[:, last:last + RANK], factor[2 * RANK:], preferred_element_...]
  transfers between devices with their start and end apart: 5 -> 45, of which waited for: 4 -> 20; matrix products, arithmetic and copies ran while one was open for 6% -> 7% of each run, Pallas kernels for 0% -> 17%
where the time goes in v1:
time: 231 us; the launch traced here: 228 us
  waiting for transfers between devices  94.7 us (41%)
  starting transfers between devices  59.8 us (26%)
  Pallas kernels  51.7 us (22%)
  other arithmetic  9.8 us (4%)
  local copies, waits for them, and re-layouts  9.61 us (4%)
    ppermute x45, waiting for transfers between devices, send(): return lax.ppermute(value, NAMES, table)  94.7 us
    ppermute x45, starting transfers between devices, send(): return lax.ppermute(value, NAMES, table)  59.8 us
    pallas_call x3, Pallas kernels, split(): pl.pallas_call(split_kernel, out_shape=jax.ShapeDtypeStruct((ROWS, NB * B...  20.9 us
    pallas_call x1, Pallas kernels, up(): pl.pallas_call(up_kernel, out_shape=jax.ShapeDtypeStruct((2, 2, TOK, ROWS...  17.8 us
    pallas_call x1, Pallas kernels, down(): pl.pallas_call(down_kernel, out_shape=[jax.ShapeDtypeStruct((2, 16, GROUP...  13 us
  transfers between devices with their start and end apart: 45, of which 20 were waited for; matrix products, arithmetic and copies ran while one was open for 7% of the time, Pallas kernels for 17%

profile of v1, /device:TPU:38, one launch (start us, length us, event | category | flops | bytes accessed | tf_op | source)
XLA Modules:
  0.0 228.3 jit_solution(5800237588714927137)
XLA Ops:
  1.9 2.1 collective-permute-start.15
  4.9 1.7 collective-permute-start.3
  8.5 2.0 collective-permute-start.18
  10.5 2.3 collective-permute-start.4
  12.8 2.0 collective-permute-start.10
  14.8 1.6 collective-permute-done.4
  17.5 1.9 collective-permute-start.11
  19.5 2.7 %collective-permute-done.5 = bf16[4,64,384]{2,1,0:T(8,128)(2,1)S(1)} collective-permute-done((bf16[4,64,384]{2,1,0:T(8,128)(2,1)S(1)}, bf16[4,64,384]{2,1,0:T(8,128)(2,1)S(1)}, u32[]{:S(2)}, u32[]{:S(2)}) %collective-permute-start.5) | collective-permute-done | bytes 196640 | tf_op jit(solution)/shard_map/ppermute | solution.py:46
  22.2 2.0 collective-permute-start.6
  24.3 5.8 %collective-permute-done.6 = bf16[2,4,64,384]{3,2,1,0:T(8,128)(2,1)S(1)} collective-permute-done((bf16[2,4,64,384]{3,2,1,0:T(8,128)(2,1)S(1)}, bf16[2,4,64,384]{3,2,1,0:T(8,128)(2,1)S(1)}, u32[]{:S(2)}, u32[]{:S(2)}) %collective-permute-start.6) | collective-permute-done | bytes 393248 | tf_op jit(solution)/shard_map/ppermute | solution.py:46
  30.9 1.8 collective-permute-start.19
  32.7 1.6 collective-permute-start.12
  34.3 12.7 %collective-permute-done.19 = bf16[1,64,384]{2,1,0:T(8,128)(2,1)S(1)} collective-permute-done((bf16[1,64,384]{2,1,0:T(8,128)(2,1)S(1)}, bf16[1,64,384]{2,1,0:T(8,128)(2,1)S(1)}, u32[]{:S(2)}, u32[]{:S(2)}) %collective-permute-start.19) | collective-permute-done | bytes 49184 | tf_op jit(solution)/shard_map/ppermute | solution.py:46
  47.0 1.6 collective-permute-start.20
  49.2 7.0 %split.3 = bf16[208,8192]{1,0:T(8,128)(2,1)} custom-call(s32[4]{0:T(128)} %pad_add_fusion.place, bf16[3,208,16384]{2,1,0:T(8,128)(2,1)} %w.9), custom_call_target="tpu_custom_call" | custom-call | tf_op jit(solution)/shard_map/split/pallas_call | solution.py:84
  56.2 7.0 %split.4 = bf16[208,8192]{1,0:T(8,128)(2,1)} custom-call(s32[4]{0:T(128)} %pad_add_fusion.place, bf16[3,208,16384]{2,1,0:T(8,128)(2,1)} %w.9), custom_call_target="tpu_custom_call" | custom-call | tf_op jit(solution)/shard_map/split/pallas_call | solution.py:84
  64.3 1.7 collective-permute-start.13
  68.2 1.8 collective-permute-start.8
  70.1 1.6 collective-permute-start.22
  71.7 7.0 %split.5 = bf16[208,8192]{1,0:T(8,128)(2,1)} custom-call(s32[4]{0:T(128)} %pad_add_fusion.place, bf16[3,208,16384]{2,1,0:T(8,128)(2,1)} %w.9), custom_call_target="tpu_custom_call" | custom-call | tf_op jit(solution)/shard_map/split/pallas_call | solution.py:84
  78.7 3.7 %collective-permute-done.22 = bf16[2,4,64,384]{3,2,1,0:T(8,128)(2,1)S(1)} collective-permute-done((bf16[2,4,64,384]{3,2,1,0:T(8,128)(2,1)S(1)}, bf16[2,4,64,384]{3,2,1,0:T(8,128)(2,1)S(1)}, u32[]{:S(2)}, u32[]{:S(2)}) %collective-permute-start.22) | collective-permute-done | bytes 393248 | tf_op jit(solution)/shard_map/ppermute | solution.py:46
  82.5 1.8 collective-permute-start.23
  86.8 7.9 %collective-permute-done.23 = bf16[16,64,384]{2,1,0:T(8,128)(2,1)} collective-permute-done((bf16[16,64,384]{2,1,0:T(8,128)(2,1)S(1)}, bf16[16,64,384]{2,1,0:T(8,128)(2,1)}, u32[]{:S(2)}, u32[]{:S(2)}) %collective-permute-start.23) | collective-permute-done | bytes 786464 | tf_op jit(solution)/shard_map/ppermute | solution.py:46
  96.1 2.0 collective-permute-start.14
  98.1 2.4 %collective-permute-start.24 = (bf16[2,16,64,384]{3,2,1,0:T(8,128)(2,1)S(1)}, bf16[2,16,64,384]{3,2,1,0:T(8,128)(2,1)S(1)}, u32[]{:S(2)}, u32[]{:S(2)}) collective-permute-start(bf16[2,16,64,384]{3,2,1,0:T(8,128)(2,1)S(1)} %pad_maximum_fusion.2.refs_4_), channel_id=1, source_target_pairs={{0,65},{1,64},{2,67},{3,66},{4,69},{5,68},{6,71},{7,70},{8,9},{9,8... | collective-permute-start | bytes 4718600 | tf_op jit(solution)/shard_map/ppermute | solution.py:46
  100.5 17.3 %collective-permute-done.14.refs_3_ = bf16[2,16,64,384]{3,2,1,0:T(8,128)(2,1)S(1)} collective-permute-done((bf16[2,16,64,384]{3,2,1,0:T(8,128)(2,1)S(1)}, bf16[2,16,64,384]{3,2,1,0:T(8,128)(2,1)S(1)}, u32[]{:S(2)}, u32[]{:S(2)}) %collective-permute-start.14) | collective-permute-done | bytes 1572896 | tf_op jit(solution)/shard_map/ppermute | solution.py:46
  120.1 17.8 %up.1.mine = bf16[2,2,512,208]{3,2,1,0:T(8,128)(2,1)} custom-call(s32[4]{0:T(128)} %pad_add_fusion.place, bf16[3,208,16384]{2,1,0:T(8,128)(2,1)} %w.9, bf16[208,8192]{1,0:T(8,128)(2,1)} %collective-permute-done.wg, bf16[208,8192]{1,0:T(8,128)(2,1)} %collective-permute-done.1.wu, bf16[3,208,64]{2,1,0:T(8,128)(2,1)} %copy-done.7, ...), custom_call_target="tpu_custom_call" | custom-call | tf_op jit(solution)/shard_map/up/pallas_call | solution.py:153
  137.9 1.5 copy.13
  139.7 2.4 %collective-permute-done.25 = bf16[2,2,512,208]{2,3,1,0:T(8,128)(2,1)S(1)} collective-permute-done((bf16[2,2,512,208]{2,3,1,0:T(8,128)(2,1)S(1)}, bf16[2,2,512,208]{2,3,1,0:T(8,128)(2,1)S(1)}, u32[]{:S(2)}, u32[]{:S(2)}) %collective-permute-start.25) | collective-permute-done | bytes 852000 | tf_op jit(solution)/shard_map/ppermute | solution.py:46
  143.3 13.0 %down.1 = (bf16[2,16,64,384]{3,2,1,0:T(8,128)(2,1)}, bf16[2,16,64,384]{3,2,1,0:T(8,128)(2,1)}, bf16[2,16,64,384]{3,2,1,0:T(8,128)(2,1)}, bf16[2,16,64,384]{3,2,1...) custom-call(s32[4]{0:T(128)} %pad_add_fusion.place, ...), custom_call_target="tpu_custom_call" | custom-call | tf_op jit(solution)/shard_map/down/pallas_call | solution.py:236
  156.3 2.4 %collective-permute-start.39 = (bf16[2,16,64,384]{3,2,1,0:T(8,128)(2,1)}, bf16[2,16,64,384]{3,2,1,0:T(8,128)(2,1)S(1)}, u32[]{:S(2)}, u32[]{:S(2)}) collective-permute-start(bf16[2,16,64,384]{3,2,1,0:T(8,128)(2,1)} %get-tuple-element.16), channel_id=1, source_target_pairs={{0,65},{1,64},{2,67},{3,66},{4,69},{5,68},{6,71},{7,70},{8,9},{9,8... | collective-permute-start | bytes 4718600 | tf_op jit(solution)/shard_map/ppermute | solution.py:46
  158.7 1.9 collective-permute-start.33
  161.7 15.6 %collective-permute-done.39 = bf16[2,16,64,384]{3,2,1,0:T(8,128)(2,1)S(1)} collective-permute-done((bf16[2,16,64,384]{3,2,1,0:T(8,128)(2,1)}, bf16[2,16,64,384]{3,2,1,0:T(8,128)(2,1)S(1)}, u32[]{:S(2)}, u32[]{:S(2)}) %collective-permute-start.39) | collective-permute-done | bytes 1572896 | tf_op jit(solution)/shard_map/ppermute | solution.py:46
  177.4 2.0 add.157
  179.4 3.3 %collective-permute-start.40 = (bf16[16,64,384]{2,1,0:T(8,128)(2,1)S(1)}, bf16[16,64,384]{2,1,0:T(8,128)(2,1)S(1)}, u32[]{:S(2)}, u32[]{:S(2)}) collective-permute-start(bf16[16,64,384]{2,1,0:T(8,128)(2,1)S(1)} %slice_bitcast_fusion), channel_id=1, source_target_pairs={{0,1},{1,0},{2,3},{3,2},{4,5},{5,4},{6,7},{7,6},{8,73},{9,72},{10,... | collective-permute-start | bytes 2359304 | tf_op jit(solution)/shard_map/ppermute | solution.py:46
  185.4 7.2 %collective-permute-done.40 = bf16[16,64,384]{2,1,0:T(8,128)(2,1)S(1)} collective-permute-done((bf16[16,64,384]{2,1,0:T(8,128)(2,1)S(1)}, bf16[16,64,384]{2,1,0:T(8,128)(2,1)S(1)}, u32[]{:S(2)}, u32[]{:S(2)}) %collective-permute-start.40) | collective-permute-done | bytes 786464 | tf_op jit(solution)/shard_map/ppermute | solution.py:46
  192.9 2.3 %collective-permute-start.41 = (bf16[2,4,64,384]{3,2,1,0:T(8,128)(2,1)S(1)}, bf16[2,4,64,384]{3,2,1,0:T(8,128)(2,1)S(1)}, u32[]{:S(2)}, u32[]{:S(2)}) collective-permute-start(bf16[2,4,64,384]{3,2,1,0:T(8,128)(2,1)S(1)} %bitcast.159), channel_id=1, source_target_pairs={{0,48},{1,49},{2,50},{3,51},{4,52},{5,53},{6,54},{7,55},{8,24},{9,... | collective-permute-start | bytes 1179656 | tf_op jit(solution)/shard_map/ppermute | solution.py:46
  195.2 2.1 collective-permute-done.34
  197.5 2.0 collective-permute-start.35
  199.6 2.9 %collective-permute-start.29 = (bf16[2,4,64,384]{3,2,1,0:T(8,128)(2,1)S(1)}, bf16[2,4,64,384]{3,2,1,0:T(8,128)(2,1)S(1)}, u32[]{:S(2)}, u32[]{:S(2)}) collective-permute-start(bf16[2,4,64,384]{3,2,1,0:T(8,128)(2,1)S(1)} %bitcast.161), channel_id=1, source_target_pairs={{0,65},{1,64},{2,67},{3,66},{4,69},{5,68},{6,71},{7,70},{8,9},{9,8... | collective-permute-start | bytes 1179656 | tf_op jit(solution)/shard_map/ppermute | solution.py:46
  204.0 3.1 %collective-permute-done.35 = bf16[2,4,64,384]{3,2,1,0:T(8,128)(2,1)S(1)} collective-permute-done((bf16[2,4,64,384]{3,2,1,0:T(8,128)(2,1)S(1)}, bf16[2,4,64,384]{3,2,1,0:T(8,128)(2,1)S(1)}, u32[]{:S(2)}, u32[]{:S(2)}) %collective-permute-start.35) | collective-permute-done | bytes 393248 | tf_op jit(solution)/shard_map/ppermute | solution.py:46
  207.3 2.2 collective-permute-done.29
  210.9 2.0 collective-permute-done.36
  213.0 3.4 %collective-permute-start.37 = (bf16[2,1,64,384]{3,2,1,0:T(8,128)(2,1)S(1)}, bf16[2,1,64,384]{3,2,1,0:T(8,128)(2,1)S(1)}, u32[]{:S(2)}, u32[]{:S(2)}) collective-permute-start(bf16[2,1,64,384]{3,2,1,0:T(8,128)(2,1)S(1)} %slice_bitcast_fusion.14), channel_id=1, source_target_pairs={{0,65},{1,64},{2,67},{3,66},{4,69},{5,68},{6,71},{7,70},{8,9},{9,8... | collective-permute-start | bytes 294920 | tf_op jit(solution)/shard_map/ppermute | solution.py:46
  216.5 1.5 collective-permute-start.31
  219.6 2.8 %collective-permute-done.31 = bf16[2,1,64,384]{3,2,1,0:T(8,128)(2,1)S(1)} collective-permute-done((bf16[2,1,64,384]{3,2,1,0:T(8,128)(2,1)S(1)}, bf16[2,1,64,384]{3,2,1,0:T(8,128)(2,1)S(1)}, u32[]{:S(2)}, u32[]{:S(2)}) %collective-permute-start.31) | collective-permute-done | bytes 98336 | tf_op jit(solution)/shard_map/ppermute | solution.py:46
  223.2 3.3 %collective-permute-done.32 = bf16[1,64,384]{2,1,0:T(8,128)(2,1)S(1)} collective-permute-done((bf16[1,64,384]{2,1,0:T(8,128)(2,1)S(1)}, bf16[1,64,384]{2,1,0:T(8,128)(2,1)S(1)}, u32[]{:S(2)}, u32[]{:S(2)}) %collective-permute-start.32) | collective-permute-done | bytes 49184 | tf_op jit(solution)/shard_map/ppermute | solution.py:46
  226.6 1.7 fusion
  (140 shorter events, 28.4 us)
Async XLA Ops:
  0.0 7.6 %collective-permute-start.17 = (bf16[192,128]{1,0:T(8,128)(2,1)}, bf16[192,128]{1,0:T(8,128)(2,1)S(1)}, u32[]{:S(2)}, u32[]{:S(2)}) collective-permute-start(bf16[192,128]{1,0:T(8,128)(2,1)} %bitcast.162), channel_id=1, source_target_pairs={{0,6},{1,7},{2,0},{3,1},{4,2},{5,3},{6,4},{7,5},{8,14},{9,15},{10,... | collective-permute-start | bytes 147464 | tf_op jit(solution)/shard_map/ppermute | solution.py:46
  0.8 6.8 %collective-permute-start.16 = (bf16[192,128]{1,0:T(8,128)(2,1)}, bf16[192,128]{1,0:T(8,128)(2,1)S(1)}, u32[]{:S(2)}, u32[]{:S(2)}) collective-permute-start(bf16[192,128]{1,0:T(8,128)(2,1)} %bitcast.163), channel_id=1, source_target_pairs={{0,4},{1,5},{2,6},{3,7},{4,0},{5,1},{6,2},{7,3},{8,12},{9,13},{10,... | collective-permute-start | bytes 147464 | tf_op jit(solution)/shard_map/ppermute | solution.py:46
  1.9 5.7 %collective-permute-start.15 = (bf16[192,128]{1,0:T(8,128)(2,1)}, bf16[192,128]{1,0:T(8,128)(2,1)S(1)}, u32[]{:S(2)}, u32[]{:S(2)}) collective-permute-start(bf16[192,128]{1,0:T(8,128)(2,1)} %bitcast.164), channel_id=1, source_target_pairs={{0,2},{1,3},{2,4},{3,5},{4,6},{5,7},{6,0},{7,1},{8,10},{9,11},{10,... | collective-permute-start | bytes 147464 | tf_op jit(solution)/shard_map/ppermute | solution.py:46
  4.9 5.6 %collective-permute-start.3 = (bf16[1,64,384]{2,1,0:T(8,128)(2,1)S(1)}, bf16[1,64,384]{2,1,0:T(8,128)(2,1)S(1)}, u32[]{:S(2)}, u32[]{:S(2)}) collective-permute-start(bf16[1,64,384]{2,1,0:T(8,128)(2,1)S(1)} %get-tuple-element.30), channel_id=1, source_target_pairs={{0,16},{1,17},{2,18},{3,19},{4,20},{5,21},{6,22},{7,23},{8,56},{9,... | collective-permute-start | bytes 147464 | tf_op jit(solution)/shard_map/ppermute | solution.py:46
  6.5 6.2 %collective-permute-start.9 = (bf16[1,64,384]{2,1,0:T(8,128)(2,1)S(1)}, bf16[1,64,384]{2,1,0:T(8,128)(2,1)S(1)}, u32[]{:S(2)}, u32[]{:S(2)}) collective-permute-start(bf16[1,64,384]{2,1,0:T(8,128)(2,1)S(1)} %get-tuple-element.31), channel_id=1, source_target_pairs={{0,1},{1,0},{2,3},{3,2},{4,5},{5,4},{6,7},{7,6},{8,73},{9,72},{10,... | collective-permute-start | bytes 147464 | tf_op jit(solution)/shard_map/ppermute | solution.py:46
  8.5 10.9 %collective-permute-start.18 = (bf16[768,128]{1,0:T(8,128)(2,1)S(1)}, bf16[768,128]{1,0:T(8,128)(2,1)S(1)}, u32[]{:S(2)}, u32[]{:S(2)}) collective-permute-start(bf16[768,128]{1,0:T(8,128)(2,1)S(1)} %pad_maximum_fusion.11), channel_id=1, source_target_pairs={{0,1},{1,0},{2,3},{3,2},{4,5},{5,4},{6,7},{7,6},{8,9},{9,8},{10,11... | collective-permute-start | bytes 589832 | tf_op jit(solution)/shard_map/ppermute | solution.py:46
  10.5 5.9 %collective-permute-start.4 = (bf16[2,1,64,384]{3,2,1,0:T(8,128)(2,1)S(1)}, bf16[2,1,64,384]{3,2,1,0:T(8,128)(2,1)S(1)}, u32[]{:S(2)}, u32[]{:S(2)}) collective-permute-start(bf16[2,1,64,384]{3,2,1,0:T(8,128)(2,1)S(1)} %pad_maximum_fusion.13), channel_id=1, source_target_pairs={{0,48},{1,49},{2,50},{3,51},{4,52},{5,53},{6,54},{7,55},{8,24},{9,... | collective-permute-start | bytes 294920 | tf_op jit(solution)/shard_map/ppermute | solution.py:46
  12.8 4.7 %collective-permute-start.10 = (bf16[2,1,64,384]{3,2,1,0:T(8,128)(2,1)S(1)}, bf16[2,1,64,384]{3,2,1,0:T(8,128)(2,1)S(1)}, u32[]{:S(2)}, u32[]{:S(2)}) collective-permute-start(bf16[2,1,64,384]{3,2,1,0:T(8,128)(2,1)S(1)} %pad_maximum_fusion.14), channel_id=1, source_target_pairs={{0,65},{1,64},{2,67},{3,66},{4,69},{5,68},{6,71},{7,70},{8,9},{9,8... | collective-permute-start | bytes 294920 | tf_op jit(solution)/shard_map/ppermute | solution.py:46
  16.4 5.7 %collective-permute-start.5 = (bf16[4,64,384]{2,1,0:T(8,128)(2,1)S(1)}, bf16[4,64,384]{2,1,0:T(8,128)(2,1)S(1)}, u32[]{:S(2)}, u32[]{:S(2)}) collective-permute-start(bf16[4,64,384]{2,1,0:T(8,128)(2,1)S(1)} %get-tuple-element.28), channel_id=1, source_target_pairs={{0,1},{1,0},{2,3},{3,2},{4,5},{5,4},{6,7},{7,6},{8,73},{9,72},{10,... | collective-permute-start | bytes 589832 | tf_op jit(solution)/shard_map/ppermute | solution.py:46
  17.5 13.1 %copy-start.11 = (bf16[64,1024]{1,0:T(8,128)(2,1)S(1)}, bf16[64,1024]{1,0:T(8,128)(2,1)}, u32[]{:S(2)}) copy-start(bf16[64,1024]{1,0:T(8,128)(2,1)} %param.4) | copy-start | bytes 393220
  17.5 15.1 %collective-permute-start.11 = (bf16[4,64,384]{2,1,0:T(8,128)(2,1)S(1)}, bf16[4,64,384]{2,1,0:T(8,128)(2,1)S(1)}, u32[]{:S(2)}, u32[]{:S(2)}) collective-permute-start(bf16[4,64,384]{2,1,0:T(8,128)(2,1)S(1)} %get-tuple-element.26), channel_id=1, source_target_pairs={{0,2},{1,3},{2,0},{3,1},{4,6},{5,7},{6,4},{7,5},{8,14},{9,15},{10,... | collective-permute-start | bytes 589832 | tf_op jit(solution)/shard_map/ppermute | solution.py:46
  22.2 7.9 %collective-permute-start.6 = (bf16[2,4,64,384]{3,2,1,0:T(8,128)(2,1)S(1)}, bf16[2,4,64,384]{3,2,1,0:T(8,128)(2,1)S(1)}, u32[]{:S(2)}, u32[]{:S(2)}) collective-permute-start(bf16[2,4,64,384]{3,2,1,0:T(8,128)(2,1)S(1)} %pad_maximum_fusion.6), channel_id=1, source_target_pairs={{0,65},{1,64},{2,67},{3,66},{4,69},{5,68},{6,71},{7,70},{8,9},{9,8... | collective-permute-start | bytes 1179656 | tf_op jit(solution)/shard_map/ppermute | solution.py:46
  30.2 35.8 %collective-permute-start.7 = (bf16[16,64,384]{2,1,0:T(8,128)(2,1)S(1)}, bf16[16,64,384]{2,1,0:T(8,128)(2,1)S(1)}, u32[]{:S(2)}, u32[]{:S(2)}) collective-permute-start(bf16[16,64,384]{2,1,0:T(8,128)(2,1)S(1)} %bitcast.143), channel_id=1, source_target_pairs={{0,2},{1,3},{2,0},{3,1},{4,6},{5,7},{6,4},{7,5},{8,14},{9,15},{10,... | collective-permute-start | bytes 2359304 | tf_op jit(solution)/shard_map/ppermute | solution.py:46
  30.9 16.1 %collective-permute-start.19 = (bf16[1,64,384]{2,1,0:T(8,128)(2,1)S(1)}, bf16[1,64,384]{2,1,0:T(8,128)(2,1)S(1)}, u32[]{:S(2)}, u32[]{:S(2)}) collective-permute-start(bf16[1,64,384]{2,1,0:T(8,128)(2,1)S(1)} %get-tuple-element.34), channel_id=1, source_target_pairs={{0,2},{1,3},{2,0},{3,1},{4,6},{5,7},{6,4},{7,5},{8,14},{9,15},{10,... | collective-permute-start | bytes 147464 | tf_op jit(solution)/shard_map/ppermute | solution.py:46
  32.7 31.5 %collective-permute-start.12 = (bf16[2,4,64,384]{3,2,1,0:T(8,128)(2,1)S(1)}, bf16[2,4,64,384]{3,2,1,0:T(8,128)(2,1)S(1)}, u32[]{:S(2)}, u32[]{:S(2)}) collective-permute-start(bf16[2,4,64,384]{3,2,1,0:T(8,128)(2,1)S(1)} %pad_maximum_fusion.7), channel_id=1, source_target_pairs={{0,6},{1,7},{2,4},{3,5},{4,2},{5,3},{6,0},{7,1},{8,10},{9,11},{10,... | collective-permute-start | bytes 1179656 | tf_op jit(solution)/shard_map/ppermute | solution.py:46
  47.0 16.7 %collective-permute-start.20 = (bf16[2,1,64,384]{3,2,1,0:T(8,128)(2,1)S(1)}, bf16[2,1,64,384]{3,2,1,0:T(8,128)(2,1)S(1)}, u32[]{:S(2)}, u32[]{:S(2)}) collective-permute-start(bf16[2,1,64,384]{3,2,1,0:T(8,128)(2,1)S(1)} %pad_maximum_fusion.15), channel_id=1, source_target_pairs={{0,6},{1,7},{2,4},{3,5},{4,2},{5,3},{6,0},{7,1},{8,10},{9,11},{10,... | collective-permute-start | bytes 294920 | tf_op jit(solution)/shard_map/ppermute | solution.py:46
  56.2 62.7 %collective-permute-start = (bf16[208,8192]{1,0:T(8,128)(2,1)}, bf16[208,8192]{1,0:T(8,128)(2,1)}, u32[]{:S(2)}, u32[]{:S(2)}) collective-permute-start(bf16[208,8192]{1,0:T(8,128)(2,1)} %split.3), channel_id=1, source_target_pairs={{0,8},{1,9},{2,10},{3,11},{4,12},{5,13},{6,14},{7,15},{8,0},{9,1},... | collective-permute-start | bytes 10223624 | tf_op jit(solution)/shard_map/ppermute | solution.py:46
  63.2 55.7 %collective-permute-start.1 = (bf16[208,8192]{1,0:T(8,128)(2,1)}, bf16[208,8192]{1,0:T(8,128)(2,1)}, u32[]{:S(2)}, u32[]{:S(2)}) collective-permute-start(bf16[208,8192]{1,0:T(8,128)(2,1)} %split.4), channel_id=1, source_target_pairs={{0,8},{1,9},{2,10},{3,11},{4,12},{5,13},{6,14},{7,15},{8,0},{9,1},... | collective-permute-start | bytes 10223624 | tf_op jit(solution)/shard_map/ppermute | solution.py:46
  63.7 6.3 %collective-permute-start.21 = (bf16[4,64,384]{2,1,0:T(8,128)(2,1)S(1)}, bf16[4,64,384]{2,1,0:T(8,128)(2,1)S(1)}, u32[]{:S(2)}, u32[]{:S(2)}) collective-permute-start(bf16[4,64,384]{2,1,0:T(8,128)(2,1)S(1)} %get-tuple-element.24), channel_id=1, source_target_pairs={{0,16},{1,17},{2,18},{3,19},{4,20},{5,21},{6,22},{7,23},{8,56},{9,... | collective-permute-start | bytes 589832 | tf_op jit(solution)/shard_map/ppermute | solution.py:46
  64.3 18.2 %collective-permute-start.13 = (bf16[16,64,384]{2,1,0:T(8,128)(2,1)S(1)}, bf16[16,64,384]{2,1,0:T(8,128)(2,1)}, u32[]{:S(2)}, u32[]{:S(2)}) collective-permute-start(bf16[16,64,384]{2,1,0:T(8,128)(2,1)S(1)} %bitcast.145), channel_id=1, source_target_pairs={{0,16},{1,17},{2,18},{3,19},{4,20},{5,21},{6,22},{7,23},{8,56},{9,... | collective-permute-start | bytes 2359304 | tf_op jit(solution)/shard_map/ppermute | solution.py:46
  68.2 29.9 %collective-permute-start.8 = (bf16[2,16,64,384]{3,2,1,0:T(8,128)(2,1)S(1)}, bf16[2,16,64,384]{3,2,1,0:T(8,128)(2,1)}, u32[]{:S(2)}, u32[]{:S(2)}) collective-permute-start(bf16[2,16,64,384]{3,2,1,0:T(8,128)(2,1)S(1)} %pad_maximum_fusion.refs_0_), channel_id=1, source_target_pairs={{0,6},{1,7},{2,4},{3,5},{4,2},{5,3},{6,0},{7,1},{8,10},{9,11},{10,... | collective-permute-start | bytes 4718600 | tf_op jit(solution)/shard_map/ppermute | solution.py:46
  70.1 12.3 %collective-permute-start.22 = (bf16[2,4,64,384]{3,2,1,0:T(8,128)(2,1)S(1)}, bf16[2,4,64,384]{3,2,1,0:T(8,128)(2,1)S(1)}, u32[]{:S(2)}, u32[]{:S(2)}) collective-permute-start(bf16[2,4,64,384]{3,2,1,0:T(8,128)(2,1)S(1)} %pad_maximum_fusion.8), channel_id=1, source_target_pairs={{0,48},{1,49},{2,50},{3,51},{4,52},{5,53},{6,54},{7,55},{8,24},{9,... | collective-permute-start | bytes 1179656 | tf_op jit(solution)/shard_map/ppermute | solution.py:46
  82.4 61.0 %collective-permute-start.26 = (bf16[208,8192]{1,0:T(8,128)(2,1)}, bf16[208,8192]{1,0:T(8,128)(2,1)}, u32[]{:S(2)}, u32[]{:S(2)}) collective-permute-start(bf16[208,8192]{1,0:T(8,128)(2,1)} %split.5), channel_id=1, source_target_pairs={{0,8},{1,9},{2,10},{3,11},{4,12},{5,13},{6,14},{7,15},{8,0},{9,1},... | collective-permute-start | bytes 10223624 | tf_op jit(solution)/shard_map/ppermute | solution.py:46
  82.5 12.2 %collective-permute-start.23 = (bf16[16,64,384]{2,1,0:T(8,128)(2,1)S(1)}, bf16[16,64,384]{2,1,0:T(8,128)(2,1)}, u32[]{:S(2)}, u32[]{:S(2)}) collective-permute-start(bf16[16,64,384]{2,1,0:T(8,128)(2,1)S(1)} %bitcast.147), channel_id=1, source_target_pairs={{0,1},{1,0},{2,3},{3,2},{4,5},{5,4},{6,7},{7,6},{8,73},{9,72},{10,... | collective-permute-start | bytes 2359304 | tf_op jit(solution)/shard_map/ppermute | solution.py:46
  94.7 1.4 collective-permute-start.2
  96.1 21.7 %copy-start.2 = (bf16[2,16,64,384]{3,2,1,0:T(8,128)(2,1)}, bf16[2,16,64,384]{3,2,1,0:T(8,128)(2,1)S(1)}, u32[]{:S(2)}) copy-start(bf16[2,16,64,384]{3,2,1,0:T(8,128)(2,1)S(1)} %pad_maximum_fusion.2.refs_4_) | copy-start | bytes 4718596
  96.1 22.8 %copy-start.9 = (bf16[3,208,64]{2,1,0:T(8,128)(2,1)}, bf16[3,208,64]{2,1,0:T(8,128)(2,1)S(1)}, u32[]{:S(2)}) copy-start(bf16[3,208,64]{2,1,0:T(8,128)(2,1)S(1)} %collective-permute-done.2.a_other) | copy-start | bytes 239620
  96.1 21.7 %collective-permute-start.14 = (bf16[2,16,64,384]{3,2,1,0:T(8,128)(2,1)S(1)}, bf16[2,16,64,384]{3,2,1,0:T(8,128)(2,1)S(1)}, u32[]{:S(2)}, u32[]{:S(2)}) collective-permute-start(bf16[2,16,64,384]{3,2,1,0:T(8,128)(2,1)S(1)} %pad_maximum_fusion.1.refs_2_), channel_id=1, source_target_pairs={{0,48},{1,49},{2,50},{3,51},{4,52},{5,53},{6,54},{7,55},{8,24},{9,... | collective-permute-start | bytes 4718600 | tf_op jit(solution)/shard_map/ppermute | solution.py:46
  98.1 20.8 %collective-permute-start.24 = (bf16[2,16,64,384]{3,2,1,0:T(8,128)(2,1)S(1)}, bf16[2,16,64,384]{3,2,1,0:T(8,128)(2,1)S(1)}, u32[]{:S(2)}, u32[]{:S(2)}) collective-permute-start(bf16[2,16,64,384]{3,2,1,0:T(8,128)(2,1)S(1)} %pad_maximum_fusion.2.refs_4_), channel_id=1, source_target_pairs={{0,65},{1,64},{2,67},{3,66},{4,69},{5,68},{6,71},{7,70},{8,9},{9,8... | collective-permute-start | bytes 4718600 | tf_op jit(solution)/shard_map/ppermute | solution.py:46
  139.4 2.6 %collective-permute-start.25 = (bf16[2,2,512,208]{2,3,1,0:T(8,128)(2,1)S(1)}, bf16[2,2,512,208]{2,3,1,0:T(8,128)(2,1)S(1)}, u32[]{:S(2)}, u32[]{:S(2)}) collective-permute-start(bf16[2,2,512,208]{2,3,1,0:T(8,128)(2,1)S(1)} %copy.13), channel_id=1, source_target_pairs={{0,8},{1,9},{2,10},{3,11},{4,12},{5,13},{6,14},{7,15},{8,0},{9,1},... | collective-permute-start | bytes 2555912 | tf_op jit(solution)/shard_map/ppermute | solution.py:46
  156.3 21.0 %collective-permute-start.39 = (bf16[2,16,64,384]{3,2,1,0:T(8,128)(2,1)}, bf16[2,16,64,384]{3,2,1,0:T(8,128)(2,1)S(1)}, u32[]{:S(2)}, u32[]{:S(2)}) collective-permute-start(bf16[2,16,64,384]{3,2,1,0:T(8,128)(2,1)} %get-tuple-element.16), channel_id=1, source_target_pairs={{0,65},{1,64},{2,67},{3,66},{4,69},{5,68},{6,71},{7,70},{8,9},{9,8... | collective-permute-start | bytes 4718600 | tf_op jit(solution)/shard_map/ppermute | solution.py:46
  158.7 24.0 %collective-permute-start.33 = (bf16[2,16,64,384]{3,2,1,0:T(8,128)(2,1)}, bf16[2,16,64,384]{3,2,1,0:T(8,128)(2,1)S(1)}, u32[]{:S(2)}, u32[]{:S(2)}) collective-permute-start(bf16[2,16,64,384]{3,2,1,0:T(8,128)(2,1)} %get-tuple-element.14), channel_id=1, source_target_pairs={{0,48},{1,49},{2,50},{3,51},{4,52},{5,53},{6,54},{7,55},{8,24},{9,... | collective-permute-start | bytes 4718600 | tf_op jit(solution)/shard_map/ppermute | solution.py:46
  160.6 22.8 %collective-permute-start.27 = (bf16[2,16,64,384]{3,2,1,0:T(8,128)(2,1)}, bf16[2,16,64,384]{3,2,1,0:T(8,128)(2,1)S(1)}, u32[]{:S(2)}, u32[]{:S(2)}) collective-permute-start(bf16[2,16,64,384]{3,2,1,0:T(8,128)(2,1)} %get-tuple-element.12), channel_id=1, source_target_pairs={{0,6},{1,7},{2,4},{3,5},{4,2},{5,3},{6,0},{7,1},{8,10},{9,11},{10,... | collective-permute-start | bytes 4718600 | tf_op jit(solution)/shard_map/ppermute | solution.py:46
  179.4 13.3 %collective-permute-start.40 = (bf16[16,64,384]{2,1,0:T(8,128)(2,1)S(1)}, bf16[16,64,384]{2,1,0:T(8,128)(2,1)S(1)}, u32[]{:S(2)}, u32[]{:S(2)}) collective-permute-start(bf16[16,64,384]{2,1,0:T(8,128)(2,1)S(1)} %slice_bitcast_fusion), channel_id=1, source_target_pairs={{0,1},{1,0},{2,3},{3,2},{4,5},{5,4},{6,7},{7,6},{8,73},{9,72},{10,... | collective-permute-start | bytes 2359304 | tf_op jit(solution)/shard_map/ppermute | solution.py:46
  183.4 13.9 %collective-permute-start.34 = (bf16[16,64,384]{2,1,0:T(8,128)(2,1)S(1)}, bf16[16,64,384]{2,1,0:T(8,128)(2,1)S(1)}, u32[]{:S(2)}, u32[]{:S(2)}) collective-permute-start(bf16[16,64,384]{2,1,0:T(8,128)(2,1)S(1)} %slice_bitcast_fusion.2), channel_id=1, source_target_pairs={{0,16},{1,17},{2,18},{3,19},{4,20},{5,21},{6,22},{7,23},{8,56},{9,... | collective-permute-start | bytes 2359304 | tf_op jit(solution)/shard_map/ppermute | solution.py:46
  185.3 14.1 %collective-permute-start.28 = (bf16[16,64,384]{2,1,0:T(8,128)(2,1)S(1)}, bf16[16,64,384]{2,1,0:T(8,128)(2,1)S(1)}, u32[]{:S(2)}, u32[]{:S(2)}) collective-permute-start(bf16[16,64,384]{2,1,0:T(8,128)(2,1)S(1)} %slice_bitcast_fusion.4), channel_id=1, source_target_pairs={{0,2},{1,3},{2,0},{3,1},{4,6},{5,7},{6,4},{7,5},{8,14},{9,15},{10,... | collective-permute-start | bytes 2359304 | tf_op jit(solution)/shard_map/ppermute | solution.py:46
  192.9 9.7 %collective-permute-start.41 = (bf16[2,4,64,384]{3,2,1,0:T(8,128)(2,1)S(1)}, bf16[2,4,64,384]{3,2,1,0:T(8,128)(2,1)S(1)}, u32[]{:S(2)}, u32[]{:S(2)}) collective-permute-start(bf16[2,4,64,384]{3,2,1,0:T(8,128)(2,1)S(1)} %bitcast.159), channel_id=1, source_target_pairs={{0,48},{1,49},{2,50},{3,51},{4,52},{5,53},{6,54},{7,55},{8,24},{9,... | collective-permute-start | bytes 1179656 | tf_op jit(solution)/shard_map/ppermute | solution.py:46
  197.5 9.6 %collective-permute-start.35 = (bf16[2,4,64,384]{3,2,1,0:T(8,128)(2,1)S(1)}, bf16[2,4,64,384]{3,2,1,0:T(8,128)(2,1)S(1)}, u32[]{:S(2)}, u32[]{:S(2)}) collective-permute-start(bf16[2,4,64,384]{3,2,1,0:T(8,128)(2,1)S(1)} %bitcast.160), channel_id=1, source_target_pairs={{0,6},{1,7},{2,4},{3,5},{4,2},{5,3},{6,0},{7,1},{8,10},{9,11},{10,... | collective-permute-start | bytes 1179656 | tf_op jit(solution)/shard_map/ppermute | solution.py:46
  199.6 9.9 %collective-permute-start.29 = (bf16[2,4,64,384]{3,2,1,0:T(8,128)(2,1)S(1)}, bf16[2,4,64,384]{3,2,1,0:T(8,128)(2,1)S(1)}, u32[]{:S(2)}, u32[]{:S(2)}) collective-permute-start(bf16[2,4,64,384]{3,2,1,0:T(8,128)(2,1)S(1)} %bitcast.161), channel_id=1, source_target_pairs={{0,65},{1,64},{2,67},{3,66},{4,69},{5,68},{6,71},{7,70},{8,9},{9,8... | collective-permute-start | bytes 1179656 | tf_op jit(solution)/shard_map/ppermute | solution.py:46
  202.7 7.1 %collective-permute-start.42 = (bf16[4,64,384]{2,1,0:T(8,128)(2,1)S(1)}, bf16[4,64,384]{2,1,0:T(8,128)(2,1)S(1)}, u32[]{:S(2)}, u32[]{:S(2)}) collective-permute-start(bf16[4,64,384]{2,1,0:T(8,128)(2,1)S(1)} %slice_bitcast_fusion.6), channel_id=1, source_target_pairs={{0,16},{1,17},{2,18},{3,19},{4,20},{5,21},{6,22},{7,23},{8,56},{9,... | collective-permute-start | bytes 589832 | tf_op jit(solution)/shard_map/ppermute | solution.py:46
  207.2 5.7 %collective-permute-start.36 = (bf16[4,64,384]{2,1,0:T(8,128)(2,1)S(1)}, bf16[4,64,384]{2,1,0:T(8,128)(2,1)S(1)}, u32[]{:S(2)}, u32[]{:S(2)}) collective-permute-start(bf16[4,64,384]{2,1,0:T(8,128)(2,1)S(1)} %slice_bitcast_fusion.8), channel_id=1, source_target_pairs={{0,2},{1,3},{2,0},{3,1},{4,6},{5,7},{6,4},{7,5},{8,14},{9,15},{10,... | collective-permute-start | bytes 589832 | tf_op jit(solution)/shard_map/ppermute | solution.py:46
  209.7 6.8 %collective-permute-start.30 = (bf16[4,64,384]{2,1,0:T(8,128)(2,1)S(1)}, bf16[4,64,384]{2,1,0:T(8,128)(2,1)S(1)}, u32[]{:S(2)}, u32[]{:S(2)}) collective-permute-start(bf16[4,64,384]{2,1,0:T(8,128)(2,1)S(1)} %slice_bitcast_fusion.10), channel_id=1, source_target_pairs={{0,1},{1,0},{2,3},{3,2},{4,5},{5,4},{6,7},{7,6},{8,73},{9,72},{10,... | collective-permute-start | bytes 589832 | tf_op jit(solution)/shard_map/ppermute | solution.py:46
  209.8 8.2 %collective-permute-start.43 = (bf16[2,1,64,384]{3,2,1,0:T(8,128)(2,1)S(1)}, bf16[2,1,64,384]{3,2,1,0:T(8,128)(2,1)S(1)}, u32[]{:S(2)}, u32[]{:S(2)}) collective-permute-start(bf16[2,1,64,384]{3,2,1,0:T(8,128)(2,1)S(1)} %slice_bitcast_fusion.12), channel_id=1, source_target_pairs={{0,6},{1,7},{2,4},{3,5},{4,2},{5,3},{6,0},{7,1},{8,10},{9,11},{10,... | collective-permute-start | bytes 294920 | tf_op jit(solution)/shard_map/ppermute | solution.py:46
  213.0 6.0 %collective-permute-start.37 = (bf16[2,1,64,384]{3,2,1,0:T(8,128)(2,1)S(1)}, bf16[2,1,64,384]{3,2,1,0:T(8,128)(2,1)S(1)}, u32[]{:S(2)}, u32[]{:S(2)}) collective-permute-start(bf16[2,1,64,384]{3,2,1,0:T(8,128)(2,1)S(1)} %slice_bitcast_fusion.14), channel_id=1, source_target_pairs={{0,65},{1,64},{2,67},{3,66},{4,69},{5,68},{6,71},{7,70},{8,9},{9,8... | collective-permute-start | bytes 294920 | tf_op jit(solution)/shard_map/ppermute | solution.py:46
  216.5 5.9 %collective-permute-start.31 = (bf16[2,1,64,384]{3,2,1,0:T(8,128)(2,1)S(1)}, bf16[2,1,64,384]{3,2,1,0:T(8,128)(2,1)S(1)}, u32[]{:S(2)}, u32[]{:S(2)}) collective-permute-start(bf16[2,1,64,384]{3,2,1,0:T(8,128)(2,1)S(1)} %slice_bitcast_fusion.16), channel_id=1, source_target_pairs={{0,48},{1,49},{2,50},{3,51},{4,52},{5,53},{6,54},{7,55},{8,24},{9,... | collective-permute-start | bytes 294920 | tf_op jit(solution)/shard_map/ppermute | solution.py:46
  218.0 4.5 %collective-permute-start.44 = (bf16[1,64,384]{2,1,0:T(8,128)(2,1)S(1)}, bf16[1,64,384]{2,1,0:T(8,128)(2,1)S(1)}, u32[]{:S(2)}, u32[]{:S(2)}) collective-permute-start(bf16[1,64,384]{2,1,0:T(8,128)(2,1)S(1)} %slice_bitcast_fusion.18), channel_id=1, source_target_pairs={{0,2},{1,3},{2,0},{3,1},{4,6},{5,7},{6,4},{7,5},{8,14},{9,15},{10,... | collective-permute-start | bytes 147464 | tf_op jit(solution)/shard_map/ppermute | solution.py:46
  219.0 4.2 %collective-permute-start.38 = (bf16[1,64,384]{2,1,0:T(8,128)(2,1)S(1)}, bf16[1,64,384]{2,1,0:T(8,128)(2,1)S(1)}, u32[]{:S(2)}, u32[]{:S(2)}) collective-permute-start(bf16[1,64,384]{2,1,0:T(8,128)(2,1)S(1)} %slice_bitcast_fusion.20), channel_id=1, source_target_pairs={{0,1},{1,0},{2,3},{3,2},{4,5},{5,4},{6,7},{7,6},{8,73},{9,72},{10,... | collective-permute-start | bytes 147464 | tf_op jit(solution)/shard_map/ppermute | solution.py:46
  222.4 4.2 %collective-permute-start.32 = (bf16[1,64,384]{2,1,0:T(8,128)(2,1)S(1)}, bf16[1,64,384]{2,1,0:T(8,128)(2,1)S(1)}, u32[]{:S(2)}, u32[]{:S(2)}) collective-permute-start(bf16[1,64,384]{2,1,0:T(8,128)(2,1)S(1)} %slice_bitcast_fusion.22), channel_id=1, source_target_pairs={{0,16},{1,17},{2,18},{3,19},{4,20},{5,21},{6,22},{7,23},{8,56},{9,... | collective-permute-start | bytes 147464 | tf_op jit(solution)/shard_map/ppermute | solution.py:46
  (10 other events, 56.8 us)

commit v2 on v0

v2 whole, which is shorter than its diff:
```python
import jax
import jax.numpy as jnp
from jax import lax
from jax.experimental import pallas as pl
from jax.experimental.pallas import tpu as pltpu
from jax.sharding import Mesh, PartitionSpec as P

NAMES = ("zh", "y", "c", "x", "zl")
SIZES = (2, 4, 2, 4, 2)
ROWS = 208
TOK = 512
GROUP = 64
BLOCK = 1024
NB = 8
RANK = 64
WIDE = BLOCK + 128
PART = WIDE // 3
SYNC = True
RSYNC = True
DIRECT = 0
ORDERS = ((1, 2, 0), (2, 0, 1), (0, 1, 2))
VMEM = 60 * 1024 * 1024


def pairs(move):
    out = []
    for i in range(128):
        zh, y, c, x, zl = i // 64, i // 16 % 4, i // 8 % 2, i // 2 % 4, i % 2
        x, y, z, c = move(x, y, 2 * zh + zl, c)
        out.append((i, (((z // 2 * 4 + y) * 2 + c) * 4 + x) * 2 + z % 2))
    return out


def axis_pairs(axis, first):
    def move(x, y, z, c):
        q = [x, y, z]
        q[axis] ^= 1 if (c == 0) == first else 3
        return (*q, c)

    return pairs(move)


FIRST = [axis_pairs(a, True) for a in range(3)]
SECOND = [axis_pairs(a, False) for a in range(3)]


def across_pairs(axis):
    def move(x, y, z, c):
        q = [x, y, z]
        q[axis] ^= 2
        return (*q, c)

    return pairs(move)


ACROSS = [across_pairs(a) for a in range(3)]
CORES = pairs(lambda x, y, z, c: (x, y, z, 1 - c))


def send(value, table):
    return lax.ppermute(value, NAMES, table)


def gather(values):
    for stage in range(3):
        axes = [order[stage] for order in ORDERS]
        if stage < DIRECT:
            got = [
                [v] + [send(v, t[a]) for t in (FIRST, SECOND, ACROSS)]
                for v, a in zip(values, axes)
            ]
            values = [jnp.stack(g).reshape(-1, *g[0].shape[1:]) for g in got]
            if SYNC: values = lax.optimization_barrier(values)
            continue
        mine = [jnp.stack([v, send(v, FIRST[a])]) for v, a in zip(values, axes)]
        if False: mine = lax.optimization_barrier(mine)
        theirs = [send(v, SECOND[a]) for v, a in zip(mine, axes)]
        if stage < 2:
            values = [
                jnp.concatenate(p).reshape(-1, *v.shape[1:])
                for p, v in zip(zip(mine, theirs), values)
            ]
            if SYNC: values = lax.optimization_barrier(values)
    return [b for p in zip(mine, theirs) for b in p]


def scatter(keep, away):
    for stage in range(2, -1, -1):
        axes = [order[stage] for order in ORDERS]
        if stage < 2:
            keep, away = zip(*(t.reshape(2, 2, -1, GROUP, PART) for t in totals))
        if stage < DIRECT:
            totals = []
            for k, w, a in zip(keep, away, axes):
                got = [send(k[1], FIRST[a]), send(w[0], SECOND[a]), send(w[1], ACROSS[a])]
                totals.append(sum((g.astype(jnp.float32) for g in got), k[0].astype(jnp.float32)).astype(jnp.bfloat16))
            continue
        pairs_ = [k + send(w, SECOND[a]) for k, w, a in zip(keep, away, axes)]
        if False: pairs_ = lax.optimization_barrier(pairs_)
        totals = [p[0] + send(p[1], FIRST[a]) for p, a in zip(pairs_, axes)]
        if RSYNC and stage > 0: totals = lax.optimization_barrier(totals)
    return [t.reshape(GROUP, PART) for t in totals]


def coordinate(place, k, core):
    return place ^ jnp.where(core == 0, (0, 1, 3, 2)[k], (0, 3, 1, 2)[k])


def relative(place, there, core):
    e = place ^ there
    zero = jnp.where(e == 1, 1, jnp.where(e == 3, 2, jnp.where(e == 2, 3, 0)))
    one = jnp.where(e == 3, 1, jnp.where(e == 1, 2, jnp.where(e == 2, 3, 0)))
    return jnp.where(core == 0, zero, one)


def dot_t(a, b):
    return lax.dot_general(a, b, (((1,), (1,)), ((), ())), preferred_element_type=jnp.float32)


def copy(source, target, sem):
    pltpu.make_async_copy(source, target, sem).start()


def await_all(target, sem):
    pltpu.make_async_copy(target, target, sem).wait()


def up_kernel(place, w, wo, a_mine, a_other, *refs):
    blocks, (out, factor, ws, xs, acc, wsems, xsems, bsems, fsem) = refs[:6], refs[6:]
    core = place[0]
    at = [[coordinate(place[1 + a], k, core) for k in range(4)] for a in range(3)]
    near = place[3] // 2
    steps = [(near if j < 4 else 1 - near, j % 4) for j in range(NB)]

    def weights(zh, ky):
        columns = pl.ds(pl.multiple_of((2 * (4 * zh + at[1][ky]) + core) * BLOCK, BLOCK), BLOCK)
        block = 4 * zh + ky
        for side, source in enumerate((w, wo)):
            for k in range(2):
                rows = pl.ds((2 * side + k) * ROWS, ROWS)
                copy(source.at[k, :, columns], ws.at[block, rows], wsems.at[block])

    weights(*steps[0])
    left, middle, right = (blocks[i : i + 2] for i in (0, 2, 4))
    for kz in range(4):
        zh, zl = at[2][kz] // 2, at[2][kz] & 1
        block = pl.ds(4 * zh, 4)
        last = BLOCK - 2 * PART
        copy(
            right[kz // 2].at[kz % 2, :, :, :, pl.ds(0, last)],
            xs.at[block, :, zl, :, pl.ds(2 * PART, last)],
            xsems.at[zh],
        )
        for k in range(4):
            copy(
                left[k // 2].at[k % 2, kz, :, :, pl.ds(0, PART)],
                xs.at[block, k, zl, :, pl.ds(0, PART)],
                xsems.at[zh],
            )
            copy(
                middle[k // 2].at[k % 2, :, kz],
                xs.at[4 * zh + k, :, zl, :, pl.ds(PART, PART)],
                xsems.at[zh],
            )
            columns = pl.ds(pl.multiple_of((2 * at[0][k] + zl) * 128, 128), 128)
            for part in range(2):
                copy(
                    right[kz // 2].at[kz % 2, :, k, :, pl.ds(last + part * 128, 128)],
                    ws.at[block, pl.ds(4 * ROWS + part * RANK, RANK), columns],
                    bsems.at[zh],
                )
    for k in range(4):
        for kz in (0, 1 + core):
            zl = place[3] & 1 if isinstance(kz, int) else 1 - (place[3] & 1)
            columns = pl.ds(pl.multiple_of((2 * at[0][k] + zl) * 128, 128), 128)
            copy(left[k // 2].at[k % 2, kz, 0, :, pl.ds(PART, 128)], factor.at[:, columns], fsem)
    for j in range(1, NB):
        weights(*steps[j])

    for j, (zh, ky) in enumerate(steps):
        block = 4 * zh + ky
        if j % 4 == 0:
            await_all(xs.at[pl.ds(4 * zh, 4)], xsems.at[zh])
            await_all(ws.at[pl.ds(4 * zh, 4), pl.ds(4 * ROWS, 2 * RANK)], bsems.at[zh])
        await_all(ws.at[block, pl.ds(0, 4 * ROWS)], wsems.at[block])
        product = dot_t(ws[block], xs[block].reshape(TOK, BLOCK))
        if j == 0:
            acc[...] = product
        else:
            acc[...] += product
    t = acc[4 * ROWS :].astype(jnp.bfloat16)
    for side, a in enumerate((a_mine, a_other)):
        for k in range(2):
            low = jnp.dot(a[k], t[k * RANK : (k + 1) * RANK], preferred_element_type=jnp.float32)
            rows = (2 * side + k) * ROWS
            out[side, k] = (acc[rows : rows + ROWS] + low).astype(jnp.bfloat16)
    await_all(factor, fsem)


ANY = pl.BlockSpec(memory_space=pl.ANY)
ON_CHIP = pl.BlockSpec(memory_space=pltpu.VMEM)
SCALARS = pl.BlockSpec(memory_space=pltpu.SMEM)


def up(place, weights, others, a_mine, a_other, blocks):
    return pl.pallas_call(
        up_kernel,
        out_shape=[
            jax.ShapeDtypeStruct((2, 2, ROWS, TOK), jnp.bfloat16),
            jax.ShapeDtypeStruct((RANK, BLOCK), jnp.bfloat16),
        ],
        in_specs=[SCALARS, ANY, ANY, ON_CHIP, ON_CHIP, *[ANY] * 6],
        out_specs=[ON_CHIP, ON_CHIP],
        scratch_shapes=[
            pltpu.VMEM((NB, 4 * ROWS + 2 * RANK, BLOCK), jnp.bfloat16),
            pltpu.VMEM((NB, 4, 2, GROUP, BLOCK), jnp.bfloat16),
            pltpu.VMEM((4 * ROWS + 2 * RANK, TOK), jnp.float32),
            pltpu.SemaphoreType.DMA((NB,)),
            pltpu.SemaphoreType.DMA((2,)),
            pltpu.SemaphoreType.DMA((2,)),
            pltpu.SemaphoreType.DMA,
        ],
        compiler_params=pltpu.CompilerParams(vmem_limit_bytes=VMEM),
        name="up",
    )(place, weights, others, a_mine, a_other, *blocks)


def down_kernel(place, mine, other, w, wo, a_mine, a_other, *refs):
    outs, (ws, hidden, ob, wsems, osems) = refs[:6], refs[6:]
    core = place[0]
    for j in range(NB):
        there = 2 * (4 * (j // 4) + coordinate(place[2], j % 4, core)) + core
        columns = pl.ds(pl.multiple_of(there * BLOCK, BLOCK), BLOCK)
        for side, source in enumerate((w, wo)):
            copy(source.at[2, :, columns], ws.at[j, pl.ds(side * ROWS, ROWS)], wsems.at[j])
    f32 = jnp.float32

    def both(side, k):
        theirs = [other[1 - side, k, :, i * 128 : (i + 1) * 128] for i in (0, 2, 1, 3)]
        return mine[side, k].astype(f32) + jnp.concatenate(theirs, axis=1).astype(f32)

    halves = []
    for side in range(2):
        gate, upper = both(side, 0), both(side, 1)
        halves.append(gate / (1.0 + jnp.exp(-gate)) * upper)
    hidden[...] = jnp.concatenate(halves, axis=0).T.astype(jnp.bfloat16)
    factor = jnp.concatenate([a_mine[2], a_other[2]], axis=0)
    low = jnp.dot(hidden[...], factor, preferred_element_type=f32)
    low = jnp.concatenate([low, jnp.zeros_like(low)], axis=1).astype(jnp.bfloat16)
    rel_z = [relative(place[3], z, core) for z in range(4)]
    left, middle, right = (outs[i : i + 2] for i in (0, 2, 4))
    for j in range(NB):
        zh, ky = j // 4, j % 4
        await_all(ws.at[j], wsems.at[j])
        value = jnp.dot(hidden[...], ws[j], preferred_element_type=f32).astype(jnp.bfloat16)
        ob[j, :, :, :, :BLOCK] = value.reshape(4, 2, GROUP, BLOCK)
        ob[j, :, :, :, BLOCK:] = low.reshape(4, 2, GROUP, 128)
        for zl in range(2):
            kz = rel_z[2 * zh + zl]
            for kx in range(4):
                copy(
                    ob.at[j, kx, zl, :, pl.ds(0, PART)],
                    left[kx // 2].at[kx % 2, kz, ky],
                    osems.at[j],
                )
            copy(
                ob.at[j, :, zl, :, pl.ds(PART, PART)],
                middle[ky // 2].at[ky % 2, :, kz],
                osems.at[j],
            )
            for half in range(2):

                @pl.when(kz // 2 == half)
                def _():
                    copy(
                        ob.at[j, :, zl, :, pl.ds(2 * PART, PART)],
                        right[half].at[kz % 2, ky],
                        osems.at[j],
                    )
    for j in range(NB):
        await_all(ob.at[j], osems.at[j])


def down(place, mine, other, weights, others, a_mine, a_other):
    return pl.pallas_call(
        down_kernel,
        out_shape=[jax.ShapeDtypeStruct((2, 4, 4, GROUP, PART), jnp.bfloat16)] * 6,
        in_specs=[SCALARS, ON_CHIP, ON_CHIP, ANY, ANY, ON_CHIP, ON_CHIP],
        out_specs=[ANY] * 6,
        scratch_shapes=[
            pltpu.VMEM((NB, 2 * ROWS, BLOCK), jnp.bfloat16),
            pltpu.VMEM((TOK, 2 * ROWS), jnp.bfloat16),
            pltpu.VMEM((NB, 4, 2, GROUP, WIDE), jnp.bfloat16),
            *[pltpu.SemaphoreType.DMA((NB,))] * 2,
        ],
        compiler_params=pltpu.CompilerParams(vmem_limit_bytes=VMEM),
        name="down",
    )(place, mine, other, weights, others, a_mine, a_other)


def per_device(tokens, frozen_weights, hidden_adapter_factor, feature_adapter_factor):
    zh, y, core, x, zl = (lax.axis_index(n) for n in NAMES)
    place = jnp.stack([core, x, y, 2 * zh + zl]).astype(jnp.int32)
    others = send(frozen_weights, CORES)
    a_other = send(hidden_adapter_factor, CORES)
    gate_factor, up_factor, down_factor = feature_adapter_factor
    blocks = gather([
        jnp.concatenate([tokens[:, :PART], down_factor], axis=1)[None],
        tokens[None, :, PART : 2 * PART],
        jnp.concatenate([tokens[:, 2 * PART :], gate_factor, up_factor], axis=1)[None],
    ])
    blocks = [v.reshape(2, 4, 4, *v.shape[2:]) for v in blocks]
    mine, factor = up(place, frozen_weights, others, hidden_adapter_factor, a_other, blocks)
    theirs = send(mine, CORES)
    sums = down(place, mine, theirs, frozen_weights, others, hidden_adapter_factor, a_other)
    left, middle, right = scatter(
        [v.reshape(2, 16, GROUP, PART) for v in sums[::2]],
        [v.reshape(2, 16, GROUP, PART) for v in sums[1::2]],
    )
    last = BLOCK - 2 * PART
    plain = jnp.concatenate([left, middle, right[:, :last]], axis=1).astype(jnp.float32)
    extra = jnp.dot(
        right[:, last : last + RANK], factor, preferred_element_type=jnp.float32
    )
    return (plain + extra).astype(jnp.bfloat16)


def solution(mesh):
    fine = Mesh(mesh.devices.reshape(SIZES), NAMES)
    units = ("zh", "y", "c", "x", "zl")
    return jax.shard_map(
        per_device,
        mesh=fine,
        in_specs=(
            P(("x", "zl"), ("zh", "y", "c")),
            P(None, units, None),
            P(None, units, None),
            P(None, None, units),
        ),
        out_specs=P(("x", "zl"), ("zh", "y", "c")),
        check_vma=False,
    )
```

time: 1080 us -> 196 us (0.18)
  waiting for transfers between devices: 890 us -> 82.3 us
  local copies, waits for them, and re-layouts: 116 us -> 5.86 us
  starting transfers between devices: 6.07 us -> 62.5 us
  matrix products: 42.8 us -> 0.82 us
  Pallas kernels: 0 us -> 25.2 us
  other arithmetic: 0 us -> 15.4 us
  between operations: 15 us -> 0.44 us
    all_to_all x1 -> x0, waiting for transfers between devices: 431 us -> none  [per_device(): lax.all_to_all(outgoing_block, 'fsdp', split_axis=2, concat_axis=1, tiled...]
    all_gather x2 -> x0, waiting for transfers between devices: 269 us -> none  [the longest x1 269 us: per_device(): lax.all_gather(feature_adapter_factor, ('fsdp', 'mp'), axis=2, tiled=True)]
    psum x1 -> x0, waiting for transfers between devices: 150 us -> none  [per_device(): lax.psum(up_part.astype(jnp.bfloat16), 'fsdp').astype(jnp.float32)]
    ppermute x0 -> x39, waiting for transfers between devices: none -> 82.3 us  [send(): return lax.ppermute(value, NAMES, table)]
    ppermute x0 -> x39, starting transfers between devices: none -> 62.5 us  [send(): return lax.ppermute(value, NAMES, table)]
    convert_element_type x1 -> x0, local copies, waits for them, and re-layouts: 47.6 us -> none  [apply_adapter_update(): return (weights.astype(jnp.float32) + weight_update).astype(jnp.bfloat16)]
    dot_general x4 -> x1, matrix products: 42.8 us -> 0.82 us  [per_device(): jnp.dot(right[:, last:last + RANK], factor, preferred_element_type=jnp.fl...]
    reduce_scatter x1 -> x0, waiting for transfers between devices: 38.5 us -> none  [per_device(): lax.psum_scatter(jnp.dot(hidden, down_weight_block, preferred_element_typ...]
  transfers between devices with their start and end apart: 5 -> 39, of which waited for: 4 -> 21; matrix products, arithmetic and copies ran while one was open for 6% -> 10% of each run, Pallas kernels for 0% -> 0%
where the time goes in v2:
time: 196 us; the launch traced here: 192 us
  waiting for transfers between devices  82.3 us (42%)
  starting transfers between devices  62.5 us (32%)
  Pallas kernels  25.2 us (13%)
  other arithmetic  15.4 us (8%)
  local copies, waits for them, and re-layouts  5.86 us (3%)
    ppermute x39, waiting for transfers between devices, send(): return lax.ppermute(value, NAMES, table)  82.3 us
    ppermute x39, starting transfers between devices, send(): return lax.ppermute(value, NAMES, table)  62.5 us
    pallas_call x1, Pallas kernels, up(): pl.pallas_call(up_kernel, out_shape=[jax.ShapeDtypeStruct((2, 2, ROWS, TO...  15.4 us
    another operation x14, other arithmetic, gather(): mine = [jnp.stack([v, send(v, FIRST[a])]) for v, a in zip(values, axes)]  10.6 us
    pallas_call x1, Pallas kernels, down(): pl.pallas_call(down_kernel, out_shape=[jax.ShapeDtypeStruct((2, 4, 4, GRO...  9.78 us
  transfers between devices with their start and end apart: 39, of which 21 were waited for; matrix products, arithmetic and copies ran while one was open for 10% of the time, Pallas kernels for 0%

profile of v2, /device:TPU:38, one launch (start us, length us, event | category | flops | bytes accessed | tf_op | source)
XLA Modules:
  0.0 192.4 jit_solution(9003924049110735831)
XLA Ops:
  3.5 1.7 collective-permute-start.2
  5.1 2.3 %collective-permute-done.4 = bf16[1,64,384]{2,1,0:T(8,128)(2,1)S(1)} collective-permute-done((bf16[1,64,384]{2,1,0:T(8,128)(2,1)S(1)}, bf16[1,64,384]{2,1,0:T(8,128)(2,1)S(1)}, u32[]{:S(2)}, u32[]{:S(2)}) %collective-permute-start.4) | collective-permute-done | bytes 49184 | tf_op jit(solution)/shard_map/ppermute | solution.py:61
  7.5 2.0 %collective-permute-start.5 = (bf16[2,1,64,384]{3,2,1,0:T(8,128)(2,1)S(1)}, bf16[2,1,64,384]{3,2,1,0:T(8,128)(2,1)S(1)}, u32[]{:S(2)}, u32[]{:S(2)}) collective-permute-start(bf16[2,1,64,384]{3,2,1,0:T(8,128)(2,1)S(1)} %pad_maximum_fusion.14), channel_id=1, source_target_pairs={{0,65},{1,64},{2,67},{3,66},{4,69},{5,68},{6,71},{7,70},{8,9},{9,8... | collective-permute-start | bytes 294920 | tf_op jit(solution)/shard_map/ppermute | solution.py:61
  9.5 1.2 collective-permute-start.7
  10.7 3.1 %collective-permute-start.3 = (bf16[2,1,64,512]{3,2,1,0:T(8,128)(2,1)S(1)}, bf16[2,1,64,512]{3,2,1,0:T(8,128)(2,1)S(1)}, u32[]{:S(2)}, u32[]{:S(2)}) collective-permute-start(bf16[2,1,64,512]{3,2,1,0:T(8,128)(2,1)S(1)} %pad_maximum_fusion.12), channel_id=1, source_target_pairs={{0,48},{1,49},{2,50},{3,51},{4,52},{5,53},{6,54},{7,55},{8,24},{9,... | collective-permute-start | bytes 393224 | tf_op jit(solution)/shard_map/ppermute | solution.py:61
  13.9 1.9 collective-permute-done.7
  15.8 1.2 collective-permute-done.3
  17.2 2.2 %collective-permute-start.8 = (bf16[4,64,512]{2,1,0:T(8,128)(2,1)S(1)}, bf16[4,64,512]{2,1,0:T(8,128)(2,1)S(1)}, u32[]{:S(2)}, u32[]{:S(2)}) collective-permute-start(bf16[4,64,512]{2,1,0:T(8,128)(2,1)S(1)} %maximum_bitcast_fusion), channel_id=1, source_target_pairs={{0,1},{1,0},{2,3},{3,2},{4,5},{5,4},{6,7},{7,6},{8,73},{9,72},{10,... | collective-permute-start | bytes 786440 | tf_op jit(solution)/shard_map/ppermute | solution.py:61
  19.8 3.0 %collective-permute-done.10 = bf16[4,64,384]{2,1,0:T(8,128)(2,1)S(1)} collective-permute-done((bf16[4,64,384]{2,1,0:T(8,128)(2,1)S(1)}, bf16[4,64,384]{2,1,0:T(8,128)(2,1)S(1)}, u32[]{:S(2)}, u32[]{:S(2)}) %collective-permute-start.10) | collective-permute-done | bytes 196640 | tf_op jit(solution)/shard_map/ppermute | solution.py:61
  22.8 2.2 %collective-permute-start.11 = (bf16[2,4,64,384]{3,2,1,0:T(8,128)(2,1)S(1)}, bf16[2,4,64,384]{3,2,1,0:T(8,128)(2,1)S(1)}, u32[]{:S(2)}, u32[]{:S(2)}) collective-permute-start(bf16[2,4,64,384]{3,2,1,0:T(8,128)(2,1)S(1)} %pad_maximum_fusion.11), channel_id=1, source_target_pairs={{0,6},{1,7},{2,4},{3,5},{4,2},{5,3},{6,0},{7,1},{8,10},{9,11},{10,... | collective-permute-start | bytes 1179656 | tf_op jit(solution)/shard_map/ppermute | solution.py:61
  25.8 3.1 %collective-permute-start.13 = (bf16[2,4,64,512]{3,2,1,0:T(8,128)(2,1)S(1)}, bf16[2,4,64,512]{3,2,1,0:T(8,128)(2,1)S(1)}, u32[]{:S(2)}, u32[]{:S(2)}) collective-permute-start(bf16[2,4,64,512]{3,2,1,0:T(8,128)(2,1)S(1)} %pad_maximum_fusion.10), channel_id=1, source_target_pairs={{0,48},{1,49},{2,50},{3,51},{4,52},{5,53},{6,54},{7,55},{8,24},{9,... | collective-permute-start | bytes 1572872 | tf_op jit(solution)/shard_map/ppermute | solution.py:61
  28.9 2.9 %collective-permute-done.11 = bf16[2,4,64,384]{3,2,1,0:T(8,128)(2,1)S(1)} collective-permute-done((bf16[2,4,64,384]{3,2,1,0:T(8,128)(2,1)S(1)}, bf16[2,4,64,384]{3,2,1,0:T(8,128)(2,1)S(1)}, u32[]{:S(2)}, u32[]{:S(2)}) %collective-permute-start.11) | collective-permute-done | bytes 393248 | tf_op jit(solution)/shard_map/ppermute | solution.py:61
  32.0 2.3 %collective-permute-done.9 = bf16[2,4,64,512]{3,2,1,0:T(8,128)(2,1)S(1)} collective-permute-done((bf16[2,4,64,512]{3,2,1,0:T(8,128)(2,1)S(1)}, bf16[2,4,64,512]{3,2,1,0:T(8,128)(2,1)S(1)}, u32[]{:S(2)}, u32[]{:S(2)}) %collective-permute-start.9) | collective-permute-done | bytes 524320 | tf_op jit(solution)/shard_map/ppermute | solution.py:61
  34.4 1.9 collective-permute-done.13
  36.4 2.0 %collective-permute-start.14 = (bf16[16,64,512]{2,1,0:T(8,128)(2,1)S(1)}, bf16[16,64,512]{2,1,0:T(8,128)(2,1)S(1)}, u32[]{:S(2)}, u32[]{:S(2)}) collective-permute-start(bf16[16,64,512]{2,1,0:T(8,128)(2,1)S(1)} %bitcast.152), channel_id=1, source_target_pairs={{0,2},{1,3},{2,0},{3,1},{4,6},{5,7},{6,4},{7,5},{8,14},{9,15},{10,... | collective-permute-start | bytes 3145736 | tf_op jit(solution)/shard_map/ppermute | solution.py:61
  39.4 11.9 %collective-permute-done.14 = bf16[16,64,512]{2,1,0:T(8,128)(2,1)S(1)} collective-permute-done((bf16[16,64,512]{2,1,0:T(8,128)(2,1)S(1)}, bf16[16,64,512]{2,1,0:T(8,128)(2,1)S(1)}, u32[]{:S(2)}, u32[]{:S(2)}) %collective-permute-start.14) | collective-permute-done | bytes 1048608 | tf_op jit(solution)/shard_map/ppermute | solution.py:61
  51.3 1.7 pad_maximum_fusion.1
  53.0 4.9 %collective-permute-start.15 = (bf16[2,16,64,512]{3,2,1,0:T(8,128)(2,1)}, bf16[2,16,64,512]{3,2,1,0:T(8,128)(2,1)}, u32[]{:S(2)}, u32[]{:S(2)}) collective-permute-start(bf16[2,16,64,512]{3,2,1,0:T(8,128)(2,1)} %pad_maximum_fusion.1), channel_id=1, source_target_pairs={{0,6},{1,7},{2,4},{3,5},{4,2},{5,3},{6,0},{7,1},{8,10},{9,11},{10,... | collective-permute-start | bytes 6291464 | tf_op jit(solution)/shard_map/ppermute | solution.py:61
  57.9 1.7 pad_maximum_fusion.3
  59.6 1.4 pad_maximum_fusion.5
  61.0 4.4 %collective-permute-start.17 = (bf16[2,16,64,384]{3,2,1,0:T(8,128)(2,1)}, bf16[2,16,64,384]{3,2,1,0:T(8,128)(2,1)}, u32[]{:S(2)}, u32[]{:S(2)}) collective-permute-start(bf16[2,16,64,384]{3,2,1,0:T(8,128)(2,1)} %pad_maximum_fusion.5), channel_id=1, source_target_pairs={{0,48},{1,49},{2,50},{3,51},{4,52},{5,53},{6,54},{7,55},{8,24},{9,... | collective-permute-start | bytes 4718600 | tf_op jit(solution)/shard_map/ppermute | solution.py:61
  66.4 2.6 %pad_maximum_fusion.4.refs_2_ = bf16[2,4,4,64,384]{4,3,2,1,0:T(8,128)(2,1)} fusion(bf16[1,4,4,64,384]{4,3,2,1,0:T(8,128)(2,1)} %bitcast.166, bf16[1,4,4,64,384]{4,3,2,1,0:T(8,128)(2,1)S(1)} %bitcast.160), kind=kLoop, calls=%fused_computation.4 | loop fusion | flops 786432 | bytes 3145728 | tf_op jit(solution)/shard_map/stack | solution.py:75
  69.0 1.5 pad_maximum_fusion.2.refs_4_
  70.5 1.5 pad_maximum_fusion.refs_0_
  72.1 12.0 %collective-permute-done.17 = bf16[2,16,64,384]{3,2,1,0:T(8,128)(2,1)} collective-permute-done((bf16[2,16,64,384]{3,2,1,0:T(8,128)(2,1)}, bf16[2,16,64,384]{3,2,1,0:T(8,128)(2,1)}, u32[]{:S(2)}, u32[]{:S(2)}) %collective-permute-start.17) | collective-permute-done | bytes 1572896 | tf_op jit(solution)/shard_map/ppermute | solution.py:61
  84.1 1.8 collective-permute-done.19
  85.9 15.4 %up.1 = (bf16[2,2,208,512]{3,2,1,0:T(8,128)(2,1)}, bf16[64,1024]{1,0:T(8,128)(2,1)}) custom-call(s32[4]{0:T(128)} %pad_add_fusion.place, bf16[3,208,16384]{2,1,0:T(8,128)(2,1)} %w.3, bf16[3,208,16384]{2,1,0:T(8,128)(2,1)} %collective-permute-done.wo, bf16[3,208,64]{2,1,0:T(8,128)(2,1)} %copy-done.7, bf16[3,208,64]{2,1,0:T(8,128)(2,1)} %copy-done.9, ...), custom_call_target="tpu_custom_call" | custom-call | tf_op jit(solution)/shard_map/up/pallas_call | solution.py:206
  101.6 2.6 %collective-permute-done.20.other = bf16[2,2,208,512]{3,2,1,0:T(8,128)(2,1)S(1)} collective-permute-done((bf16[2,2,208,512]{3,2,1,0:T(8,128)(2,1)}, bf16[2,2,208,512]{3,2,1,0:T(8,128)(2,1)S(1)}, u32[]{:S(2)}, u32[]{:S(2)}) %collective-permute-start.20) | collective-permute-done | bytes 852000 | tf_op jit(solution)/shard_map/ppermute | solution.py:61
  105.1 9.8 %down.1 = (bf16[2,4,4,64,384]{4,3,2,1,0:T(8,128)(2,1)}, bf16[2,4,4,64,384]{4,3,2,1,0:T(8,128)(2,1)}, bf16[2,4,4,64,384]{4,3,2,1,0:T(8,128)(2,1)}, bf16[2,4,4,64,...) custom-call(s32[4]{0:T(128)} %pad_add_fusion.place, ...), custom_call_target="tpu_custom_call" | custom-call | tf_op jit(solution)/shard_map/down/pallas_call | solution.py:285
  115.0 4.5 %collective-permute-start.23 = (bf16[2,16,64,384]{3,2,1,0:T(8,128)(2,1)}, bf16[2,16,64,384]{3,2,1,0:T(8,128)(2,1)S(1)}, u32[]{:S(2)}, u32[]{:S(2)}) collective-permute-start(bf16[2,16,64,384]{3,2,1,0:T(8,128)(2,1)} %bitcast.195), channel_id=1, source_target_pairs={{0,48},{1,49},{2,50},{3,51},{4,52},{5,53},{6,54},{7,55},{8,24},{9,... | collective-permute-start | bytes 4718600 | tf_op jit(solution)/shard_map/ppermute | solution.py:61
  119.4 17.3 %collective-permute-done.21 = bf16[2,16,64,384]{3,2,1,0:T(8,128)(2,1)S(1)} collective-permute-done((bf16[2,16,64,384]{3,2,1,0:T(8,128)(2,1)}, bf16[2,16,64,384]{3,2,1,0:T(8,128)(2,1)S(1)}, u32[]{:S(2)}, u32[]{:S(2)}) %collective-permute-start.21) | collective-permute-done | bytes 1572896 | tf_op jit(solution)/shard_map/ppermute | solution.py:61
  136.8 2.0 %add.61 = bf16[2,16,64,384]{3,2,1,0:T(8,128)(2,1)S(1)} add(bf16[2,16,64,384]{3,2,1,0:T(8,128)(2,1)} %bitcast.177, bf16[2,16,64,384]{3,2,1,0:T(8,128)(2,1)S(1)} %collective-permute-done.21) | non-fusion elementwise | flops 786432 | bytes 4718592 | tf_op jit(solution)/shard_map/add | solution.py:98
  140.9 1.2 copy-done.5
  142.8 2.4 %collective-permute-start.26 = (bf16[16,64,384]{2,1,0:T(8,128)(2,1)S(1)}, bf16[16,64,384]{2,1,0:T(8,128)(2,1)S(1)}, u32[]{:S(2)}, u32[]{:S(2)}) collective-permute-start(bf16[16,64,384]{2,1,0:T(8,128)(2,1)S(1)} %slice_bitcast_fusion), channel_id=1, source_target_pairs={{0,1},{1,0},{2,3},{3,2},{4,5},{5,4},{6,7},{7,6},{8,73},{9,72},{10,... | collective-permute-start | bytes 2359304 | tf_op jit(solution)/shard_map/ppermute | solution.py:61
  145.2 5.7 %collective-permute-done.22 = bf16[16,64,384]{2,1,0:T(8,128)(2,1)S(1)} collective-permute-done((bf16[16,64,384]{2,1,0:T(8,128)(2,1)S(1)}, bf16[16,64,384]{2,1,0:T(8,128)(2,1)S(1)}, u32[]{:S(2)}, u32[]{:S(2)}) %collective-permute-start.22) | collective-permute-done | bytes 786464 | tf_op jit(solution)/shard_map/ppermute | solution.py:61
  151.0 1.9 collective-permute-done.24
  153.0 2.2 %collective-permute-done.26 = bf16[16,64,384]{2,1,0:T(8,128)(2,1)S(1)} collective-permute-done((bf16[16,64,384]{2,1,0:T(8,128)(2,1)S(1)}, bf16[16,64,384]{2,1,0:T(8,128)(2,1)S(1)}, u32[]{:S(2)}, u32[]{:S(2)}) %collective-permute-start.26) | collective-permute-done | bytes 786464 | tf_op jit(solution)/shard_map/ppermute | solution.py:61
  155.4 2.7 %collective-permute-start.27 = (bf16[2,4,64,384]{3,2,1,0:T(8,128)(2,1)S(1)}, bf16[2,4,64,384]{3,2,1,0:T(8,128)(2,1)S(1)}, u32[]{:S(2)}, u32[]{:S(2)}) collective-permute-start(bf16[2,4,64,384]{3,2,1,0:T(8,128)(2,1)S(1)} %bitcast.187), channel_id=1, source_target_pairs={{0,65},{1,64},{2,67},{3,66},{4,69},{5,68},{6,71},{7,70},{8,9},{9,8... | collective-permute-start | bytes 1179656 | tf_op jit(solution)/shard_map/ppermute | solution.py:61
  158.2 3.5 %collective-permute-start.31 = (bf16[2,4,64,384]{3,2,1,0:T(8,128)(2,1)S(1)}, bf16[2,4,64,384]{3,2,1,0:T(8,128)(2,1)S(1)}, u32[]{:S(2)}, u32[]{:S(2)}) collective-permute-start(bf16[2,4,64,384]{3,2,1,0:T(8,128)(2,1)S(1)} %bitcast.186), channel_id=1, source_target_pairs={{0,48},{1,49},{2,50},{3,51},{4,52},{5,53},{6,54},{7,55},{8,24},{9,... | collective-permute-start | bytes 1179656 | tf_op jit(solution)/shard_map/ppermute | solution.py:61
  161.8 2.0 %collective-permute-done.27 = bf16[2,4,64,384]{3,2,1,0:T(8,128)(2,1)S(1)} collective-permute-done((bf16[2,4,64,384]{3,2,1,0:T(8,128)(2,1)S(1)}, bf16[2,4,64,384]{3,2,1,0:T(8,128)(2,1)S(1)}, u32[]{:S(2)}, u32[]{:S(2)}) %collective-permute-start.27) | collective-permute-done | bytes 393248 | tf_op jit(solution)/shard_map/ppermute | solution.py:61
  163.9 2.7 %collective-permute-start.28 = (bf16[4,64,384]{2,1,0:T(8,128)(2,1)S(1)}, bf16[4,64,384]{2,1,0:T(8,128)(2,1)S(1)}, u32[]{:S(2)}, u32[]{:S(2)}) collective-permute-start(bf16[4,64,384]{2,1,0:T(8,128)(2,1)S(1)} %slice_bitcast_fusion.10), channel_id=1, source_target_pairs={{0,1},{1,0},{2,3},{3,2},{4,5},{5,4},{6,7},{7,6},{8,73},{9,72},{10,... | collective-permute-start | bytes 589832 | tf_op jit(solution)/shard_map/ppermute | solution.py:61
  167.6 3.2 %collective-permute-start.32 = (bf16[4,64,384]{2,1,0:T(8,128)(2,1)S(1)}, bf16[4,64,384]{2,1,0:T(8,128)(2,1)S(1)}, u32[]{:S(2)}, u32[]{:S(2)}) collective-permute-start(bf16[4,64,384]{2,1,0:T(8,128)(2,1)S(1)} %slice_bitcast_fusion.6), channel_id=1, source_target_pairs={{0,16},{1,17},{2,18},{3,19},{4,20},{5,21},{6,22},{7,23},{8,56},{9,... | collective-permute-start | bytes 589832 | tf_op jit(solution)/shard_map/ppermute | solution.py:61
  171.8 2.7 %collective-permute-done.32 = bf16[4,64,384]{2,1,0:T(8,128)(2,1)S(1)} collective-permute-done((bf16[4,64,384]{2,1,0:T(8,128)(2,1)S(1)}, bf16[4,64,384]{2,1,0:T(8,128)(2,1)S(1)}, u32[]{:S(2)}, u32[]{:S(2)}) %collective-permute-start.32) | collective-permute-done | bytes 196640 | tf_op jit(solution)/shard_map/ppermute | solution.py:61
  174.5 3.2 %collective-permute-done.30 = bf16[4,64,384]{2,1,0:T(8,128)(2,1)S(1)} collective-permute-done((bf16[4,64,384]{2,1,0:T(8,128)(2,1)S(1)}, bf16[4,64,384]{2,1,0:T(8,128)(2,1)S(1)}, u32[]{:S(2)}, u32[]{:S(2)}) %collective-permute-start.30) | collective-permute-done | bytes 196640 | tf_op jit(solution)/shard_map/ppermute | solution.py:61
  178.4 5.4 %collective-permute-start.33 = (bf16[2,1,64,384]{3,2,1,0:T(8,128)(2,1)S(1)}, bf16[2,1,64,384]{3,2,1,0:T(8,128)(2,1)S(1)}, u32[]{:S(2)}, u32[]{:S(2)}) collective-permute-start(bf16[2,1,64,384]{3,2,1,0:T(8,128)(2,1)S(1)} %slice_bitcast_fusion.14), channel_id=1, source_target_pairs={{0,48},{1,49},{2,50},{3,51},{4,52},{5,53},{6,54},{7,55},{8,24},{9,... | collective-permute-start | bytes 294920 | tf_op jit(solution)/shard_map/ppermute | solution.py:61
  184.9 2.5 %collective-permute-start.36 = (bf16[1,64,384]{2,1,0:T(8,128)(2,1)S(1)}, bf16[1,64,384]{2,1,0:T(8,128)(2,1)S(1)}, u32[]{:S(2)}, u32[]{:S(2)}) collective-permute-start(bf16[1,64,384]{2,1,0:T(8,128)(2,1)S(1)} %slice_bitcast_fusion.17), channel_id=1, source_target_pairs={{0,1},{1,0},{2,3},{3,2},{4,5},{5,4},{6,7},{7,6},{8,73},{9,72},{10,... | collective-permute-start | bytes 147464 | tf_op jit(solution)/shard_map/ppermute | solution.py:61
  187.4 2.0 %collective-permute-start.34 = (bf16[1,64,384]{2,1,0:T(8,128)(2,1)S(1)}, bf16[1,64,384]{2,1,0:T(8,128)(2,1)S(1)}, u32[]{:S(2)}, u32[]{:S(2)}) collective-permute-start(bf16[1,64,384]{2,1,0:T(8,128)(2,1)S(1)} %slice_bitcast_fusion.19), channel_id=1, source_target_pairs={{0,16},{1,17},{2,18},{3,19},{4,20},{5,21},{6,22},{7,23},{8,56},{9,... | collective-permute-start | bytes 147464 | tf_op jit(solution)/shard_map/ppermute | solution.py:61
  189.5 2.1 %collective-permute-done.34 = bf16[1,64,384]{2,1,0:T(8,128)(2,1)S(1)} collective-permute-done((bf16[1,64,384]{2,1,0:T(8,128)(2,1)S(1)}, bf16[1,64,384]{2,1,0:T(8,128)(2,1)S(1)}, u32[]{:S(2)}, u32[]{:S(2)}) %collective-permute-start.34) | collective-permute-done | bytes 49184 | tf_op jit(solution)/shard_map/ppermute | solution.py:61
  (115 shorter events, 16.7 us)
Async XLA Ops:
  0.0 85.9 %collective-permute-start = (bf16[3,208,16384]{2,1,0:T(8,128)(2,1)}, bf16[3,208,16384]{2,1,0:T(8,128)(2,1)}, u32[]{:S(2)}, u32[]{:S(2)}) collective-permute-start(bf16[3,208,16384]{2,1,0:T(8,128)(2,1)} %w.3), channel_id=1, source_target_pairs={{0,8},{1,9},{2,10},{3,11},{4,12},{5,13},{6,14},{7,15},{8,0},{9,1},... | collective-permute-start | bytes 61341704 | tf_op jit(solution)/shard_map/ppermute | solution.py:61
  1.5 7.9 %collective-permute-start.6 = (bf16[1,64,512]{2,1,0:T(8,128)(2,1)S(1)}, bf16[1,64,512]{2,1,0:T(8,128)(2,1)S(1)}, u32[]{:S(2)}, u32[]{:S(2)}) collective-permute-start(bf16[1,64,512]{2,1,0:T(8,128)(2,1)S(1)} %get-tuple-element.55), channel_id=1, source_target_pairs={{0,2},{1,3},{2,0},{3,1},{4,6},{5,7},{6,4},{7,5},{8,14},{9,15},{10,... | collective-permute-start | bytes 196616 | tf_op jit(solution)/shard_map/ppermute | solution.py:61
  3.3 4.2 %collective-permute-start.4 = (bf16[1,64,384]{2,1,0:T(8,128)(2,1)S(1)}, bf16[1,64,384]{2,1,0:T(8,128)(2,1)S(1)}, u32[]{:S(2)}, u32[]{:S(2)}) collective-permute-start(bf16[1,64,384]{2,1,0:T(8,128)(2,1)S(1)} %get-tuple-element.52), channel_id=1, source_target_pairs={{0,1},{1,0},{2,3},{3,2},{4,5},{5,4},{6,7},{7,6},{8,73},{9,72},{10,... | collective-permute-start | bytes 147464 | tf_op jit(solution)/shard_map/ppermute | solution.py:61
  3.5 7.2 %collective-permute-start.2 = (bf16[1,64,512]{2,1,0:T(8,128)(2,1)S(1)}, bf16[1,64,512]{2,1,0:T(8,128)(2,1)S(1)}, u32[]{:S(2)}, u32[]{:S(2)}) collective-permute-start(bf16[1,64,512]{2,1,0:T(8,128)(2,1)S(1)} %get-tuple-element.57), channel_id=1, source_target_pairs={{0,16},{1,17},{2,18},{3,19},{4,20},{5,21},{6,22},{7,23},{8,56},{9,... | collective-permute-start | bytes 196616 | tf_op jit(solution)/shard_map/ppermute | solution.py:61
  7.5 6.4 %collective-permute-start.5 = (bf16[2,1,64,384]{3,2,1,0:T(8,128)(2,1)S(1)}, bf16[2,1,64,384]{3,2,1,0:T(8,128)(2,1)S(1)}, u32[]{:S(2)}, u32[]{:S(2)}) collective-permute-start(bf16[2,1,64,384]{3,2,1,0:T(8,128)(2,1)S(1)} %pad_maximum_fusion.14), channel_id=1, source_target_pairs={{0,65},{1,64},{2,67},{3,66},{4,69},{5,68},{6,71},{7,70},{8,9},{9,8... | collective-permute-start | bytes 294920 | tf_op jit(solution)/shard_map/ppermute | solution.py:61
  9.5 6.3 %collective-permute-start.7 = (bf16[2,1,64,512]{3,2,1,0:T(8,128)(2,1)S(1)}, bf16[2,1,64,512]{3,2,1,0:T(8,128)(2,1)S(1)}, u32[]{:S(2)}, u32[]{:S(2)}) collective-permute-start(bf16[2,1,64,512]{3,2,1,0:T(8,128)(2,1)S(1)} %pad_maximum_fusion.13), channel_id=1, source_target_pairs={{0,6},{1,7},{2,4},{3,5},{4,2},{5,3},{6,0},{7,1},{8,10},{9,11},{10,... | collective-permute-start | bytes 393224 | tf_op jit(solution)/shard_map/ppermute | solution.py:61
  10.7 6.3 %collective-permute-start.3 = (bf16[2,1,64,512]{3,2,1,0:T(8,128)(2,1)S(1)}, bf16[2,1,64,512]{3,2,1,0:T(8,128)(2,1)S(1)}, u32[]{:S(2)}, u32[]{:S(2)}) collective-permute-start(bf16[2,1,64,512]{3,2,1,0:T(8,128)(2,1)S(1)} %pad_maximum_fusion.12), channel_id=1, source_target_pairs={{0,48},{1,49},{2,50},{3,51},{4,52},{5,53},{6,54},{7,55},{8,24},{9,... | collective-permute-start | bytes 393224 | tf_op jit(solution)/shard_map/ppermute | solution.py:61
  17.0 5.7 %collective-permute-start.10 = (bf16[4,64,384]{2,1,0:T(8,128)(2,1)S(1)}, bf16[4,64,384]{2,1,0:T(8,128)(2,1)S(1)}, u32[]{:S(2)}, u32[]{:S(2)}) collective-permute-start(bf16[4,64,384]{2,1,0:T(8,128)(2,1)S(1)} %maximum_bitcast_fusion.2), channel_id=1, source_target_pairs={{0,2},{1,3},{2,0},{3,1},{4,6},{5,7},{6,4},{7,5},{8,14},{9,15},{10,... | collective-permute-start | bytes 589832 | tf_op jit(solution)/shard_map/ppermute | solution.py:61
  17.2 7.8 %collective-permute-start.8 = (bf16[4,64,512]{2,1,0:T(8,128)(2,1)S(1)}, bf16[4,64,512]{2,1,0:T(8,128)(2,1)S(1)}, u32[]{:S(2)}, u32[]{:S(2)}) collective-permute-start(bf16[4,64,512]{2,1,0:T(8,128)(2,1)S(1)} %maximum_bitcast_fusion), channel_id=1, source_target_pairs={{0,1},{1,0},{2,3},{3,2},{4,5},{5,4},{6,7},{7,6},{8,73},{9,72},{10,... | collective-permute-start | bytes 786440 | tf_op jit(solution)/shard_map/ppermute | solution.py:61
  19.4 6.4 %collective-permute-start.12 = (bf16[4,64,512]{2,1,0:T(8,128)(2,1)S(1)}, bf16[4,64,512]{2,1,0:T(8,128)(2,1)S(1)}, u32[]{:S(2)}, u32[]{:S(2)}) collective-permute-start(bf16[4,64,512]{2,1,0:T(8,128)(2,1)S(1)} %maximum_bitcast_fusion.1), channel_id=1, source_target_pairs={{0,16},{1,17},{2,18},{3,19},{4,20},{5,21},{6,22},{7,23},{8,56},{9,... | collective-permute-start | bytes 786440 | tf_op jit(solution)/shard_map/ppermute | solution.py:61
  22.8 9.1 %collective-permute-start.11 = (bf16[2,4,64,384]{3,2,1,0:T(8,128)(2,1)S(1)}, bf16[2,4,64,384]{3,2,1,0:T(8,128)(2,1)S(1)}, u32[]{:S(2)}, u32[]{:S(2)}) collective-permute-start(bf16[2,4,64,384]{3,2,1,0:T(8,128)(2,1)S(1)} %pad_maximum_fusion.11), channel_id=1, source_target_pairs={{0,6},{1,7},{2,4},{3,5},{4,2},{5,3},{6,0},{7,1},{8,10},{9,11},{10,... | collective-permute-start | bytes 1179656 | tf_op jit(solution)/shard_map/ppermute | solution.py:61
  25.1 9.3 %collective-permute-start.9 = (bf16[2,4,64,512]{3,2,1,0:T(8,128)(2,1)S(1)}, bf16[2,4,64,512]{3,2,1,0:T(8,128)(2,1)S(1)}, u32[]{:S(2)}, u32[]{:S(2)}) collective-permute-start(bf16[2,4,64,512]{3,2,1,0:T(8,128)(2,1)S(1)} %pad_maximum_fusion.9), channel_id=1, source_target_pairs={{0,65},{1,64},{2,67},{3,66},{4,69},{5,68},{6,71},{7,70},{8,9},{9,8... | collective-permute-start | bytes 1572872 | tf_op jit(solution)/shard_map/ppermute | solution.py:61
  25.8 10.5 %collective-permute-start.13 = (bf16[2,4,64,512]{3,2,1,0:T(8,128)(2,1)S(1)}, bf16[2,4,64,512]{3,2,1,0:T(8,128)(2,1)S(1)}, u32[]{:S(2)}, u32[]{:S(2)}) collective-permute-start(bf16[2,4,64,512]{3,2,1,0:T(8,128)(2,1)S(1)} %pad_maximum_fusion.10), channel_id=1, source_target_pairs={{0,48},{1,49},{2,50},{3,51},{4,52},{5,53},{6,54},{7,55},{8,24},{9,... | collective-permute-start | bytes 1572872 | tf_op jit(solution)/shard_map/ppermute | solution.py:61
  36.4 14.9 %collective-permute-start.14 = (bf16[16,64,512]{2,1,0:T(8,128)(2,1)S(1)}, bf16[16,64,512]{2,1,0:T(8,128)(2,1)S(1)}, u32[]{:S(2)}, u32[]{:S(2)}) collective-permute-start(bf16[16,64,512]{2,1,0:T(8,128)(2,1)S(1)} %bitcast.152), channel_id=1, source_target_pairs={{0,2},{1,3},{2,0},{3,1},{4,6},{5,7},{6,4},{7,5},{8,14},{9,15},{10,... | collective-permute-start | bytes 3145736 | tf_op jit(solution)/shard_map/ppermute | solution.py:61
  38.4 19.4 %collective-permute-start.18 = (bf16[16,64,512]{2,1,0:T(8,128)(2,1)S(1)}, bf16[16,64,512]{2,1,0:T(8,128)(2,1)S(1)}, u32[]{:S(2)}, u32[]{:S(2)}) collective-permute-start(bf16[16,64,512]{2,1,0:T(8,128)(2,1)S(1)} %bitcast.155), channel_id=1, source_target_pairs={{0,1},{1,0},{2,3},{3,2},{4,5},{5,4},{6,7},{7,6},{8,73},{9,72},{10,... | collective-permute-start | bytes 3145736 | tf_op jit(solution)/shard_map/ppermute | solution.py:61
  39.2 20.4 %collective-permute-start.16 = (bf16[16,64,384]{2,1,0:T(8,128)(2,1)S(1)}, bf16[16,64,384]{2,1,0:T(8,128)(2,1)S(1)}, u32[]{:S(2)}, u32[]{:S(2)}) collective-permute-start(bf16[16,64,384]{2,1,0:T(8,128)(2,1)S(1)} %bitcast.158), channel_id=1, source_target_pairs={{0,16},{1,17},{2,18},{3,19},{4,20},{5,21},{6,22},{7,23},{8,56},{9,... | collective-permute-start | bytes 2359304 | tf_op jit(solution)/shard_map/ppermute | solution.py:61
  51.3 1.7 copy-start
  53.0 31.1 %collective-permute-start.15 = (bf16[2,16,64,512]{3,2,1,0:T(8,128)(2,1)}, bf16[2,16,64,512]{3,2,1,0:T(8,128)(2,1)}, u32[]{:S(2)}, u32[]{:S(2)}) collective-permute-start(bf16[2,16,64,512]{3,2,1,0:T(8,128)(2,1)} %pad_maximum_fusion.1), channel_id=1, source_target_pairs={{0,6},{1,7},{2,4},{3,5},{4,2},{5,3},{6,0},{7,1},{8,10},{9,11},{10,... | collective-permute-start | bytes 6291464 | tf_op jit(solution)/shard_map/ppermute | solution.py:61
  57.9 1.7 copy-start.2
  59.6 26.4 %collective-permute-start.19 = (bf16[2,16,64,512]{3,2,1,0:T(8,128)(2,1)}, bf16[2,16,64,512]{3,2,1,0:T(8,128)(2,1)}, u32[]{:S(2)}, u32[]{:S(2)}) collective-permute-start(bf16[2,16,64,512]{3,2,1,0:T(8,128)(2,1)} %pad_maximum_fusion.3), channel_id=1, source_target_pairs={{0,65},{1,64},{2,67},{3,66},{4,69},{5,68},{6,71},{7,70},{8,9},{9,8... | collective-permute-start | bytes 6291464 | tf_op jit(solution)/shard_map/ppermute | solution.py:61
  59.6 1.4 copy-start.4
  59.6 5.8 %copy-start.10 = (bf16[3,208,64]{1,2,0:T(8,128)(2,1)S(1)}, bf16[3,208,64]{1,2,0:T(8,128)(2,1)}, u32[]{:S(2)}) copy-start(bf16[3,208,64]{1,2,0:T(8,128)(2,1)} %param.6) | copy-start | bytes 239620
  61.0 23.1 %collective-permute-start.17 = (bf16[2,16,64,384]{3,2,1,0:T(8,128)(2,1)}, bf16[2,16,64,384]{3,2,1,0:T(8,128)(2,1)}, u32[]{:S(2)}, u32[]{:S(2)}) collective-permute-start(bf16[2,16,64,384]{3,2,1,0:T(8,128)(2,1)} %pad_maximum_fusion.5), channel_id=1, source_target_pairs={{0,48},{1,49},{2,50},{3,51},{4,52},{5,53},{6,54},{7,55},{8,24},{9,... | collective-permute-start | bytes 4718600 | tf_op jit(solution)/shard_map/ppermute | solution.py:61
  65.5 3.5 %copy-start.7 = (bf16[3,208,64]{2,1,0:T(8,128)(2,1)}, bf16[3,208,64]{2,1,0:T(8,128)(2,1)S(1)}, u32[]{:S(2)}) copy-start(bf16[3,208,64]{2,1,0:T(8,128)(2,1)S(1)} %copy.6.a_mine) | copy-start | bytes 239620
  65.5 6.5 %collective-permute-start.1 = (bf16[3,208,64]{2,1,0:T(8,128)(2,1)S(1)}, bf16[3,208,64]{2,1,0:T(8,128)(2,1)S(1)}, u32[]{:S(2)}, u32[]{:S(2)}) collective-permute-start(bf16[3,208,64]{2,1,0:T(8,128)(2,1)S(1)} %copy.6.a_mine), channel_id=1, source_target_pairs={{0,8},{1,9},{2,10},{3,11},{4,12},{5,13},{6,14},{7,15},{8,0},{9,1},... | collective-permute-start | bytes 239624 | tf_op jit(solution)/shard_map/ppermute | solution.py:61
  66.4 2.6 %copy-start.3 = (bf16[16,64,512]{2,1,0:T(8,128)(2,1)S(1)}, bf16[16,64,512]{2,1,0:T(8,128)(2,1)}, u32[]{:S(2)}) copy-start(bf16[16,64,512]{2,1,0:T(8,128)(2,1)} %copy-done.2) | copy-start | bytes 3145732
  69.0 1.5 copy-start.1
  72.0 13.9 %copy-start.9 = (bf16[3,208,64]{2,1,0:T(8,128)(2,1)}, bf16[3,208,64]{2,1,0:T(8,128)(2,1)S(1)}, u32[]{:S(2)}) copy-start(bf16[3,208,64]{2,1,0:T(8,128)(2,1)S(1)} %collective-permute-done.1.a_other) | copy-start | bytes 239620
  101.3 2.9 %collective-permute-start.20 = (bf16[2,2,208,512]{3,2,1,0:T(8,128)(2,1)}, bf16[2,2,208,512]{3,2,1,0:T(8,128)(2,1)S(1)}, u32[]{:S(2)}, u32[]{:S(2)}) collective-permute-start(bf16[2,2,208,512]{3,2,1,0:T(8,128)(2,1)} %get-tuple-element.31.mine), channel_id=1, source_target_pairs={{0,8},{1,9},{2,10},{3,11},{4,12},{5,13},{6,14},{7,15},{8,0},{9,1},... | collective-permute-start | bytes 2555912 | tf_op jit(solution)/shard_map/ppermute | solution.py:61
  114.9 21.9 %collective-permute-start.21 = (bf16[2,16,64,384]{3,2,1,0:T(8,128)(2,1)}, bf16[2,16,64,384]{3,2,1,0:T(8,128)(2,1)S(1)}, u32[]{:S(2)}, u32[]{:S(2)}) collective-permute-start(bf16[2,16,64,384]{3,2,1,0:T(8,128)(2,1)} %bitcast.196), channel_id=1, source_target_pairs={{0,6},{1,7},{2,4},{3,5},{4,2},{5,3},{6,0},{7,1},{8,10},{9,11},{10,... | collective-permute-start | bytes 4718600 | tf_op jit(solution)/shard_map/ppermute | solution.py:61
  115.0 24.6 %collective-permute-start.23 = (bf16[2,16,64,384]{3,2,1,0:T(8,128)(2,1)}, bf16[2,16,64,384]{3,2,1,0:T(8,128)(2,1)S(1)}, u32[]{:S(2)}, u32[]{:S(2)}) collective-permute-start(bf16[2,16,64,384]{3,2,1,0:T(8,128)(2,1)} %bitcast.195), channel_id=1, source_target_pairs={{0,48},{1,49},{2,50},{3,51},{4,52},{5,53},{6,54},{7,55},{8,24},{9,... | collective-permute-start | bytes 4718600 | tf_op jit(solution)/shard_map/ppermute | solution.py:61
  119.4 21.5 %collective-permute-start.25 = (bf16[2,16,64,384]{3,2,1,0:T(8,128)(2,1)}, bf16[2,16,64,384]{3,2,1,0:T(8,128)(2,1)S(1)}, u32[]{:S(2)}, u32[]{:S(2)}) collective-permute-start(bf16[2,16,64,384]{3,2,1,0:T(8,128)(2,1)} %bitcast.194), channel_id=1, source_target_pairs={{0,65},{1,64},{2,67},{3,66},{4,69},{5,68},{6,71},{7,70},{8,9},{9,8... | collective-permute-start | bytes 4718600 | tf_op jit(solution)/shard_map/ppermute | solution.py:61
  138.9 12.1 %collective-permute-start.22 = (bf16[16,64,384]{2,1,0:T(8,128)(2,1)S(1)}, bf16[16,64,384]{2,1,0:T(8,128)(2,1)S(1)}, u32[]{:S(2)}, u32[]{:S(2)}) collective-permute-start(bf16[16,64,384]{2,1,0:T(8,128)(2,1)S(1)} %slice_bitcast_fusion.4), channel_id=1, source_target_pairs={{0,2},{1,3},{2,0},{3,1},{4,6},{5,7},{6,4},{7,5},{8,14},{9,15},{10,... | collective-permute-start | bytes 2359304 | tf_op jit(solution)/shard_map/ppermute | solution.py:61
  140.8 12.1 %collective-permute-start.24 = (bf16[16,64,384]{2,1,0:T(8,128)(2,1)S(1)}, bf16[16,64,384]{2,1,0:T(8,128)(2,1)S(1)}, u32[]{:S(2)}, u32[]{:S(2)}) collective-permute-start(bf16[16,64,384]{2,1,0:T(8,128)(2,1)S(1)} %slice_bitcast_fusion.2), channel_id=1, source_target_pairs={{0,16},{1,17},{2,18},{3,19},{4,20},{5,21},{6,22},{7,23},{8,56},{9,... | collective-permute-start | bytes 2359304 | tf_op jit(solution)/shard_map/ppermute | solution.py:61
  142.8 12.4 %collective-permute-start.26 = (bf16[16,64,384]{2,1,0:T(8,128)(2,1)S(1)}, bf16[16,64,384]{2,1,0:T(8,128)(2,1)S(1)}, u32[]{:S(2)}, u32[]{:S(2)}) collective-permute-start(bf16[16,64,384]{2,1,0:T(8,128)(2,1)S(1)} %slice_bitcast_fusion), channel_id=1, source_target_pairs={{0,1},{1,0},{2,3},{3,2},{4,5},{5,4},{6,7},{7,6},{8,73},{9,72},{10,... | collective-permute-start | bytes 2359304 | tf_op jit(solution)/shard_map/ppermute | solution.py:61
  155.4 8.4 %collective-permute-start.27 = (bf16[2,4,64,384]{3,2,1,0:T(8,128)(2,1)S(1)}, bf16[2,4,64,384]{3,2,1,0:T(8,128)(2,1)S(1)}, u32[]{:S(2)}, u32[]{:S(2)}) collective-permute-start(bf16[2,4,64,384]{3,2,1,0:T(8,128)(2,1)S(1)} %bitcast.187), channel_id=1, source_target_pairs={{0,65},{1,64},{2,67},{3,66},{4,69},{5,68},{6,71},{7,70},{8,9},{9,8... | collective-permute-start | bytes 1179656 | tf_op jit(solution)/shard_map/ppermute | solution.py:61
  158.2 9.3 %collective-permute-start.31 = (bf16[2,4,64,384]{3,2,1,0:T(8,128)(2,1)S(1)}, bf16[2,4,64,384]{3,2,1,0:T(8,128)(2,1)S(1)}, u32[]{:S(2)}, u32[]{:S(2)}) collective-permute-start(bf16[2,4,64,384]{3,2,1,0:T(8,128)(2,1)S(1)} %bitcast.186), channel_id=1, source_target_pairs={{0,48},{1,49},{2,50},{3,51},{4,52},{5,53},{6,54},{7,55},{8,24},{9,... | collective-permute-start | bytes 1179656 | tf_op jit(solution)/shard_map/ppermute | solution.py:61
  161.8 9.1 %collective-permute-start.29 = (bf16[2,4,64,384]{3,2,1,0:T(8,128)(2,1)S(1)}, bf16[2,4,64,384]{3,2,1,0:T(8,128)(2,1)S(1)}, u32[]{:S(2)}, u32[]{:S(2)}) collective-permute-start(bf16[2,4,64,384]{3,2,1,0:T(8,128)(2,1)S(1)} %bitcast.185), channel_id=1, source_target_pairs={{0,6},{1,7},{2,4},{3,5},{4,2},{5,3},{6,0},{7,1},{8,10},{9,11},{10,... | collective-permute-start | bytes 1179656 | tf_op jit(solution)/shard_map/ppermute | solution.py:61
  163.9 7.8 %collective-permute-start.28 = (bf16[4,64,384]{2,1,0:T(8,128)(2,1)S(1)}, bf16[4,64,384]{2,1,0:T(8,128)(2,1)S(1)}, u32[]{:S(2)}, u32[]{:S(2)}) collective-permute-start(bf16[4,64,384]{2,1,0:T(8,128)(2,1)S(1)} %slice_bitcast_fusion.10), channel_id=1, source_target_pairs={{0,1},{1,0},{2,3},{3,2},{4,5},{5,4},{6,7},{7,6},{8,73},{9,72},{10,... | collective-permute-start | bytes 589832 | tf_op jit(solution)/shard_map/ppermute | solution.py:61
  167.6 6.8 %collective-permute-start.32 = (bf16[4,64,384]{2,1,0:T(8,128)(2,1)S(1)}, bf16[4,64,384]{2,1,0:T(8,128)(2,1)S(1)}, u32[]{:S(2)}, u32[]{:S(2)}) collective-permute-start(bf16[4,64,384]{2,1,0:T(8,128)(2,1)S(1)} %slice_bitcast_fusion.6), channel_id=1, source_target_pairs={{0,16},{1,17},{2,18},{3,19},{4,20},{5,21},{6,22},{7,23},{8,56},{9,... | collective-permute-start | bytes 589832 | tf_op jit(solution)/shard_map/ppermute | solution.py:61
  171.0 6.8 %collective-permute-start.30 = (bf16[4,64,384]{2,1,0:T(8,128)(2,1)S(1)}, bf16[4,64,384]{2,1,0:T(8,128)(2,1)S(1)}, u32[]{:S(2)}, u32[]{:S(2)}) collective-permute-start(bf16[4,64,384]{2,1,0:T(8,128)(2,1)S(1)} %slice_bitcast_fusion.8), channel_id=1, source_target_pairs={{0,2},{1,3},{2,0},{3,1},{4,6},{5,7},{6,4},{7,5},{8,14},{9,15},{10,... | collective-permute-start | bytes 589832 | tf_op jit(solution)/shard_map/ppermute | solution.py:61
  174.5 17.1 %copy-start.11 = (bf16[64,1024]{1,0:T(8,128)(2,1)S(1)}, bf16[64,1024]{1,0:T(8,128)(2,1)}, u32[]{:S(2)}) copy-start(bf16[64,1024]{1,0:T(8,128)(2,1)} %get-tuple-element.44) | copy-start | bytes 393220
  177.8 6.0 %collective-permute-start.37 = (bf16[2,1,64,384]{3,2,1,0:T(8,128)(2,1)S(1)}, bf16[2,1,64,384]{3,2,1,0:T(8,128)(2,1)S(1)}, u32[]{:S(2)}, u32[]{:S(2)}) collective-permute-start(bf16[2,1,64,384]{3,2,1,0:T(8,128)(2,1)S(1)} %slice_bitcast_fusion.12), channel_id=1, source_target_pairs={{0,6},{1,7},{2,4},{3,5},{4,2},{5,3},{6,0},{7,1},{8,10},{9,11},{10,... | collective-permute-start | bytes 294920 | tf_op jit(solution)/shard_map/ppermute | solution.py:61
  178.0 6.9 %collective-permute-start.35 = (bf16[2,1,64,384]{3,2,1,0:T(8,128)(2,1)S(1)}, bf16[2,1,64,384]{3,2,1,0:T(8,128)(2,1)S(1)}, u32[]{:S(2)}, u32[]{:S(2)}) collective-permute-start(bf16[2,1,64,384]{3,2,1,0:T(8,128)(2,1)S(1)} %slice_bitcast_fusion.13), channel_id=1, source_target_pairs={{0,65},{1,64},{2,67},{3,66},{4,69},{5,68},{6,71},{7,70},{8,9},{9,8... | collective-permute-start | bytes 294920 | tf_op jit(solution)/shard_map/ppermute | solution.py:61
  178.4 8.9 %collective-permute-start.33 = (bf16[2,1,64,384]{3,2,1,0:T(8,128)(2,1)S(1)}, bf16[2,1,64,384]{3,2,1,0:T(8,128)(2,1)S(1)}, u32[]{:S(2)}, u32[]{:S(2)}) collective-permute-start(bf16[2,1,64,384]{3,2,1,0:T(8,128)(2,1)S(1)} %slice_bitcast_fusion.14), channel_id=1, source_target_pairs={{0,48},{1,49},{2,50},{3,51},{4,52},{5,53},{6,54},{7,55},{8,24},{9,... | collective-permute-start | bytes 294920 | tf_op jit(solution)/shard_map/ppermute | solution.py:61
  183.9 5.6 %collective-permute-start.38 = (bf16[1,64,384]{2,1,0:T(8,128)(2,1)S(1)}, bf16[1,64,384]{2,1,0:T(8,128)(2,1)S(1)}, u32[]{:S(2)}, u32[]{:S(2)}) collective-permute-start(bf16[1,64,384]{2,1,0:T(8,128)(2,1)S(1)} %slice_bitcast_fusion.15), channel_id=1, source_target_pairs={{0,2},{1,3},{2,0},{3,1},{4,6},{5,7},{6,4},{7,5},{8,14},{9,15},{10,... | collective-permute-start | bytes 147464 | tf_op jit(solution)/shard_map/ppermute | solution.py:61
  184.9 4.6 %collective-permute-start.36 = (bf16[1,64,384]{2,1,0:T(8,128)(2,1)S(1)}, bf16[1,64,384]{2,1,0:T(8,128)(2,1)S(1)}, u32[]{:S(2)}, u32[]{:S(2)}) collective-permute-start(bf16[1,64,384]{2,1,0:T(8,128)(2,1)S(1)} %slice_bitcast_fusion.17), channel_id=1, source_target_pairs={{0,1},{1,0},{2,3},{3,2},{4,5},{5,4},{6,7},{7,6},{8,73},{9,72},{10,... | collective-permute-start | bytes 147464 | tf_op jit(solution)/shard_map/ppermute | solution.py:61
  187.4 4.2 %collective-permute-start.34 = (bf16[1,64,384]{2,1,0:T(8,128)(2,1)S(1)}, bf16[1,64,384]{2,1,0:T(8,128)(2,1)S(1)}, u32[]{:S(2)}, u32[]{:S(2)}) collective-permute-start(bf16[1,64,384]{2,1,0:T(8,128)(2,1)S(1)} %slice_bitcast_fusion.19), channel_id=1, source_target_pairs={{0,16},{1,17},{2,18},{3,19},{4,20},{5,21},{6,22},{7,23},{8,56},{9,... | collective-permute-start | bytes 147464 | tf_op jit(solution)/shard_map/ppermute | solution.py:61
  (3 other events, 3.7 us)

commit v3 on v2

--- a/solution.py
+++ b/solution.py
@@ -15,9 +15,6 @@
 RANK = 64
 WIDE = BLOCK + 128
 PART = WIDE // 3
-SYNC = True
-RSYNC = True
-DIRECT = 0
 ORDERS = ((1, 2, 0), (2, 0, 1), (0, 1, 2))
 VMEM = 60 * 1024 * 1024
 
@@ -44,16 +41,6 @@
 SECOND = [axis_pairs(a, False) for a in range(3)]
 
 
-def across_pairs(axis):
-    def move(x, y, z, c):
-        q = [x, y, z]
-        q[axis] ^= 2
-        return (*q, c)
-
-    return pairs(move)
-
-
-ACROSS = [across_pairs(a) for a in range(3)]
 CORES = pairs(lambda x, y, z, c: (x, y, z, 1 - c))
 
 
@@ -61,44 +48,38 @@
     return lax.ppermute(value, NAMES, table)
 
 
-def gather(values):
-    for stage in range(3):
+def gather(values, late):
+    for stage in range(2):
         axes = [order[stage] for order in ORDERS]
-        if stage < DIRECT:
-            got = [
-                [v] + [send(v, t[a]) for t in (FIRST, SECOND, ACROSS)]
-                for v, a in zip(values, axes)
-            ]
-            values = [jnp.stack(g).reshape(-1, *g[0].shape[1:]) for g in got]
-            if SYNC: values = lax.optimization_barrier(values)
-            continue
         mine = [jnp.stack([v, send(v, FIRST[a])]) for v, a in zip(values, axes)]
-        if False: mine = lax.optimization_barrier(mine)
         theirs = [send(v, SECOND[a]) for v, a in zip(mine, axes)]
-        if stage < 2:
-            values = [
-                jnp.concatenate(p).reshape(-1, *v.shape[1:])
-                for p, v in zip(zip(mine, theirs), values)
-            ]
-            if SYNC: values = lax.optimization_barrier(values)
-    return [b for p in zip(mine, theirs) for b in p]
-
-
-def scatter(keep, away):
-    for stage in range(2, -1, -1):
+        values = [
+            jnp.concatenate(p).reshape(-1, *v.shape[1:])
+            for p, v in zip(zip(mine, theirs), values)
+        ]
+        if stage == 1:
+            values[1], late = lax.optimization_barrier((values[1], late))
+    out = []
+    for v, order in zip(values, ORDERS):
+        near = send(v, FIRST[order[2]])
+        out += [v, near, send(v, SECOND[order[2]]), send(near, SECOND[order[2]])]
+    return out, late
+
+
+def scatter(sums):
+    totals = []
+    for part, order in enumerate(ORDERS):
+        blocks = [v.reshape(16, GROUP, PART) for v in sums[4 * part : 4 * part + 4]]
+        across = blocks[1] + send(blocks[3], SECOND[order[2]])
+        second = send(blocks[2], SECOND[order[2]])
+        first = send(across, FIRST[order[2]])
+        total = sum(v.astype(jnp.float32) for v in (blocks[0], second, first))
+        totals.append(total.astype(jnp.bfloat16))
+    for stage in (1, 0):
         axes = [order[stage] for order in ORDERS]
-        if stage < 2:
-            keep, away = zip(*(t.reshape(2, 2, -1, GROUP, PART) for t in totals))
-        if stage < DIRECT:
-            totals = []
-            for k, w, a in zip(keep, away, axes):
-                got = [send(k[1], FIRST[a]), send(w[0], SECOND[a]), send(w[1], ACROSS[a])]
-                totals.append(sum((g.astype(jnp.float32) for g in got), k[0].astype(jnp.float32)).astype(jnp.bfloat16))
-            continue
-        pairs_ = [k + send(w, SECOND[a]) for k, w, a in zip(keep, away, axes)]
-        if False: pairs_ = lax.optimization_barrier(pairs_)
-        totals = [p[0] + send(p[1], FIRST[a]) for p, a in zip(pairs_, axes)]
-        if RSYNC and stage > 0: totals = lax.optimization_barrier(totals)
+        keep, away = zip(*(t.reshape(2, 2, -1, GROUP, PART) for t in totals))
+        halves = [k + send(w, SECOND[a]) for k, w, a in zip(keep, away, axes)]
+        totals = [p[0] + send(p[1], FIRST[a]) for p, a in zip(halves, axes)]
     return [t.reshape(GROUP, PART) for t in totals]
 
 
@@ -126,7 +107,7 @@
 
 
 def up_kernel(place, w, wo, a_mine, a_other, *refs):
-    blocks, (out, factor, ws, xs, acc, wsems, xsems, bsems, fsem) = refs[:6], refs[6:]
+    blocks, (out, factor, ws, xs, acc, wsems, xsems, bsems, fsem) = refs[:12], refs[12:]
     core = place[0]
     at = [[coordinate(place[1 + a], k, core) for k in range(4)] for a in range(3)]
     near = place[3] // 2
@@ -141,31 +122,31 @@
                 copy(source.at[k, :, columns], ws.at[block, rows], wsems.at[block])
 
     weights(*steps[0])
-    left, middle, right = (blocks[i : i + 2] for i in (0, 2, 4))
+    left, middle, right = (blocks[i : i + 4] for i in (0, 4, 8))
     for kz in range(4):
         zh, zl = at[2][kz] // 2, at[2][kz] & 1
         block = pl.ds(4 * zh, 4)
         last = BLOCK - 2 * PART
         copy(
-            right[kz // 2].at[kz % 2, :, :, :, pl.ds(0, last)],
+            right[kz].at[:, :, :, pl.ds(0, last)],
             xs.at[block, :, zl, :, pl.ds(2 * PART, last)],
             xsems.at[zh],
         )
         for k in range(4):
             copy(
-                left[k // 2].at[k % 2, kz, :, :, pl.ds(0, PART)],
+                left[k].at[kz, :, :, pl.ds(0, PART)],
                 xs.at[block, k, zl, :, pl.ds(0, PART)],
                 xsems.at[zh],
             )
             copy(
-                middle[k // 2].at[k % 2, :, kz],
+                middle[k].at[:, kz],
                 xs.at[4 * zh + k, :, zl, :, pl.ds(PART, PART)],
                 xsems.at[zh],
             )
             columns = pl.ds(pl.multiple_of((2 * at[0][k] + zl) * 128, 128), 128)
             for part in range(2):
                 copy(
-                    right[kz // 2].at[kz % 2, :, k, :, pl.ds(last + part * 128, 128)],
+                    right[kz].at[:, k, :, pl.ds(last + part * 128, 128)],
                     ws.at[block, pl.ds(4 * ROWS + part * RANK, RANK), columns],
                     bsems.at[zh],
                 )
@@ -173,7 +154,7 @@
         for kz in (0, 1 + core):
             zl = place[3] & 1 if isinstance(kz, int) else 1 - (place[3] & 1)
             columns = pl.ds(pl.multiple_of((2 * at[0][k] + zl) * 128, 128), 128)
-            copy(left[k // 2].at[k % 2, kz, 0, :, pl.ds(PART, 128)], factor.at[:, columns], fsem)
+            copy(left[k].at[kz, 0, :, pl.ds(PART, 128)], factor.at[:, columns], fsem)
     for j in range(1, NB):
         weights(*steps[j])
 
@@ -209,7 +190,7 @@
             jax.ShapeDtypeStruct((2, 2, ROWS, TOK), jnp.bfloat16),
             jax.ShapeDtypeStruct((RANK, BLOCK), jnp.bfloat16),
         ],
-        in_specs=[SCALARS, ANY, ANY, ON_CHIP, ON_CHIP, *[ANY] * 6],
+        in_specs=[SCALARS, ANY, ANY, ON_CHIP, ON_CHIP, *[ANY] * 12],
         out_specs=[ON_CHIP, ON_CHIP],
         scratch_shapes=[
             pltpu.VMEM((NB, 4 * ROWS + 2 * RANK, BLOCK), jnp.bfloat16),
@@ -226,7 +207,7 @@
 
 
 def down_kernel(place, mine, other, w, wo, a_mine, a_other, *refs):
-    outs, (ws, hidden, ob, wsems, osems) = refs[:6], refs[6:]
+    outs, (ws, hidden, ob, wsems, osems) = refs[:12], refs[12:]
     core = place[0]
     for j in range(NB):
         there = 2 * (4 * (j // 4) + coordinate(place[2], j % 4, core)) + core
@@ -248,7 +229,7 @@
     low = jnp.dot(hidden[...], factor, preferred_element_type=f32)
     low = jnp.concatenate([low, jnp.zeros_like(low)], axis=1).astype(jnp.bfloat16)
     rel_z = [relative(place[3], z, core) for z in range(4)]
-    left, middle, right = (outs[i : i + 2] for i in (0, 2, 4))
+    left, middle, right = (outs[i : i + 4] for i in (0, 4, 8))
     for j in range(NB):
         zh, ky = j // 4, j % 4
         await_all(ws.at[j], wsems.at[j])
@@ -260,21 +241,21 @@
             for kx in range(4):
                 copy(
                     ob.at[j, kx, zl, :, pl.ds(0, PART)],
-                    left[kx // 2].at[kx % 2, kz, ky],
+                    left[kx].at[kz, ky],
                     osems.at[j],
                 )
             copy(
                 ob.at[j, :, zl, :, pl.ds(PART, PART)],
-                middle[ky // 2].at[ky % 2, :, kz],
+                middle[ky].at[:, kz],
                 osems.at[j],
             )
-            for half in range(2):
-
-                @pl.when(kz // 2 == half)
+            for k in range(4):
+
+                @pl.when(kz == k)
                 def _():
                     copy(
                         ob.at[j, :, zl, :, pl.ds(2 * PART, PART)],
-                        right[half].at[kz % 2, ky],
+                        right[k].at[ky],
                         osems.at[j],
                     )
     for j in range(NB):
@@ -284,9 +265,9 @@
 def down(place, mine, other, weights, others, a_mine, a_other):
     return pl.pallas_call(
         down_kernel,
-        out_shape=[jax.ShapeDtypeStruct((2, 4, 4, GROUP, PART), jnp.bfloat16)] * 6,
+        out_shape=[jax.ShapeDtypeStruct((4, 4, GROUP, PART), jnp.bfloat16)] * 12,
         in_specs=[SCALARS, ON_CHIP, ON_CHIP, ANY, ANY, ON_CHIP, ON_CHIP],
-        out_specs=[ANY] * 6,
+        out_specs=[ANY] * 12,
         scratch_shapes=[
             pltpu.VMEM((NB, 2 * ROWS, BLOCK), jnp.bfloat16),
             pltpu.VMEM((TOK, 2 * ROWS), jnp.bfloat16),
@@ -304,19 +285,16 @@
     others = send(frozen_weights, CORES)
     a_other = send(hidden_adapter_factor, CORES)
     gate_factor, up_factor, down_factor = feature_adapter_factor
-    blocks = gather([
+    blocks, (others, a_other) = gather([
         jnp.concatenate([tokens[:, :PART], down_factor], axis=1)[None],
         tokens[None, :, PART : 2 * PART],
         jnp.concatenate([tokens[:, 2 * PART :], gate_factor, up_factor], axis=1)[None],
-    ])
-    blocks = [v.reshape(2, 4, 4, *v.shape[2:]) for v in blocks]
+    ], (others, a_other))
+    blocks = [v.reshape(4, 4, *v.shape[1:]) for v in blocks]
     mine, factor = up(place, frozen_weights, others, hidden_adapter_factor, a_other, blocks)
     theirs = send(mine, CORES)
     sums = down(place, mine, theirs, frozen_weights, others, hidden_adapter_factor, a_other)
-    left, middle, right = scatter(
-        [v.reshape(2, 16, GROUP, PART) for v in sums[::2]],
-        [v.reshape(2, 16, GROUP, PART) for v in sums[1::2]],
-    )
+    left, middle, right = scatter(sums)
     last = BLOCK - 2 * PART
     plain = jnp.concatenate([left, middle, right[:, :last]], axis=1).astype(jnp.float32)
     extra = jnp.dot(

time: 196 us -> 188 us (0.959); the launches traced: 192 us -> 187 us
  waiting for transfers between devices: 82.3 us -> 97.8 us
  starting transfers between devices: 62.5 us -> 52.6 us
  other arithmetic: 15.4 us -> 6.35 us
    ppermute x39 -> x45, waiting for transfers between devices: 82.3 us -> 97.8 us  [send(): return lax.ppermute(value, NAMES, table)]
    ppermute x39 -> x45, starting transfers between devices: 62.5 us -> 52.6 us  [send(): return lax.ppermute(value, NAMES, table)]
    another operation x14 -> x11, other arithmetic: 10.6 us -> 1.08 us  [gather(): mine = [jnp.stack([v, send(v, FIRST[a])]) for v, a in zip(values, axes)]]
  transfers between devices with their start and end apart: 39 -> 45, of which waited for: 21 -> 22; matrix products, arithmetic and copies ran while one was open for 10% -> 5% of each run, Pallas kernels for 0% -> 0%
where the time goes in v3:
time: 188 us; the launch traced here: 187 us
  waiting for transfers between devices  97.8 us (52%)
  starting transfers between devices  52.6 us (28%)
  Pallas kernels  25.3 us (13%)
  other arithmetic  6.35 us (3%)
  local copies, waits for them, and re-layouts  3.92 us (2%)
    ppermute x45, waiting for transfers between devices, send(): return lax.ppermute(value, NAMES, table)  97.8 us
    ppermute x45, starting transfers between devices, send(): return lax.ppermute(value, NAMES, table)  52.6 us
    pallas_call x1, Pallas kernels, up(): pl.pallas_call(up_kernel, out_shape=[jax.ShapeDtypeStruct((2, 2, ROWS, TO...  15.4 us
    pallas_call x1, Pallas kernels, down(): pl.pallas_call(down_kernel, out_shape=[jax.ShapeDtypeStruct((4, 4, GROUP,...  9.93 us
  transfers between devices with their start and end apart: 45, of which 22 were waited for; matrix products, arithmetic and copies ran while one was open for 5% of the time, Pallas kernels for 0%

profile of v3, /device:TPU:38, one launch (start us, length us, event | category | flops | bytes accessed | tf_op | source)
XLA Modules:
  0.0 187.4 jit_solution(3285304609380409380)
XLA Ops:
  1.6 1.7 collective-permute-start.6
  4.0 0.9 collective-permute-start.16
  5.0 1.0 collective-permute-done.6
  6.0 3.1 %collective-permute-start.7 = (bf16[2,1,64,512]{3,2,0,1:T(8,128)(2,1)S(1)}, bf16[2,1,64,512]{3,2,0,1:T(8,128)(2,1)S(1)}, u32[]{:S(2)}, u32[]{:S(2)}) collective-permute-start(bf16[2,1,64,512]{3,2,0,1:T(8,128)(2,1)S(1)} %pad_maximum_fusion.9), channel_id=1, source_target_pairs={{0,48},{1,49},{2,50},{3,51},{4,52},{5,53},{6,54},{7,55},{8,24},{9,... | collective-permute-start | bytes 393224 | tf_op jit(solution)/shard_map/ppermute | solution.py:48
  9.7 2.6 %collective-permute-done.7 = bf16[2,1,64,512]{3,2,0,1:T(8,128)(2,1)S(1)} collective-permute-done((bf16[2,1,64,512]{3,2,0,1:T(8,128)(2,1)S(1)}, bf16[2,1,64,512]{3,2,0,1:T(8,128)(2,1)S(1)}, u32[]{:S(2)}, u32[]{:S(2)}) %collective-permute-start.7) | collective-permute-done | bytes 131104 | tf_op jit(solution)/shard_map/ppermute | solution.py:48
  12.5 1.9 %collective-permute-start = (bf16[1,64,384]{2,1,0:T(8,128)(2,1)S(1)}, bf16[1,64,384]{2,1,0:T(8,128)(2,1)S(1)}, u32[]{:S(2)}, u32[]{:S(2)}) collective-permute-start(bf16[1,64,384]{2,1,0:T(8,128)(2,1)S(1)} %get-tuple-element.52), channel_id=1, source_target_pairs={{0,1},{1,0},{2,3},{3,2},{4,5},{5,4},{6,7},{7,6},{8,73},{9,72},{10,... | collective-permute-start | bytes 147464 | tf_op jit(solution)/shard_map/ppermute | solution.py:48
  14.4 1.0 collective-permute-done.17
  15.6 3.6 %collective-permute-done = bf16[1,64,384]{2,1,0:T(8,128)(2,1)S(1)} collective-permute-done((bf16[1,64,384]{2,1,0:T(8,128)(2,1)S(1)}, bf16[1,64,384]{2,1,0:T(8,128)(2,1)S(1)}, u32[]{:S(2)}, u32[]{:S(2)}) %collective-permute-start) | collective-permute-done | bytes 49184 | tf_op jit(solution)/shard_map/ppermute | solution.py:48
  19.3 2.0 %collective-permute-start.1 = (bf16[2,1,64,384]{3,2,1,0:T(8,128)(2,1)S(1)}, bf16[2,1,64,384]{3,2,1,0:T(8,128)(2,1)S(1)}, u32[]{:S(2)}, u32[]{:S(2)}) collective-permute-start(bf16[2,1,64,384]{3,2,1,0:T(8,128)(2,1)S(1)} %pad_maximum_fusion.11), channel_id=1, source_target_pairs={{0,65},{1,64},{2,67},{3,66},{4,69},{5,68},{6,71},{7,70},{8,9},{9,8... | collective-permute-start | bytes 294920 | tf_op jit(solution)/shard_map/ppermute | solution.py:48
  21.9 2.8 %collective-permute-start.19 = (bf16[2,4,64,512]{3,2,1,0:T(8,128)(2,1)S(1)}, bf16[2,4,64,512]{3,2,1,0:T(8,128)(2,1)S(1)}, u32[]{:S(2)}, u32[]{:S(2)}) collective-permute-start(bf16[2,4,64,512]{3,2,1,0:T(8,128)(2,1)S(1)} %pad_maximum_fusion.4), channel_id=1, source_target_pairs={{0,48},{1,49},{2,50},{3,51},{4,52},{5,53},{6,54},{7,55},{8,24},{9,... | collective-permute-start | bytes 1572872 | tf_op jit(solution)/shard_map/ppermute | solution.py:48
  24.7 0.9 collective-permute-start.2
  25.6 4.8 %collective-permute-done.2 = bf16[4,64,384]{2,1,0:T(8,128)(2,1)S(1)} collective-permute-done((bf16[4,64,384]{2,1,0:T(8,128)(2,1)S(1)}, bf16[4,64,384]{2,1,0:T(8,128)(2,1)S(1)}, u32[]{:S(2)}, u32[]{:S(2)}) %collective-permute-start.2) | collective-permute-done | bytes 196640 | tf_op jit(solution)/shard_map/ppermute | solution.py:48
  31.9 1.0 collective-permute-start.10
  33.0 3.1 %collective-permute-start.20 = (bf16[16,64,512]{2,1,0:T(8,128)(2,1)S(1)}, bf16[16,64,512]{2,1,0:T(8,128)(2,1)}, u32[]{:S(2)}, u32[]{:S(2)}) collective-permute-start(bf16[16,64,512]{2,1,0:T(8,128)(2,1)S(1)} %bitcast.161), channel_id=1, source_target_pairs={{0,1},{1,0},{2,3},{3,2},{4,5},{5,4},{6,7},{7,6},{8,73},{9,72},{10,... | collective-permute-start | bytes 3145736 | tf_op jit(solution)/shard_map/ppermute | solution.py:48
  36.0 2.6 %collective-permute-start.11 = (bf16[16,64,512]{2,1,0:T(8,128)(2,1)S(1)}, bf16[16,64,512]{2,1,0:T(8,128)(2,1)}, u32[]{:S(2)}, u32[]{:S(2)}) collective-permute-start(bf16[16,64,512]{2,1,0:T(8,128)(2,1)S(1)} %bitcast.160), channel_id=1, source_target_pairs={{0,6},{1,7},{2,4},{3,5},{4,2},{5,3},{6,0},{7,1},{8,10},{9,11},{10,... | collective-permute-start | bytes 3145736 | tf_op jit(solution)/shard_map/ppermute | solution.py:48
  38.9 6.0 %collective-permute-done.3 = bf16[2,4,64,384]{3,2,1,0:T(8,128)(2,1)} collective-permute-done((bf16[2,4,64,384]{3,2,1,0:T(8,128)(2,1)}, bf16[2,4,64,384]{3,2,1,0:T(8,128)(2,1)}, u32[]{:S(2)}, u32[]{:S(2)}) %collective-permute-start.3) | collective-permute-done | bytes 393248 | tf_op jit(solution)/shard_map/ppermute | solution.py:48
  44.8 1.1 pad_maximum_fusion.2
  46.2 2.0 %collective-permute-start.21 = (bf16[16,64,512]{2,1,0:T(8,128)(2,1)S(1)}, bf16[16,64,512]{2,1,0:T(8,128)(2,1)}, u32[]{:S(2)}, u32[]{:S(2)}) collective-permute-start(bf16[16,64,512]{2,1,0:T(8,128)(2,1)S(1)} %bitcast.162), channel_id=1, source_target_pairs={{0,65},{1,64},{2,67},{3,66},{4,69},{5,68},{6,71},{7,70},{8,9},{9,8... | collective-permute-start | bytes 3145736 | tf_op jit(solution)/shard_map/ppermute | solution.py:48
  48.2 9.9 %collective-permute-done.10 = bf16[16,64,512]{2,1,0:T(8,128)(2,1)} collective-permute-done((bf16[16,64,512]{2,1,0:T(8,128)(2,1)S(1)}, bf16[16,64,512]{2,1,0:T(8,128)(2,1)}, u32[]{:S(2)}, u32[]{:S(2)}) %collective-permute-start.10) | collective-permute-done | bytes 1048608 | tf_op jit(solution)/shard_map/ppermute | solution.py:48
  58.2 2.8 %collective-permute-start.12 = (bf16[16,64,512]{2,1,0:T(8,128)(2,1)}, bf16[16,64,512]{2,1,0:T(8,128)(2,1)}, u32[]{:S(2)}, u32[]{:S(2)}) collective-permute-start(bf16[16,64,512]{2,1,0:T(8,128)(2,1)} %collective-permute-done.10), channel_id=1, source_target_pairs={{0,6},{1,7},{2,4},{3,5},{4,2},{5,3},{6,0},{7,1},{8,10},{9,11},{10,... | collective-permute-start | bytes 3145736 | tf_op jit(solution)/shard_map/ppermute | solution.py:48
  60.9 1.9 %collective-permute-start.22 = (bf16[16,64,512]{2,1,0:T(8,128)(2,1)}, bf16[16,64,512]{2,1,0:T(8,128)(2,1)}, u32[]{:S(2)}, u32[]{:S(2)}) collective-permute-start(bf16[16,64,512]{2,1,0:T(8,128)(2,1)} %collective-permute-done.20), channel_id=1, source_target_pairs={{0,65},{1,64},{2,67},{3,66},{4,69},{5,68},{6,71},{7,70},{8,9},{9,8... | collective-permute-start | bytes 3145736 | tf_op jit(solution)/shard_map/ppermute | solution.py:48
  62.8 2.3 %collective-permute-start.14 = (bf16[16,64,384]{2,1,0:T(8,128)(2,1)S(1)}, bf16[16,64,384]{2,1,0:T(8,128)(2,1)S(1)}, u32[]{:S(2)}, u32[]{:S(2)}) collective-permute-start(bf16[16,64,384]{2,1,0:T(8,128)(2,1)S(1)} %bitcast.164), channel_id=1, source_target_pairs={{0,48},{1,49},{2,50},{3,51},{4,52},{5,53},{6,54},{7,55},{8,24},{9,... | collective-permute-start | bytes 2359304 | tf_op jit(solution)/shard_map/ppermute | solution.py:48
  65.2 0.9 collective-permute-start.15
  66.7 7.8 %collective-permute-done.12 = bf16[16,64,512]{2,1,0:T(8,128)(2,1)} collective-permute-done((bf16[16,64,512]{2,1,0:T(8,128)(2,1)}, bf16[16,64,512]{2,1,0:T(8,128)(2,1)}, u32[]{:S(2)}, u32[]{:S(2)}) %collective-permute-start.12) | collective-permute-done | bytes 1048608 | tf_op jit(solution)/shard_map/ppermute | solution.py:48
  74.5 1.6 collective-permute-done.22
  76.0 8.5 %collective-permute-done.15 = bf16[16,64,384]{2,1,0:T(8,128)(2,1)} collective-permute-done((bf16[16,64,384]{2,1,0:T(8,128)(2,1)}, bf16[16,64,384]{2,1,0:T(8,128)(2,1)}, u32[]{:S(2)}, u32[]{:S(2)}) %collective-permute-start.15) | collective-permute-done | bytes 786464 | tf_op jit(solution)/shard_map/ppermute | solution.py:48
  84.6 15.4 %up.1 = (bf16[2,2,208,512]{3,2,1,0:T(8,128)(2,1)}, bf16[64,1024]{1,0:T(8,128)(2,1)}) custom-call(s32[4]{0:T(128)} %pad_add_fusion.place, bf16[3,208,16384]{2,1,0:T(8,128)(2,1)} %w.3, bf16[3,208,16384]{2,1,0:T(8,128)(2,1)} %collective-permute-done.4.wo, bf16[3,208,64]{2,1,0:T(8,128)(2,1)} %copy-done.3, bf16[3,208,64]{2,1,0:T(8,128)(2,1)} %copy-done.11, ...), custom_call_target="tpu_custom_call" | custom-call | tf_op jit(solution)/shard_map/up/pallas_call | solution.py:187
  100.1 2.6 %collective-permute-done.23.other = bf16[2,2,208,512]{3,2,1,0:T(8,128)(2,1)S(1)} collective-permute-done((bf16[2,2,208,512]{3,2,1,0:T(8,128)(2,1)}, bf16[2,2,208,512]{3,2,1,0:T(8,128)(2,1)S(1)}, u32[]{:S(2)}, u32[]{:S(2)}) %collective-permute-start.23) | collective-permute-done | bytes 852000 | tf_op jit(solution)/shard_map/ppermute | solution.py:48
  102.7 1.0 copy-done.4
  103.6 9.9 %down.1 = (bf16[4,4,64,384]{3,2,1,0:T(8,128)(2,1)}, bf16[4,4,64,384]{3,2,1,0:T(8,128)(2,1)}, bf16[4,4,64,384]{3,2,1,0:T(8,128)(2,1)}, bf16[4,4,64,384]{3,2,1,0:T...) custom-call(s32[4]{0:T(128)} %pad_add_fusion.place, ...), custom_call_target="tpu_custom_call" | custom-call | tf_op jit(solution)/shard_map/down/pallas_call | solution.py:266
  114.2 2.3 %collective-permute-start.32 = (bf16[16,64,384]{2,1,0:T(8,128)(2,1)}, bf16[16,64,384]{2,1,0:T(8,128)(2,1)S(1)}, u32[]{:S(2)}, u32[]{:S(2)}) collective-permute-start(bf16[16,64,384]{2,1,0:T(8,128)(2,1)} %bitcast.188), channel_id=1, source_target_pairs={{0,48},{1,49},{2,50},{3,51},{4,52},{5,53},{6,54},{7,55},{8,24},{9,... | collective-permute-start | bytes 2359304 | tf_op jit(solution)/shard_map/ppermute | solution.py:48
  116.7 2.8 %collective-permute-start.24 = (bf16[16,64,384]{2,1,0:T(8,128)(2,1)}, bf16[16,64,384]{2,1,0:T(8,128)(2,1)S(1)}, u32[]{:S(2)}, u32[]{:S(2)}) collective-permute-start(bf16[16,64,384]{2,1,0:T(8,128)(2,1)} %bitcast.186), channel_id=1, source_target_pairs={{0,6},{1,7},{2,4},{3,5},{4,2},{5,3},{6,0},{7,1},{8,10},{9,11},{10,... | collective-permute-start | bytes 2359304 | tf_op jit(solution)/shard_map/ppermute | solution.py:48
  119.4 7.7 %collective-permute-done.25 = bf16[16,64,384]{2,1,0:T(8,128)(2,1)S(1)} collective-permute-done((bf16[16,64,384]{2,1,0:T(8,128)(2,1)}, bf16[16,64,384]{2,1,0:T(8,128)(2,1)S(1)}, u32[]{:S(2)}, u32[]{:S(2)}) %collective-permute-start.25) | collective-permute-done | bytes 786464 | tf_op jit(solution)/shard_map/ppermute | solution.py:48
  127.1 1.2 bitcast_add_fusion.2
  128.4 2.4 %collective-permute-start.31 = (bf16[16,64,384]{2,1,0:T(8,128)(2,1)S(1)}, bf16[16,64,384]{2,1,0:T(8,128)(2,1)S(1)}, u32[]{:S(2)}, u32[]{:S(2)}) collective-permute-start(bf16[16,64,384]{2,1,0:T(8,128)(2,1)S(1)} %bitcast.185), channel_id=1, source_target_pairs={{0,48},{1,49},{2,50},{3,51},{4,52},{5,53},{6,54},{7,55},{8,24},{9,... | collective-permute-start | bytes 2359304 | tf_op jit(solution)/shard_map/ppermute | solution.py:48
  131.5 9.2 %collective-permute-done.24 = bf16[16,64,384]{2,1,0:T(8,128)(2,1)S(1)} collective-permute-done((bf16[16,64,384]{2,1,0:T(8,128)(2,1)}, bf16[16,64,384]{2,1,0:T(8,128)(2,1)S(1)}, u32[]{:S(2)}, u32[]{:S(2)}) %collective-permute-start.24) | collective-permute-done | bytes 786464 | tf_op jit(solution)/shard_map/ppermute | solution.py:48
  140.7 3.9 %collective-permute-start.40 = (bf16[16,64,384]{2,1,0:T(8,128)(2,1)S(1)}, bf16[16,64,384]{2,1,0:T(8,128)(2,1)S(1)}, u32[]{:S(2)}, u32[]{:S(2)}) collective-permute-start(bf16[16,64,384]{2,1,0:T(8,128)(2,1)S(1)} %bitcast_add_fusion), channel_id=1, source_target_pairs={{0,1},{1,0},{2,3},{3,2},{4,5},{5,4},{6,7},{7,6},{8,73},{9,72},{10,... | collective-permute-start | bytes 2359304 | tf_op jit(solution)/shard_map/ppermute | solution.py:48
  145.2 3.9 %collective-permute-done.31 = bf16[16,64,384]{2,1,0:T(8,128)(2,1)S(1)} collective-permute-done((bf16[16,64,384]{2,1,0:T(8,128)(2,1)S(1)}, bf16[16,64,384]{2,1,0:T(8,128)(2,1)S(1)}, u32[]{:S(2)}, u32[]{:S(2)}) %collective-permute-start.31) | collective-permute-done | bytes 786464 | tf_op jit(solution)/shard_map/ppermute | solution.py:48
  149.7 9.0 %collective-permute-done.40 = bf16[16,64,384]{2,1,0:T(8,128)(2,1)S(1)} collective-permute-done((bf16[16,64,384]{2,1,0:T(8,128)(2,1)S(1)}, bf16[16,64,384]{2,1,0:T(8,128)(2,1)S(1)}, u32[]{:S(2)}, u32[]{:S(2)}) %collective-permute-start.40) | collective-permute-done | bytes 786464 | tf_op jit(solution)/shard_map/ppermute | solution.py:48
  159.3 2.1 %collective-permute-start.41 = (bf16[2,4,64,384]{3,2,1,0:T(8,128)(2,1)S(1)}, bf16[2,4,64,384]{3,2,1,0:T(8,128)(2,1)S(1)}, u32[]{:S(2)}, u32[]{:S(2)}) collective-permute-start(bf16[2,4,64,384]{3,2,1,0:T(8,128)(2,1)S(1)} %bitcast.177), channel_id=1, source_target_pairs={{0,48},{1,49},{2,50},{3,51},{4,52},{5,53},{6,54},{7,55},{8,24},{9,... | collective-permute-start | bytes 1179656 | tf_op jit(solution)/shard_map/ppermute | solution.py:48
  161.5 2.1 %collective-permute-start.28 = (bf16[4,64,384]{2,1,0:T(8,128)(2,1)S(1)}, bf16[4,64,384]{2,1,0:T(8,128)(2,1)S(1)}, u32[]{:S(2)}, u32[]{:S(2)}) collective-permute-start(bf16[4,64,384]{2,1,0:T(8,128)(2,1)S(1)} %slice_bitcast_fusion.4), channel_id=1, source_target_pairs={{0,1},{1,0},{2,3},{3,2},{4,5},{5,4},{6,7},{7,6},{8,73},{9,72},{10,... | collective-permute-start | bytes 589832 | tf_op jit(solution)/shard_map/ppermute | solution.py:48
  163.8 6.6 %collective-permute-done.41 = bf16[2,4,64,384]{3,2,1,0:T(8,128)(2,1)S(1)} collective-permute-done((bf16[2,4,64,384]{3,2,1,0:T(8,128)(2,1)S(1)}, bf16[2,4,64,384]{3,2,1,0:T(8,128)(2,1)S(1)}, u32[]{:S(2)}, u32[]{:S(2)}) %collective-permute-start.41) | collective-permute-done | bytes 393248 | tf_op jit(solution)/shard_map/ppermute | solution.py:48
  170.7 1.8 collective-permute-start.29
  172.7 3.6 %collective-permute-done.42 = bf16[4,64,384]{2,1,0:T(8,128)(2,1)S(1)} collective-permute-done((bf16[4,64,384]{2,1,0:T(8,128)(2,1)S(1)}, bf16[4,64,384]{2,1,0:T(8,128)(2,1)S(1)}, u32[]{:S(2)}, u32[]{:S(2)}) %collective-permute-start.42) | collective-permute-done | bytes 196640 | tf_op jit(solution)/shard_map/ppermute | solution.py:48
  176.7 0.9 collective-permute-start.30
  177.6 1.2 collective-permute-start.37
  178.8 3.5 %collective-permute-done.43 = bf16[2,1,64,384]{3,2,1,0:T(8,128)(2,1)S(1)} collective-permute-done((bf16[2,1,64,384]{3,2,1,0:T(8,128)(2,1)S(1)}, bf16[2,1,64,384]{3,2,1,0:T(8,128)(2,1)S(1)}, u32[]{:S(2)}, u32[]{:S(2)}) %collective-permute-start.43) | collective-permute-done | bytes 98336 | tf_op jit(solution)/shard_map/ppermute | solution.py:48
  182.4 4.0 %collective-permute-done.44 = bf16[1,64,384]{2,1,0:T(8,128)(2,1)S(1)} collective-permute-done((bf16[1,64,384]{2,1,0:T(8,128)(2,1)S(1)}, bf16[1,64,384]{2,1,0:T(8,128)(2,1)S(1)}, u32[]{:S(2)}, u32[]{:S(2)}) %collective-permute-start.44) | collective-permute-done | bytes 49184 | tf_op jit(solution)/shard_map/ppermute | solution.py:48
  (127 shorter events, 12.1 us)
Async XLA Ops:
  0.0 46.2 %collective-permute-start.4 = (bf16[3,208,16384]{2,1,0:T(8,128)(2,1)}, bf16[3,208,16384]{2,1,0:T(8,128)(2,1)}, u32[]{:S(2)}, u32[]{:S(2)}) collective-permute-start(bf16[3,208,16384]{2,1,0:T(8,128)(2,1)} %w.3), channel_id=1, source_target_pairs={{0,8},{1,9},{2,10},{3,11},{4,12},{5,13},{6,14},{7,15},{8,0},{9,1},... | collective-permute-start | bytes 61341704 | tf_op jit(solution)/shard_map/ppermute | solution.py:48
  1.6 4.3 %collective-permute-start.6 = (bf16[1,64,512]{2,1,0:T(8,128)(2,1)S(1)}, bf16[1,64,512]{2,1,0:T(8,128)(2,1)S(1)}, u32[]{:S(2)}, u32[]{:S(2)}) collective-permute-start(bf16[1,64,512]{2,1,0:T(8,128)(2,1)S(1)} %get-tuple-element.57), channel_id=1, source_target_pairs={{0,16},{1,17},{2,18},{3,19},{4,20},{5,21},{6,22},{7,23},{8,56},{9,... | collective-permute-start | bytes 196616 | tf_op jit(solution)/shard_map/ppermute | solution.py:48
  4.0 5.0 %collective-permute-start.16 = (bf16[1,64,512]{2,1,0:T(8,128)(2,1)S(1)}, bf16[1,64,512]{2,1,0:T(8,128)(2,1)S(1)}, u32[]{:S(2)}, u32[]{:S(2)}) collective-permute-start(bf16[1,64,512]{2,1,0:T(8,128)(2,1)S(1)} %get-tuple-element.55), channel_id=1, source_target_pairs={{0,2},{1,3},{2,0},{3,1},{4,6},{5,7},{6,4},{7,5},{8,14},{9,15},{10,... | collective-permute-start | bytes 196616 | tf_op jit(solution)/shard_map/ppermute | solution.py:48
  6.0 6.3 %collective-permute-start.7 = (bf16[2,1,64,512]{3,2,0,1:T(8,128)(2,1)S(1)}, bf16[2,1,64,512]{3,2,0,1:T(8,128)(2,1)S(1)}, u32[]{:S(2)}, u32[]{:S(2)}) collective-permute-start(bf16[2,1,64,512]{3,2,0,1:T(8,128)(2,1)S(1)} %pad_maximum_fusion.9), channel_id=1, source_target_pairs={{0,48},{1,49},{2,50},{3,51},{4,52},{5,53},{6,54},{7,55},{8,24},{9,... | collective-permute-start | bytes 393224 | tf_op jit(solution)/shard_map/ppermute | solution.py:48
  9.1 6.3 %collective-permute-start.17 = (bf16[2,1,64,512]{3,2,0,1:T(8,128)(2,1)S(1)}, bf16[2,1,64,512]{3,2,0,1:T(8,128)(2,1)S(1)}, u32[]{:S(2)}, u32[]{:S(2)}) collective-permute-start(bf16[2,1,64,512]{3,2,0,1:T(8,128)(2,1)S(1)} %pad_maximum_fusion.10), channel_id=1, source_target_pairs={{0,6},{1,7},{2,4},{3,5},{4,2},{5,3},{6,0},{7,1},{8,10},{9,11},{10,... | collective-permute-start | bytes 393224 | tf_op jit(solution)/shard_map/ppermute | solution.py:48
  12.3 9.0 %collective-permute-start.8 = (bf16[4,64,512]{2,1,0:T(8,128)(2,1)S(1)}, bf16[4,64,512]{2,1,0:T(8,128)(2,1)S(1)}, u32[]{:S(2)}, u32[]{:S(2)}) collective-permute-start(bf16[4,64,512]{2,1,0:T(8,128)(2,1)S(1)} %get-tuple-element.48), channel_id=1, source_target_pairs={{0,1},{1,0},{2,3},{3,2},{4,5},{5,4},{6,7},{7,6},{8,73},{9,72},{10,... | collective-permute-start | bytes 786440 | tf_op jit(solution)/shard_map/ppermute | solution.py:48
  12.5 6.8 %collective-permute-start = (bf16[1,64,384]{2,1,0:T(8,128)(2,1)S(1)}, bf16[1,64,384]{2,1,0:T(8,128)(2,1)S(1)}, u32[]{:S(2)}, u32[]{:S(2)}) collective-permute-start(bf16[1,64,384]{2,1,0:T(8,128)(2,1)S(1)} %get-tuple-element.52), channel_id=1, source_target_pairs={{0,1},{1,0},{2,3},{3,2},{4,5},{5,4},{6,7},{7,6},{8,73},{9,72},{10,... | collective-permute-start | bytes 147464 | tf_op jit(solution)/shard_map/ppermute | solution.py:48
  15.4 6.5 %collective-permute-start.18 = (bf16[4,64,512]{2,1,0:T(8,128)(2,1)S(1)}, bf16[4,64,512]{2,1,0:T(8,128)(2,1)S(1)}, u32[]{:S(2)}, u32[]{:S(2)}) collective-permute-start(bf16[4,64,512]{2,1,0:T(8,128)(2,1)S(1)} %get-tuple-element.46), channel_id=1, source_target_pairs={{0,16},{1,17},{2,18},{3,19},{4,20},{5,21},{6,22},{7,23},{8,56},{9,... | collective-permute-start | bytes 786440 | tf_op jit(solution)/shard_map/ppermute | solution.py:48
  19.3 5.4 %collective-permute-start.1 = (bf16[2,1,64,384]{3,2,1,0:T(8,128)(2,1)S(1)}, bf16[2,1,64,384]{3,2,1,0:T(8,128)(2,1)S(1)}, u32[]{:S(2)}, u32[]{:S(2)}) collective-permute-start(bf16[2,1,64,384]{3,2,1,0:T(8,128)(2,1)S(1)} %pad_maximum_fusion.11), channel_id=1, source_target_pairs={{0,65},{1,64},{2,67},{3,66},{4,69},{5,68},{6,71},{7,70},{8,9},{9,8... | collective-permute-start | bytes 294920 | tf_op jit(solution)/shard_map/ppermute | solution.py:48
  21.3 10.4 %collective-permute-start.9 = (bf16[2,4,64,512]{3,2,1,0:T(8,128)(2,1)S(1)}, bf16[2,4,64,512]{3,2,1,0:T(8,128)(2,1)S(1)}, u32[]{:S(2)}, u32[]{:S(2)}) collective-permute-start(bf16[2,4,64,512]{3,2,1,0:T(8,128)(2,1)S(1)} %pad_maximum_fusion.3), channel_id=1, source_target_pairs={{0,65},{1,64},{2,67},{3,66},{4,69},{5,68},{6,71},{7,70},{8,9},{9,8... | collective-permute-start | bytes 1572872 | tf_op jit(solution)/shard_map/ppermute | solution.py:48
  21.9 10.9 %collective-permute-start.19 = (bf16[2,4,64,512]{3,2,1,0:T(8,128)(2,1)S(1)}, bf16[2,4,64,512]{3,2,1,0:T(8,128)(2,1)S(1)}, u32[]{:S(2)}, u32[]{:S(2)}) collective-permute-start(bf16[2,4,64,512]{3,2,1,0:T(8,128)(2,1)S(1)} %pad_maximum_fusion.4), channel_id=1, source_target_pairs={{0,48},{1,49},{2,50},{3,51},{4,52},{5,53},{6,54},{7,55},{8,24},{9,... | collective-permute-start | bytes 1572872 | tf_op jit(solution)/shard_map/ppermute | solution.py:48
  24.7 5.7 %collective-permute-start.2 = (bf16[4,64,384]{2,1,0:T(8,128)(2,1)S(1)}, bf16[4,64,384]{2,1,0:T(8,128)(2,1)S(1)}, u32[]{:S(2)}, u32[]{:S(2)}) collective-permute-start(bf16[4,64,384]{2,1,0:T(8,128)(2,1)S(1)} %get-tuple-element.50), channel_id=1, source_target_pairs={{0,2},{1,3},{2,0},{3,1},{4,6},{5,7},{6,4},{7,5},{8,14},{9,15},{10,... | collective-permute-start | bytes 589832 | tf_op jit(solution)/shard_map/ppermute | solution.py:48
  31.3 13.6 %collective-permute-start.3 = (bf16[2,4,64,384]{3,2,1,0:T(8,128)(2,1)}, bf16[2,4,64,384]{3,2,1,0:T(8,128)(2,1)}, u32[]{:S(2)}, u32[]{:S(2)}) collective-permute-start(bf16[2,4,64,384]{3,2,1,0:T(8,128)(2,1)} %pad_maximum_fusion.5), channel_id=1, source_target_pairs={{0,6},{1,7},{2,4},{3,5},{4,2},{5,3},{6,0},{7,1},{8,10},{9,11},{10,... | collective-permute-start | bytes 1179656 | tf_op jit(solution)/shard_map/ppermute | solution.py:48
  31.9 26.3 %collective-permute-start.10 = (bf16[16,64,512]{2,1,0:T(8,128)(2,1)S(1)}, bf16[16,64,512]{2,1,0:T(8,128)(2,1)}, u32[]{:S(2)}, u32[]{:S(2)}) collective-permute-start(bf16[16,64,512]{2,1,0:T(8,128)(2,1)S(1)} %bitcast.159), channel_id=1, source_target_pairs={{0,2},{1,3},{2,0},{3,1},{4,6},{5,7},{6,4},{7,5},{8,14},{9,15},{10,... | collective-permute-start | bytes 3145736 | tf_op jit(solution)/shard_map/ppermute | solution.py:48
  33.0 51.6 %copy-start.1 = (bf16[4,4,64,512]{3,2,1,0:T(8,128)(2,1)}, bf16[4,4,64,512]{3,2,1,0:T(8,128)(2,1)S(1)}, u32[]{:S(2)}) copy-start(bf16[4,4,64,512]{3,2,1,0:T(8,128)(2,1)S(1)} %pad_maximum_fusion.1.refs_8_) | copy-start | bytes 3145732
  33.0 28.0 %collective-permute-start.20 = (bf16[16,64,512]{2,1,0:T(8,128)(2,1)S(1)}, bf16[16,64,512]{2,1,0:T(8,128)(2,1)}, u32[]{:S(2)}, u32[]{:S(2)}) collective-permute-start(bf16[16,64,512]{2,1,0:T(8,128)(2,1)S(1)} %bitcast.161), channel_id=1, source_target_pairs={{0,1},{1,0},{2,3},{3,2},{4,5},{5,4},{6,7},{7,6},{8,73},{9,72},{10,... | collective-permute-start | bytes 3145736 | tf_op jit(solution)/shard_map/ppermute | solution.py:48
  36.0 26.8 %collective-permute-start.11 = (bf16[16,64,512]{2,1,0:T(8,128)(2,1)S(1)}, bf16[16,64,512]{2,1,0:T(8,128)(2,1)}, u32[]{:S(2)}, u32[]{:S(2)}) collective-permute-start(bf16[16,64,512]{2,1,0:T(8,128)(2,1)S(1)} %bitcast.160), channel_id=1, source_target_pairs={{0,6},{1,7},{2,4},{3,5},{4,2},{5,3},{6,0},{7,1},{8,10},{9,11},{10,... | collective-permute-start | bytes 3145736 | tf_op jit(solution)/shard_map/ppermute | solution.py:48
  38.8 45.7 %copy-start.3 = (bf16[3,208,64]{2,1,0:T(8,128)(2,1)}, bf16[3,208,64]{2,1,0:T(8,128)(2,1)S(1)}, u32[]{:S(2)}) copy-start(bf16[3,208,64]{2,1,0:T(8,128)(2,1)S(1)} %copy.5.a_mine) | copy-start | bytes 239620
  44.8 1.4 collective-permute-start.5
  46.0 38.6 %copy-start.2 = (bf16[4,4,64,384]{3,2,1,0:T(8,128)(2,1)}, bf16[4,4,64,384]{3,2,1,0:T(8,128)(2,1)S(1)}, u32[]{:S(2)}) copy-start(bf16[4,4,64,384]{3,2,1,0:T(8,128)(2,1)S(1)} %pad_maximum_fusion.2) | copy-start | bytes 2359300
  46.2 18.9 %collective-permute-start.13 = (bf16[16,64,384]{2,1,0:T(8,128)(2,1)S(1)}, bf16[16,64,384]{2,1,0:T(8,128)(2,1)}, u32[]{:S(2)}, u32[]{:S(2)}) collective-permute-start(bf16[16,64,384]{2,1,0:T(8,128)(2,1)S(1)} %bitcast.163), channel_id=1, source_target_pairs={{0,16},{1,17},{2,18},{3,19},{4,20},{5,21},{6,22},{7,23},{8,56},{9,... | collective-permute-start | bytes 2359304 | tf_op jit(solution)/shard_map/ppermute | solution.py:48
  46.2 20.5 %collective-permute-start.21 = (bf16[16,64,512]{2,1,0:T(8,128)(2,1)S(1)}, bf16[16,64,512]{2,1,0:T(8,128)(2,1)}, u32[]{:S(2)}, u32[]{:S(2)}) collective-permute-start(bf16[16,64,512]{2,1,0:T(8,128)(2,1)S(1)} %bitcast.162), channel_id=1, source_target_pairs={{0,65},{1,64},{2,67},{3,66},{4,69},{5,68},{6,71},{7,70},{8,9},{9,8... | collective-permute-start | bytes 3145736 | tf_op jit(solution)/shard_map/ppermute | solution.py:48
  58.2 16.3 %collective-permute-start.12 = (bf16[16,64,512]{2,1,0:T(8,128)(2,1)}, bf16[16,64,512]{2,1,0:T(8,128)(2,1)}, u32[]{:S(2)}, u32[]{:S(2)}) collective-permute-start(bf16[16,64,512]{2,1,0:T(8,128)(2,1)} %collective-permute-done.10), channel_id=1, source_target_pairs={{0,6},{1,7},{2,4},{3,5},{4,2},{5,3},{6,0},{7,1},{8,10},{9,11},{10,... | collective-permute-start | bytes 3145736 | tf_op jit(solution)/shard_map/ppermute | solution.py:48
  60.9 15.1 %collective-permute-start.22 = (bf16[16,64,512]{2,1,0:T(8,128)(2,1)}, bf16[16,64,512]{2,1,0:T(8,128)(2,1)}, u32[]{:S(2)}, u32[]{:S(2)}) collective-permute-start(bf16[16,64,512]{2,1,0:T(8,128)(2,1)} %collective-permute-done.20), channel_id=1, source_target_pairs={{0,65},{1,64},{2,67},{3,66},{4,69},{5,68},{6,71},{7,70},{8,9},{9,8... | collective-permute-start | bytes 3145736 | tf_op jit(solution)/shard_map/ppermute | solution.py:48
  62.8 13.2 %collective-permute-start.14 = (bf16[16,64,384]{2,1,0:T(8,128)(2,1)S(1)}, bf16[16,64,384]{2,1,0:T(8,128)(2,1)S(1)}, u32[]{:S(2)}, u32[]{:S(2)}) collective-permute-start(bf16[16,64,384]{2,1,0:T(8,128)(2,1)S(1)} %bitcast.164), channel_id=1, source_target_pairs={{0,48},{1,49},{2,50},{3,51},{4,52},{5,53},{6,54},{7,55},{8,24},{9,... | collective-permute-start | bytes 2359304 | tf_op jit(solution)/shard_map/ppermute | solution.py:48
  65.2 19.4 %collective-permute-start.15 = (bf16[16,64,384]{2,1,0:T(8,128)(2,1)}, bf16[16,64,384]{2,1,0:T(8,128)(2,1)}, u32[]{:S(2)}, u32[]{:S(2)}) collective-permute-start(bf16[16,64,384]{2,1,0:T(8,128)(2,1)} %collective-permute-done.13), channel_id=1, source_target_pairs={{0,48},{1,49},{2,50},{3,51},{4,52},{5,53},{6,54},{7,55},{8,24},{9,... | collective-permute-start | bytes 2359304 | tf_op jit(solution)/shard_map/ppermute | solution.py:48
  100.0 2.7 %collective-permute-start.23 = (bf16[2,2,208,512]{3,2,1,0:T(8,128)(2,1)}, bf16[2,2,208,512]{3,2,1,0:T(8,128)(2,1)S(1)}, u32[]{:S(2)}, u32[]{:S(2)}) collective-permute-start(bf16[2,2,208,512]{3,2,1,0:T(8,128)(2,1)} %get-tuple-element.25.mine), channel_id=1, source_target_pairs={{0,8},{1,9},{2,10},{3,11},{4,12},{5,13},{6,14},{7,15},{8,0},{9,1},... | collective-permute-start | bytes 2555912 | tf_op jit(solution)/shard_map/ppermute | solution.py:48
  113.6 13.5 %collective-permute-start.25 = (bf16[16,64,384]{2,1,0:T(8,128)(2,1)}, bf16[16,64,384]{2,1,0:T(8,128)(2,1)S(1)}, u32[]{:S(2)}, u32[]{:S(2)}) collective-permute-start(bf16[16,64,384]{2,1,0:T(8,128)(2,1)} %bitcast.189), channel_id=1, source_target_pairs={{0,6},{1,7},{2,4},{3,5},{4,2},{5,3},{6,0},{7,1},{8,10},{9,11},{10,... | collective-permute-start | bytes 2359304 | tf_op jit(solution)/shard_map/ppermute | solution.py:48
  114.2 16.7 %collective-permute-start.32 = (bf16[16,64,384]{2,1,0:T(8,128)(2,1)}, bf16[16,64,384]{2,1,0:T(8,128)(2,1)S(1)}, u32[]{:S(2)}, u32[]{:S(2)}) collective-permute-start(bf16[16,64,384]{2,1,0:T(8,128)(2,1)} %bitcast.188), channel_id=1, source_target_pairs={{0,48},{1,49},{2,50},{3,51},{4,52},{5,53},{6,54},{7,55},{8,24},{9,... | collective-permute-start | bytes 2359304 | tf_op jit(solution)/shard_map/ppermute | solution.py:48
  116.5 14.7 %collective-permute-start.39 = (bf16[16,64,384]{2,1,0:T(8,128)(2,1)}, bf16[16,64,384]{2,1,0:T(8,128)(2,1)S(1)}, u32[]{:S(2)}, u32[]{:S(2)}) collective-permute-start(bf16[16,64,384]{2,1,0:T(8,128)(2,1)} %bitcast.187), channel_id=1, source_target_pairs={{0,65},{1,64},{2,67},{3,66},{4,69},{5,68},{6,71},{7,70},{8,9},{9,8... | collective-permute-start | bytes 2359304 | tf_op jit(solution)/shard_map/ppermute | solution.py:48
  116.7 24.0 %collective-permute-start.24 = (bf16[16,64,384]{2,1,0:T(8,128)(2,1)}, bf16[16,64,384]{2,1,0:T(8,128)(2,1)S(1)}, u32[]{:S(2)}, u32[]{:S(2)}) collective-permute-start(bf16[16,64,384]{2,1,0:T(8,128)(2,1)} %bitcast.186), channel_id=1, source_target_pairs={{0,6},{1,7},{2,4},{3,5},{4,2},{5,3},{6,0},{7,1},{8,10},{9,11},{10,... | collective-permute-start | bytes 2359304 | tf_op jit(solution)/shard_map/ppermute | solution.py:48
  128.3 16.2 %collective-permute-start.26 = (bf16[16,64,384]{2,1,0:T(8,128)(2,1)S(1)}, bf16[16,64,384]{2,1,0:T(8,128)(2,1)S(1)}, u32[]{:S(2)}, u32[]{:S(2)}) collective-permute-start(bf16[16,64,384]{2,1,0:T(8,128)(2,1)S(1)} %bitcast_add_fusion.2), channel_id=1, source_target_pairs={{0,2},{1,3},{2,0},{3,1},{4,6},{5,7},{6,4},{7,5},{8,14},{9,15},{10,... | collective-permute-start | bytes 2359304 | tf_op jit(solution)/shard_map/ppermute | solution.py:48
  128.4 20.6 %collective-permute-start.31 = (bf16[16,64,384]{2,1,0:T(8,128)(2,1)S(1)}, bf16[16,64,384]{2,1,0:T(8,128)(2,1)S(1)}, u32[]{:S(2)}, u32[]{:S(2)}) collective-permute-start(bf16[16,64,384]{2,1,0:T(8,128)(2,1)S(1)} %bitcast.185), channel_id=1, source_target_pairs={{0,48},{1,49},{2,50},{3,51},{4,52},{5,53},{6,54},{7,55},{8,24},{9,... | collective-permute-start | bytes 2359304 | tf_op jit(solution)/shard_map/ppermute | solution.py:48
  130.8 18.9 %collective-permute-start.38 = (bf16[16,64,384]{2,1,0:T(8,128)(2,1)S(1)}, bf16[16,64,384]{2,1,0:T(8,128)(2,1)S(1)}, u32[]{:S(2)}, u32[]{:S(2)}) collective-permute-start(bf16[16,64,384]{2,1,0:T(8,128)(2,1)S(1)} %bitcast.184), channel_id=1, source_target_pairs={{0,65},{1,64},{2,67},{3,66},{4,69},{5,68},{6,71},{7,70},{8,9},{9,8... | collective-permute-start | bytes 2359304 | tf_op jit(solution)/shard_map/ppermute | solution.py:48
  131.2 17.9 %collective-permute-start.33 = (bf16[16,64,384]{2,1,0:T(8,128)(2,1)S(1)}, bf16[16,64,384]{2,1,0:T(8,128)(2,1)S(1)}, u32[]{:S(2)}, u32[]{:S(2)}) collective-permute-start(bf16[16,64,384]{2,1,0:T(8,128)(2,1)S(1)} %bitcast_add_fusion.1), channel_id=1, source_target_pairs={{0,16},{1,17},{2,18},{3,19},{4,20},{5,21},{6,22},{7,23},{8,56},{9,... | collective-permute-start | bytes 2359304 | tf_op jit(solution)/shard_map/ppermute | solution.py:48
  140.7 18.0 %collective-permute-start.40 = (bf16[16,64,384]{2,1,0:T(8,128)(2,1)S(1)}, bf16[16,64,384]{2,1,0:T(8,128)(2,1)S(1)}, u32[]{:S(2)}, u32[]{:S(2)}) collective-permute-start(bf16[16,64,384]{2,1,0:T(8,128)(2,1)S(1)} %bitcast_add_fusion), channel_id=1, source_target_pairs={{0,1},{1,0},{2,3},{3,2},{4,5},{5,4},{6,7},{7,6},{8,73},{9,72},{10,... | collective-permute-start | bytes 2359304 | tf_op jit(solution)/shard_map/ppermute | solution.py:48
  145.1 16.2 %collective-permute-start.27 = (bf16[2,4,64,384]{3,2,1,0:T(8,128)(2,1)S(1)}, bf16[2,4,64,384]{3,2,1,0:T(8,128)(2,1)S(1)}, u32[]{:S(2)}, u32[]{:S(2)}) collective-permute-start(bf16[2,4,64,384]{3,2,1,0:T(8,128)(2,1)S(1)} %bitcast.175), channel_id=1, source_target_pairs={{0,65},{1,64},{2,67},{3,66},{4,69},{5,68},{6,71},{7,70},{8,9},{9,8... | collective-permute-start | bytes 1179656 | tf_op jit(solution)/shard_map/ppermute | solution.py:48
  149.6 13.9 %collective-permute-start.34 = (bf16[2,4,64,384]{3,2,1,0:T(8,128)(2,1)S(1)}, bf16[2,4,64,384]{3,2,1,0:T(8,128)(2,1)S(1)}, u32[]{:S(2)}, u32[]{:S(2)}) collective-permute-start(bf16[2,4,64,384]{3,2,1,0:T(8,128)(2,1)S(1)} %bitcast.176), channel_id=1, source_target_pairs={{0,6},{1,7},{2,4},{3,5},{4,2},{5,3},{6,0},{7,1},{8,10},{9,11},{10,... | collective-permute-start | bytes 1179656 | tf_op jit(solution)/shard_map/ppermute | solution.py:48
  159.3 11.2 %collective-permute-start.41 = (bf16[2,4,64,384]{3,2,1,0:T(8,128)(2,1)S(1)}, bf16[2,4,64,384]{3,2,1,0:T(8,128)(2,1)S(1)}, u32[]{:S(2)}, u32[]{:S(2)}) collective-permute-start(bf16[2,4,64,384]{3,2,1,0:T(8,128)(2,1)S(1)} %bitcast.177), channel_id=1, source_target_pairs={{0,48},{1,49},{2,50},{3,51},{4,52},{5,53},{6,54},{7,55},{8,24},{9,... | collective-permute-start | bytes 1179656 | tf_op jit(solution)/shard_map/ppermute | solution.py:48
  161.5 9.2 %collective-permute-start.28 = (bf16[4,64,384]{2,1,0:T(8,128)(2,1)S(1)}, bf16[4,64,384]{2,1,0:T(8,128)(2,1)S(1)}, u32[]{:S(2)}, u32[]{:S(2)}) collective-permute-start(bf16[4,64,384]{2,1,0:T(8,128)(2,1)S(1)} %slice_bitcast_fusion.4), channel_id=1, source_target_pairs={{0,1},{1,0},{2,3},{3,2},{4,5},{5,4},{6,7},{7,6},{8,73},{9,72},{10,... | collective-permute-start | bytes 589832 | tf_op jit(solution)/shard_map/ppermute | solution.py:48
  163.7 8.9 %collective-permute-start.35 = (bf16[4,64,384]{2,1,0:T(8,128)(2,1)S(1)}, bf16[4,64,384]{2,1,0:T(8,128)(2,1)S(1)}, u32[]{:S(2)}, u32[]{:S(2)}) collective-permute-start(bf16[4,64,384]{2,1,0:T(8,128)(2,1)S(1)} %slice_bitcast_fusion.2), channel_id=1, source_target_pairs={{0,2},{1,3},{2,0},{3,1},{4,6},{5,7},{6,4},{7,5},{8,14},{9,15},{10,... | collective-permute-start | bytes 589832 | tf_op jit(solution)/shard_map/ppermute | solution.py:48
  170.6 5.7 %collective-permute-start.42 = (bf16[4,64,384]{2,1,0:T(8,128)(2,1)S(1)}, bf16[4,64,384]{2,1,0:T(8,128)(2,1)S(1)}, u32[]{:S(2)}, u32[]{:S(2)}) collective-permute-start(bf16[4,64,384]{2,1,0:T(8,128)(2,1)S(1)} %slice_bitcast_fusion), channel_id=1, source_target_pairs={{0,16},{1,17},{2,18},{3,19},{4,20},{5,21},{6,22},{7,23},{8,56},{9,... | collective-permute-start | bytes 589832 | tf_op jit(solution)/shard_map/ppermute | solution.py:48
  170.7 5.9 %collective-permute-start.29 = (bf16[2,1,64,384]{3,2,1,0:T(8,128)(2,1)S(1)}, bf16[2,1,64,384]{3,2,1,0:T(8,128)(2,1)S(1)}, u32[]{:S(2)}, u32[]{:S(2)}) collective-permute-start(bf16[2,1,64,384]{3,2,1,0:T(8,128)(2,1)S(1)} %slice_bitcast_fusion.10), channel_id=1, source_target_pairs={{0,48},{1,49},{2,50},{3,51},{4,52},{5,53},{6,54},{7,55},{8,24},{9,... | collective-permute-start | bytes 294920 | tf_op jit(solution)/shard_map/ppermute | solution.py:48
  172.6 4.9 %collective-permute-start.36 = (bf16[2,1,64,384]{3,2,1,0:T(8,128)(2,1)S(1)}, bf16[2,1,64,384]{3,2,1,0:T(8,128)(2,1)S(1)}, u32[]{:S(2)}, u32[]{:S(2)}) collective-permute-start(bf16[2,1,64,384]{3,2,1,0:T(8,128)(2,1)S(1)} %slice_bitcast_fusion.8), channel_id=1, source_target_pairs={{0,65},{1,64},{2,67},{3,66},{4,69},{5,68},{6,71},{7,70},{8,9},{9,8... | collective-permute-start | bytes 294920 | tf_op jit(solution)/shard_map/ppermute | solution.py:48
  176.4 5.9 %collective-permute-start.43 = (bf16[2,1,64,384]{3,2,1,0:T(8,128)(2,1)S(1)}, bf16[2,1,64,384]{3,2,1,0:T(8,128)(2,1)S(1)}, u32[]{:S(2)}, u32[]{:S(2)}) collective-permute-start(bf16[2,1,64,384]{3,2,1,0:T(8,128)(2,1)S(1)} %slice_bitcast_fusion.6), channel_id=1, source_target_pairs={{0,6},{1,7},{2,4},{3,5},{4,2},{5,3},{6,0},{7,1},{8,10},{9,11},{10,... | collective-permute-start | bytes 294920 | tf_op jit(solution)/shard_map/ppermute | solution.py:48
  176.7 5.7 %collective-permute-start.30 = (bf16[1,64,384]{2,1,0:T(8,128)(2,1)S(1)}, bf16[1,64,384]{2,1,0:T(8,128)(2,1)S(1)}, u32[]{:S(2)}, u32[]{:S(2)}) collective-permute-start(bf16[1,64,384]{2,1,0:T(8,128)(2,1)S(1)} %slice_bitcast_fusion.16), channel_id=1, source_target_pairs={{0,16},{1,17},{2,18},{3,19},{4,20},{5,21},{6,22},{7,23},{8,56},{9,... | collective-permute-start | bytes 147464 | tf_op jit(solution)/shard_map/ppermute | solution.py:48
  177.6 8.9 %collective-permute-start.37 = (bf16[1,64,384]{2,1,0:T(8,128)(2,1)S(1)}, bf16[1,64,384]{2,1,0:T(8,128)(2,1)S(1)}, u32[]{:S(2)}, u32[]{:S(2)}) collective-permute-start(bf16[1,64,384]{2,1,0:T(8,128)(2,1)S(1)} %slice_bitcast_fusion.14), channel_id=1, source_target_pairs={{0,1},{1,0},{2,3},{3,2},{4,5},{5,4},{6,7},{7,6},{8,73},{9,72},{10,... | collective-permute-start | bytes 147464 | tf_op jit(solution)/shard_map/ppermute | solution.py:48
  182.3 4.2 %collective-permute-start.44 = (bf16[1,64,384]{2,1,0:T(8,128)(2,1)S(1)}, bf16[1,64,384]{2,1,0:T(8,128)(2,1)S(1)}, u32[]{:S(2)}, u32[]{:S(2)}) collective-permute-start(bf16[1,64,384]{2,1,0:T(8,128)(2,1)S(1)} %slice_bitcast_fusion.12), channel_id=1, source_target_pairs={{0,2},{1,3},{2,0},{3,1},{4,6},{5,7},{6,4},{7,5},{8,14},{9,15},{10,... | collective-permute-start | bytes 147464 | tf_op jit(solution)/shard_map/ppermute | solution.py:48
  (13 other events, 144.3 us)

commit v4 on v3

--- a/solution.py
+++ b/solution.py
@@ -59,10 +59,12 @@
         ]
         if stage == 1:
             values[1], late = lax.optimization_barrier((values[1], late))
-    out = []
-    for v, order in zip(values, ORDERS):
-        near = send(v, FIRST[order[2]])
-        out += [v, near, send(v, SECOND[order[2]]), send(near, SECOND[order[2]])]
+    axes = [order[2] for order in ORDERS]
+    turns = (2, 0, 1)
+    near = {p: send(values[p], FIRST[axes[p]]) for p in turns}
+    second = {p: send(values[p], SECOND[axes[p]]) for p in turns}
+    across = {p: send(near[p], SECOND[axes[p]]) for p in turns}
+    out = [b for p in range(3) for b in (values[p], near[p], second[p], across[p])]
     return out, late
 
 

time: 188 us -> 188 us (level)
  no operation moved by 1% of the time
where the time goes in v4:
time: 188 us; the launch traced here: 187 us
  waiting for transfers between devices  97.8 us (52%)
  starting transfers between devices  52.6 us (28%)
  Pallas kernels  25.3 us (13%)
  other arithmetic  6.35 us (3%)
  local copies, waits for them, and re-layouts  3.92 us (2%)
    ppermute x45, waiting for transfers between devices, send(): return lax.ppermute(value, NAMES, table)  97.8 us
    ppermute x45, starting transfers between devices, send(): return lax.ppermute(value, NAMES, table)  52.6 us
    pallas_call x1, Pallas kernels, up(): pl.pallas_call(up_kernel, out_shape=[jax.ShapeDtypeStruct((2, 2, ROWS, TO...  15.4 us
    pallas_call x1, Pallas kernels, down(): pl.pallas_call(down_kernel, out_shape=[jax.ShapeDtypeStruct((4, 4, GROUP,...  9.93 us
  transfers between devices with their start and end apart: 45, of which 22 were waited for; matrix products, arithmetic and copies ran while one was open for 5% of the time, Pallas kernels for 0%

profile of v4, /device:TPU:38, one launch (start us, length us, event | category | flops | bytes accessed | tf_op | source)
XLA Modules:
  0.0 187.4 jit_solution(3285304609380409380)
XLA Ops:
  1.6 1.7 collective-permute-start.6
  4.0 0.9 collective-permute-start.16
  5.0 1.0 collective-permute-done.6
  6.0 3.1 %collective-permute-start.7 = (bf16[2,1,64,512]{3,2,0,1:T(8,128)(2,1)S(1)}, bf16[2,1,64,512]{3,2,0,1:T(8,128)(2,1)S(1)}, u32[]{:S(2)}, u32[]{:S(2)}) collective-permute-start(bf16[2,1,64,512]{3,2,0,1:T(8,128)(2,1)S(1)} %pad_maximum_fusion.9), channel_id=1, source_target_pairs={{0,48},{1,49},{2,50},{3,51},{4,52},{5,53},{6,54},{7,55},{8,24},{9,... | collective-permute-start | bytes 393224 | tf_op jit(solution)/shard_map/ppermute | solution.py:48
  9.7 2.6 %collective-permute-done.7 = bf16[2,1,64,512]{3,2,0,1:T(8,128)(2,1)S(1)} collective-permute-done((bf16[2,1,64,512]{3,2,0,1:T(8,128)(2,1)S(1)}, bf16[2,1,64,512]{3,2,0,1:T(8,128)(2,1)S(1)}, u32[]{:S(2)}, u32[]{:S(2)}) %collective-permute-start.7) | collective-permute-done | bytes 131104 | tf_op jit(solution)/shard_map/ppermute | solution.py:48
  12.5 1.9 %collective-permute-start = (bf16[1,64,384]{2,1,0:T(8,128)(2,1)S(1)}, bf16[1,64,384]{2,1,0:T(8,128)(2,1)S(1)}, u32[]{:S(2)}, u32[]{:S(2)}) collective-permute-start(bf16[1,64,384]{2,1,0:T(8,128)(2,1)S(1)} %get-tuple-element.52), channel_id=1, source_target_pairs={{0,1},{1,0},{2,3},{3,2},{4,5},{5,4},{6,7},{7,6},{8,73},{9,72},{10,... | collective-permute-start | bytes 147464 | tf_op jit(solution)/shard_map/ppermute | solution.py:48
  14.4 1.0 collective-permute-done.17
  15.6 3.6 %collective-permute-done = bf16[1,64,384]{2,1,0:T(8,128)(2,1)S(1)} collective-permute-done((bf16[1,64,384]{2,1,0:T(8,128)(2,1)S(1)}, bf16[1,64,384]{2,1,0:T(8,128)(2,1)S(1)}, u32[]{:S(2)}, u32[]{:S(2)}) %collective-permute-start) | collective-permute-done | bytes 49184 | tf_op jit(solution)/shard_map/ppermute | solution.py:48
  19.3 2.0 %collective-permute-start.1 = (bf16[2,1,64,384]{3,2,1,0:T(8,128)(2,1)S(1)}, bf16[2,1,64,384]{3,2,1,0:T(8,128)(2,1)S(1)}, u32[]{:S(2)}, u32[]{:S(2)}) collective-permute-start(bf16[2,1,64,384]{3,2,1,0:T(8,128)(2,1)S(1)} %pad_maximum_fusion.11), channel_id=1, source_target_pairs={{0,65},{1,64},{2,67},{3,66},{4,69},{5,68},{6,71},{7,70},{8,9},{9,8... | collective-permute-start | bytes 294920 | tf_op jit(solution)/shard_map/ppermute | solution.py:48
  21.9 2.8 %collective-permute-start.19 = (bf16[2,4,64,512]{3,2,1,0:T(8,128)(2,1)S(1)}, bf16[2,4,64,512]{3,2,1,0:T(8,128)(2,1)S(1)}, u32[]{:S(2)}, u32[]{:S(2)}) collective-permute-start(bf16[2,4,64,512]{3,2,1,0:T(8,128)(2,1)S(1)} %pad_maximum_fusion.4), channel_id=1, source_target_pairs={{0,48},{1,49},{2,50},{3,51},{4,52},{5,53},{6,54},{7,55},{8,24},{9,... | collective-permute-start | bytes 1572872 | tf_op jit(solution)/shard_map/ppermute | solution.py:48
  24.7 0.9 collective-permute-start.2
  25.6 4.8 %collective-permute-done.2 = bf16[4,64,384]{2,1,0:T(8,128)(2,1)S(1)} collective-permute-done((bf16[4,64,384]{2,1,0:T(8,128)(2,1)S(1)}, bf16[4,64,384]{2,1,0:T(8,128)(2,1)S(1)}, u32[]{:S(2)}, u32[]{:S(2)}) %collective-permute-start.2) | collective-permute-done | bytes 196640 | tf_op jit(solution)/shard_map/ppermute | solution.py:48
  31.9 1.0 collective-permute-start.10
  33.0 3.1 %collective-permute-start.20 = (bf16[16,64,512]{2,1,0:T(8,128)(2,1)S(1)}, bf16[16,64,512]{2,1,0:T(8,128)(2,1)}, u32[]{:S(2)}, u32[]{:S(2)}) collective-permute-start(bf16[16,64,512]{2,1,0:T(8,128)(2,1)S(1)} %bitcast.161), channel_id=1, source_target_pairs={{0,1},{1,0},{2,3},{3,2},{4,5},{5,4},{6,7},{7,6},{8,73},{9,72},{10,... | collective-permute-start | bytes 3145736 | tf_op jit(solution)/shard_map/ppermute | solution.py:48
  36.0 2.6 %collective-permute-start.11 = (bf16[16,64,512]{2,1,0:T(8,128)(2,1)S(1)}, bf16[16,64,512]{2,1,0:T(8,128)(2,1)}, u32[]{:S(2)}, u32[]{:S(2)}) collective-permute-start(bf16[16,64,512]{2,1,0:T(8,128)(2,1)S(1)} %bitcast.160), channel_id=1, source_target_pairs={{0,6},{1,7},{2,4},{3,5},{4,2},{5,3},{6,0},{7,1},{8,10},{9,11},{10,... | collective-permute-start | bytes 3145736 | tf_op jit(solution)/shard_map/ppermute | solution.py:48
  38.9 6.0 %collective-permute-done.3 = bf16[2,4,64,384]{3,2,1,0:T(8,128)(2,1)} collective-permute-done((bf16[2,4,64,384]{3,2,1,0:T(8,128)(2,1)}, bf16[2,4,64,384]{3,2,1,0:T(8,128)(2,1)}, u32[]{:S(2)}, u32[]{:S(2)}) %collective-permute-start.3) | collective-permute-done | bytes 393248 | tf_op jit(solution)/shard_map/ppermute | solution.py:48
  44.8 1.1 pad_maximum_fusion.2
  46.2 2.0 %collective-permute-start.21 = (bf16[16,64,512]{2,1,0:T(8,128)(2,1)S(1)}, bf16[16,64,512]{2,1,0:T(8,128)(2,1)}, u32[]{:S(2)}, u32[]{:S(2)}) collective-permute-start(bf16[16,64,512]{2,1,0:T(8,128)(2,1)S(1)} %bitcast.162), channel_id=1, source_target_pairs={{0,65},{1,64},{2,67},{3,66},{4,69},{5,68},{6,71},{7,70},{8,9},{9,8... | collective-permute-start | bytes 3145736 | tf_op jit(solution)/shard_map/ppermute | solution.py:48
  48.2 9.9 %collective-permute-done.10 = bf16[16,64,512]{2,1,0:T(8,128)(2,1)} collective-permute-done((bf16[16,64,512]{2,1,0:T(8,128)(2,1)S(1)}, bf16[16,64,512]{2,1,0:T(8,128)(2,1)}, u32[]{:S(2)}, u32[]{:S(2)}) %collective-permute-start.10) | collective-permute-done | bytes 1048608 | tf_op jit(solution)/shard_map/ppermute | solution.py:48
  58.2 2.8 %collective-permute-start.12 = (bf16[16,64,512]{2,1,0:T(8,128)(2,1)}, bf16[16,64,512]{2,1,0:T(8,128)(2,1)}, u32[]{:S(2)}, u32[]{:S(2)}) collective-permute-start(bf16[16,64,512]{2,1,0:T(8,128)(2,1)} %collective-permute-done.10), channel_id=1, source_target_pairs={{0,6},{1,7},{2,4},{3,5},{4,2},{5,3},{6,0},{7,1},{8,10},{9,11},{10,... | collective-permute-start | bytes 3145736 | tf_op jit(solution)/shard_map/ppermute | solution.py:48
  60.9 1.9 %collective-permute-start.22 = (bf16[16,64,512]{2,1,0:T(8,128)(2,1)}, bf16[16,64,512]{2,1,0:T(8,128)(2,1)}, u32[]{:S(2)}, u32[]{:S(2)}) collective-permute-start(bf16[16,64,512]{2,1,0:T(8,128)(2,1)} %collective-permute-done.20), channel_id=1, source_target_pairs={{0,65},{1,64},{2,67},{3,66},{4,69},{5,68},{6,71},{7,70},{8,9},{9,8... | collective-permute-start | bytes 3145736 | tf_op jit(solution)/shard_map/ppermute | solution.py:48
  62.8 2.3 %collective-permute-start.14 = (bf16[16,64,384]{2,1,0:T(8,128)(2,1)S(1)}, bf16[16,64,384]{2,1,0:T(8,128)(2,1)S(1)}, u32[]{:S(2)}, u32[]{:S(2)}) collective-permute-start(bf16[16,64,384]{2,1,0:T(8,128)(2,1)S(1)} %bitcast.164), channel_id=1, source_target_pairs={{0,48},{1,49},{2,50},{3,51},{4,52},{5,53},{6,54},{7,55},{8,24},{9,... | collective-permute-start | bytes 2359304 | tf_op jit(solution)/shard_map/ppermute | solution.py:48
  65.2 0.9 collective-permute-start.15
  66.7 7.8 %collective-permute-done.12 = bf16[16,64,512]{2,1,0:T(8,128)(2,1)} collective-permute-done((bf16[16,64,512]{2,1,0:T(8,128)(2,1)}, bf16[16,64,512]{2,1,0:T(8,128)(2,1)}, u32[]{:S(2)}, u32[]{:S(2)}) %collective-permute-start.12) | collective-permute-done | bytes 1048608 | tf_op jit(solution)/shard_map/ppermute | solution.py:48
  74.5 1.6 collective-permute-done.22
  76.0 8.5 %collective-permute-done.15 = bf16[16,64,384]{2,1,0:T(8,128)(2,1)} collective-permute-done((bf16[16,64,384]{2,1,0:T(8,128)(2,1)}, bf16[16,64,384]{2,1,0:T(8,128)(2,1)}, u32[]{:S(2)}, u32[]{:S(2)}) %collective-permute-start.15) | collective-permute-done | bytes 786464 | tf_op jit(solution)/shard_map/ppermute | solution.py:48
  84.6 15.4 %up.1 = (bf16[2,2,208,512]{3,2,1,0:T(8,128)(2,1)}, bf16[64,1024]{1,0:T(8,128)(2,1)}) custom-call(s32[4]{0:T(128)} %pad_add_fusion.place, bf16[3,208,16384]{2,1,0:T(8,128)(2,1)} %w.3, bf16[3,208,16384]{2,1,0:T(8,128)(2,1)} %collective-permute-done.4.wo, bf16[3,208,64]{2,1,0:T(8,128)(2,1)} %copy-done.3, bf16[3,208,64]{2,1,0:T(8,128)(2,1)} %copy-done.11, ...), custom_call_target="tpu_custom_call" | custom-call | tf_op jit(solution)/shard_map/up/pallas_call | solution.py:189
  100.1 2.6 %collective-permute-done.23.other = bf16[2,2,208,512]{3,2,1,0:T(8,128)(2,1)S(1)} collective-permute-done((bf16[2,2,208,512]{3,2,1,0:T(8,128)(2,1)}, bf16[2,2,208,512]{3,2,1,0:T(8,128)(2,1)S(1)}, u32[]{:S(2)}, u32[]{:S(2)}) %collective-permute-start.23) | collective-permute-done | bytes 852000 | tf_op jit(solution)/shard_map/ppermute | solution.py:48
  102.7 1.0 copy-done.4
  103.6 9.9 %down.1 = (bf16[4,4,64,384]{3,2,1,0:T(8,128)(2,1)}, bf16[4,4,64,384]{3,2,1,0:T(8,128)(2,1)}, bf16[4,4,64,384]{3,2,1,0:T(8,128)(2,1)}, bf16[4,4,64,384]{3,2,1,0:T...) custom-call(s32[4]{0:T(128)} %pad_add_fusion.place, ...), custom_call_target="tpu_custom_call" | custom-call | tf_op jit(solution)/shard_map/down/pallas_call | solution.py:268
  114.2 2.3 %collective-permute-start.32 = (bf16[16,64,384]{2,1,0:T(8,128)(2,1)}, bf16[16,64,384]{2,1,0:T(8,128)(2,1)S(1)}, u32[]{:S(2)}, u32[]{:S(2)}) collective-permute-start(bf16[16,64,384]{2,1,0:T(8,128)(2,1)} %bitcast.188), channel_id=1, source_target_pairs={{0,48},{1,49},{2,50},{3,51},{4,52},{5,53},{6,54},{7,55},{8,24},{9,... | collective-permute-start | bytes 2359304 | tf_op jit(solution)/shard_map/ppermute | solution.py:48
  116.7 2.8 %collective-permute-start.24 = (bf16[16,64,384]{2,1,0:T(8,128)(2,1)}, bf16[16,64,384]{2,1,0:T(8,128)(2,1)S(1)}, u32[]{:S(2)}, u32[]{:S(2)}) collective-permute-start(bf16[16,64,384]{2,1,0:T(8,128)(2,1)} %bitcast.186), channel_id=1, source_target_pairs={{0,6},{1,7},{2,4},{3,5},{4,2},{5,3},{6,0},{7,1},{8,10},{9,11},{10,... | collective-permute-start | bytes 2359304 | tf_op jit(solution)/shard_map/ppermute | solution.py:48
  119.4 7.7 %collective-permute-done.25 = bf16[16,64,384]{2,1,0:T(8,128)(2,1)S(1)} collective-permute-done((bf16[16,64,384]{2,1,0:T(8,128)(2,1)}, bf16[16,64,384]{2,1,0:T(8,128)(2,1)S(1)}, u32[]{:S(2)}, u32[]{:S(2)}) %collective-permute-start.25) | collective-permute-done | bytes 786464 | tf_op jit(solution)/shard_map/ppermute | solution.py:48
  127.1 1.2 bitcast_add_fusion.2
  128.4 2.4 %collective-permute-start.31 = (bf16[16,64,384]{2,1,0:T(8,128)(2,1)S(1)}, bf16[16,64,384]{2,1,0:T(8,128)(2,1)S(1)}, u32[]{:S(2)}, u32[]{:S(2)}) collective-permute-start(bf16[16,64,384]{2,1,0:T(8,128)(2,1)S(1)} %bitcast.185), channel_id=1, source_target_pairs={{0,48},{1,49},{2,50},{3,51},{4,52},{5,53},{6,54},{7,55},{8,24},{9,... | collective-permute-start | bytes 2359304 | tf_op jit(solution)/shard_map/ppermute | solution.py:48
  131.5 9.2 %collective-permute-done.24 = bf16[16,64,384]{2,1,0:T(8,128)(2,1)S(1)} collective-permute-done((bf16[16,64,384]{2,1,0:T(8,128)(2,1)}, bf16[16,64,384]{2,1,0:T(8,128)(2,1)S(1)}, u32[]{:S(2)}, u32[]{:S(2)}) %collective-permute-start.24) | collective-permute-done | bytes 786464 | tf_op jit(solution)/shard_map/ppermute | solution.py:48
  140.7 3.9 %collective-permute-start.40 = (bf16[16,64,384]{2,1,0:T(8,128)(2,1)S(1)}, bf16[16,64,384]{2,1,0:T(8,128)(2,1)S(1)}, u32[]{:S(2)}, u32[]{:S(2)}) collective-permute-start(bf16[16,64,384]{2,1,0:T(8,128)(2,1)S(1)} %bitcast_add_fusion), channel_id=1, source_target_pairs={{0,1},{1,0},{2,3},{3,2},{4,5},{5,4},{6,7},{7,6},{8,73},{9,72},{10,... | collective-permute-start | bytes 2359304 | tf_op jit(solution)/shard_map/ppermute | solution.py:48
  145.2 3.9 %collective-permute-done.31 = bf16[16,64,384]{2,1,0:T(8,128)(2,1)S(1)} collective-permute-done((bf16[16,64,384]{2,1,0:T(8,128)(2,1)S(1)}, bf16[16,64,384]{2,1,0:T(8,128)(2,1)S(1)}, u32[]{:S(2)}, u32[]{:S(2)}) %collective-permute-start.31) | collective-permute-done | bytes 786464 | tf_op jit(solution)/shard_map/ppermute | solution.py:48
  149.7 9.0 %collective-permute-done.40 = bf16[16,64,384]{2,1,0:T(8,128)(2,1)S(1)} collective-permute-done((bf16[16,64,384]{2,1,0:T(8,128)(2,1)S(1)}, bf16[16,64,384]{2,1,0:T(8,128)(2,1)S(1)}, u32[]{:S(2)}, u32[]{:S(2)}) %collective-permute-start.40) | collective-permute-done | bytes 786464 | tf_op jit(solution)/shard_map/ppermute | solution.py:48
  159.3 2.1 %collective-permute-start.41 = (bf16[2,4,64,384]{3,2,1,0:T(8,128)(2,1)S(1)}, bf16[2,4,64,384]{3,2,1,0:T(8,128)(2,1)S(1)}, u32[]{:S(2)}, u32[]{:S(2)}) collective-permute-start(bf16[2,4,64,384]{3,2,1,0:T(8,128)(2,1)S(1)} %bitcast.177), channel_id=1, source_target_pairs={{0,48},{1,49},{2,50},{3,51},{4,52},{5,53},{6,54},{7,55},{8,24},{9,... | collective-permute-start | bytes 1179656 | tf_op jit(solution)/shard_map/ppermute | solution.py:48
  161.5 2.1 %collective-permute-start.28 = (bf16[4,64,384]{2,1,0:T(8,128)(2,1)S(1)}, bf16[4,64,384]{2,1,0:T(8,128)(2,1)S(1)}, u32[]{:S(2)}, u32[]{:S(2)}) collective-permute-start(bf16[4,64,384]{2,1,0:T(8,128)(2,1)S(1)} %slice_bitcast_fusion.4), channel_id=1, source_target_pairs={{0,1},{1,0},{2,3},{3,2},{4,5},{5,4},{6,7},{7,6},{8,73},{9,72},{10,... | collective-permute-start | bytes 589832 | tf_op jit(solution)/shard_map/ppermute | solution.py:48
  163.8 6.6 %collective-permute-done.41 = bf16[2,4,64,384]{3,2,1,0:T(8,128)(2,1)S(1)} collective-permute-done((bf16[2,4,64,384]{3,2,1,0:T(8,128)(2,1)S(1)}, bf16[2,4,64,384]{3,2,1,0:T(8,128)(2,1)S(1)}, u32[]{:S(2)}, u32[]{:S(2)}) %collective-permute-start.41) | collective-permute-done | bytes 393248 | tf_op jit(solution)/shard_map/ppermute | solution.py:48
  170.7 1.8 collective-permute-start.29
  172.7 3.6 %collective-permute-done.42 = bf16[4,64,384]{2,1,0:T(8,128)(2,1)S(1)} collective-permute-done((bf16[4,64,384]{2,1,0:T(8,128)(2,1)S(1)}, bf16[4,64,384]{2,1,0:T(8,128)(2,1)S(1)}, u32[]{:S(2)}, u32[]{:S(2)}) %collective-permute-start.42) | collective-permute-done | bytes 196640 | tf_op jit(solution)/shard_map/ppermute | solution.py:48
  176.7 0.9 collective-permute-start.30
  177.6 1.2 collective-permute-start.37
  178.8 3.5 %collective-permute-done.43 = bf16[2,1,64,384]{3,2,1,0:T(8,128)(2,1)S(1)} collective-permute-done((bf16[2,1,64,384]{3,2,1,0:T(8,128)(2,1)S(1)}, bf16[2,1,64,384]{3,2,1,0:T(8,128)(2,1)S(1)}, u32[]{:S(2)}, u32[]{:S(2)}) %collective-permute-start.43) | collective-permute-done | bytes 98336 | tf_op jit(solution)/shard_map/ppermute | solution.py:48
  182.4 4.0 %collective-permute-done.44 = bf16[1,64,384]{2,1,0:T(8,128)(2,1)S(1)} collective-permute-done((bf16[1,64,384]{2,1,0:T(8,128)(2,1)S(1)}, bf16[1,64,384]{2,1,0:T(8,128)(2,1)S(1)}, u32[]{:S(2)}, u32[]{:S(2)}) %collective-permute-start.44) | collective-permute-done | bytes 49184 | tf_op jit(solution)/shard_map/ppermute | solution.py:48
  (127 shorter events, 12.1 us)
Async XLA Ops:
  0.0 46.2 %collective-permute-start.4 = (bf16[3,208,16384]{2,1,0:T(8,128)(2,1)}, bf16[3,208,16384]{2,1,0:T(8,128)(2,1)}, u32[]{:S(2)}, u32[]{:S(2)}) collective-permute-start(bf16[3,208,16384]{2,1,0:T(8,128)(2,1)} %w.3), channel_id=1, source_target_pairs={{0,8},{1,9},{2,10},{3,11},{4,12},{5,13},{6,14},{7,15},{8,0},{9,1},... | collective-permute-start | bytes 61341704 | tf_op jit(solution)/shard_map/ppermute | solution.py:48
  1.6 4.3 %collective-permute-start.6 = (bf16[1,64,512]{2,1,0:T(8,128)(2,1)S(1)}, bf16[1,64,512]{2,1,0:T(8,128)(2,1)S(1)}, u32[]{:S(2)}, u32[]{:S(2)}) collective-permute-start(bf16[1,64,512]{2,1,0:T(8,128)(2,1)S(1)} %get-tuple-element.57), channel_id=1, source_target_pairs={{0,16},{1,17},{2,18},{3,19},{4,20},{5,21},{6,22},{7,23},{8,56},{9,... | collective-permute-start | bytes 196616 | tf_op jit(solution)/shard_map/ppermute | solution.py:48
  4.0 5.0 %collective-permute-start.16 = (bf16[1,64,512]{2,1,0:T(8,128)(2,1)S(1)}, bf16[1,64,512]{2,1,0:T(8,128)(2,1)S(1)}, u32[]{:S(2)}, u32[]{:S(2)}) collective-permute-start(bf16[1,64,512]{2,1,0:T(8,128)(2,1)S(1)} %get-tuple-element.55), channel_id=1, source_target_pairs={{0,2},{1,3},{2,0},{3,1},{4,6},{5,7},{6,4},{7,5},{8,14},{9,15},{10,... | collective-permute-start | bytes 196616 | tf_op jit(solution)/shard_map/ppermute | solution.py:48
  6.0 6.3 %collective-permute-start.7 = (bf16[2,1,64,512]{3,2,0,1:T(8,128)(2,1)S(1)}, bf16[2,1,64,512]{3,2,0,1:T(8,128)(2,1)S(1)}, u32[]{:S(2)}, u32[]{:S(2)}) collective-permute-start(bf16[2,1,64,512]{3,2,0,1:T(8,128)(2,1)S(1)} %pad_maximum_fusion.9), channel_id=1, source_target_pairs={{0,48},{1,49},{2,50},{3,51},{4,52},{5,53},{6,54},{7,55},{8,24},{9,... | collective-permute-start | bytes 393224 | tf_op jit(solution)/shard_map/ppermute | solution.py:48
  9.1 6.3 %collective-permute-start.17 = (bf16[2,1,64,512]{3,2,0,1:T(8,128)(2,1)S(1)}, bf16[2,1,64,512]{3,2,0,1:T(8,128)(2,1)S(1)}, u32[]{:S(2)}, u32[]{:S(2)}) collective-permute-start(bf16[2,1,64,512]{3,2,0,1:T(8,128)(2,1)S(1)} %pad_maximum_fusion.10), channel_id=1, source_target_pairs={{0,6},{1,7},{2,4},{3,5},{4,2},{5,3},{6,0},{7,1},{8,10},{9,11},{10,... | collective-permute-start | bytes 393224 | tf_op jit(solution)/shard_map/ppermute | solution.py:48
  12.3 9.0 %collective-permute-start.8 = (bf16[4,64,512]{2,1,0:T(8,128)(2,1)S(1)}, bf16[4,64,512]{2,1,0:T(8,128)(2,1)S(1)}, u32[]{:S(2)}, u32[]{:S(2)}) collective-permute-start(bf16[4,64,512]{2,1,0:T(8,128)(2,1)S(1)} %get-tuple-element.48), channel_id=1, source_target_pairs={{0,1},{1,0},{2,3},{3,2},{4,5},{5,4},{6,7},{7,6},{8,73},{9,72},{10,... | collective-permute-start | bytes 786440 | tf_op jit(solution)/shard_map/ppermute | solution.py:48
  12.5 6.8 %collective-permute-start = (bf16[1,64,384]{2,1,0:T(8,128)(2,1)S(1)}, bf16[1,64,384]{2,1,0:T(8,128)(2,1)S(1)}, u32[]{:S(2)}, u32[]{:S(2)}) collective-permute-start(bf16[1,64,384]{2,1,0:T(8,128)(2,1)S(1)} %get-tuple-element.52), channel_id=1, source_target_pairs={{0,1},{1,0},{2,3},{3,2},{4,5},{5,4},{6,7},{7,6},{8,73},{9,72},{10,... | collective-permute-start | bytes 147464 | tf_op jit(solution)/shard_map/ppermute | solution.py:48
  15.4 6.5 %collective-permute-start.18 = (bf16[4,64,512]{2,1,0:T(8,128)(2,1)S(1)}, bf16[4,64,512]{2,1,0:T(8,128)(2,1)S(1)}, u32[]{:S(2)}, u32[]{:S(2)}) collective-permute-start(bf16[4,64,512]{2,1,0:T(8,128)(2,1)S(1)} %get-tuple-element.46), channel_id=1, source_target_pairs={{0,16},{1,17},{2,18},{3,19},{4,20},{5,21},{6,22},{7,23},{8,56},{9,... | collective-permute-start | bytes 786440 | tf_op jit(solution)/shard_map/ppermute | solution.py:48
  19.3 5.4 %collective-permute-start.1 = (bf16[2,1,64,384]{3,2,1,0:T(8,128)(2,1)S(1)}, bf16[2,1,64,384]{3,2,1,0:T(8,128)(2,1)S(1)}, u32[]{:S(2)}, u32[]{:S(2)}) collective-permute-start(bf16[2,1,64,384]{3,2,1,0:T(8,128)(2,1)S(1)} %pad_maximum_fusion.11), channel_id=1, source_target_pairs={{0,65},{1,64},{2,67},{3,66},{4,69},{5,68},{6,71},{7,70},{8,9},{9,8... | collective-permute-start | bytes 294920 | tf_op jit(solution)/shard_map/ppermute | solution.py:48
  21.3 10.4 %collective-permute-start.9 = (bf16[2,4,64,512]{3,2,1,0:T(8,128)(2,1)S(1)}, bf16[2,4,64,512]{3,2,1,0:T(8,128)(2,1)S(1)}, u32[]{:S(2)}, u32[]{:S(2)}) collective-permute-start(bf16[2,4,64,512]{3,2,1,0:T(8,128)(2,1)S(1)} %pad_maximum_fusion.3), channel_id=1, source_target_pairs={{0,65},{1,64},{2,67},{3,66},{4,69},{5,68},{6,71},{7,70},{8,9},{9,8... | collective-permute-start | bytes 1572872 | tf_op jit(solution)/shard_map/ppermute | solution.py:48
  21.9 10.9 %collective-permute-start.19 = (bf16[2,4,64,512]{3,2,1,0:T(8,128)(2,1)S(1)}, bf16[2,4,64,512]{3,2,1,0:T(8,128)(2,1)S(1)}, u32[]{:S(2)}, u32[]{:S(2)}) collective-permute-start(bf16[2,4,64,512]{3,2,1,0:T(8,128)(2,1)S(1)} %pad_maximum_fusion.4), channel_id=1, source_target_pairs={{0,48},{1,49},{2,50},{3,51},{4,52},{5,53},{6,54},{7,55},{8,24},{9,... | collective-permute-start | bytes 1572872 | tf_op jit(solution)/shard_map/ppermute | solution.py:48
  24.7 5.7 %collective-permute-start.2 = (bf16[4,64,384]{2,1,0:T(8,128)(2,1)S(1)}, bf16[4,64,384]{2,1,0:T(8,128)(2,1)S(1)}, u32[]{:S(2)}, u32[]{:S(2)}) collective-permute-start(bf16[4,64,384]{2,1,0:T(8,128)(2,1)S(1)} %get-tuple-element.50), channel_id=1, source_target_pairs={{0,2},{1,3},{2,0},{3,1},{4,6},{5,7},{6,4},{7,5},{8,14},{9,15},{10,... | collective-permute-start | bytes 589832 | tf_op jit(solution)/shard_map/ppermute | solution.py:48
  31.3 13.6 %collective-permute-start.3 = (bf16[2,4,64,384]{3,2,1,0:T(8,128)(2,1)}, bf16[2,4,64,384]{3,2,1,0:T(8,128)(2,1)}, u32[]{:S(2)}, u32[]{:S(2)}) collective-permute-start(bf16[2,4,64,384]{3,2,1,0:T(8,128)(2,1)} %pad_maximum_fusion.5), channel_id=1, source_target_pairs={{0,6},{1,7},{2,4},{3,5},{4,2},{5,3},{6,0},{7,1},{8,10},{9,11},{10,... | collective-permute-start | bytes 1179656 | tf_op jit(solution)/shard_map/ppermute | solution.py:48
  31.9 26.3 %collective-permute-start.10 = (bf16[16,64,512]{2,1,0:T(8,128)(2,1)S(1)}, bf16[16,64,512]{2,1,0:T(8,128)(2,1)}, u32[]{:S(2)}, u32[]{:S(2)}) collective-permute-start(bf16[16,64,512]{2,1,0:T(8,128)(2,1)S(1)} %bitcast.159), channel_id=1, source_target_pairs={{0,2},{1,3},{2,0},{3,1},{4,6},{5,7},{6,4},{7,5},{8,14},{9,15},{10,... | collective-permute-start | bytes 3145736 | tf_op jit(solution)/shard_map/ppermute | solution.py:48
  33.0 51.6 %copy-start.1 = (bf16[4,4,64,512]{3,2,1,0:T(8,128)(2,1)}, bf16[4,4,64,512]{3,2,1,0:T(8,128)(2,1)S(1)}, u32[]{:S(2)}) copy-start(bf16[4,4,64,512]{3,2,1,0:T(8,128)(2,1)S(1)} %pad_maximum_fusion.1.refs_8_) | copy-start | bytes 3145732
  33.0 28.0 %collective-permute-start.20 = (bf16[16,64,512]{2,1,0:T(8,128)(2,1)S(1)}, bf16[16,64,512]{2,1,0:T(8,128)(2,1)}, u32[]{:S(2)}, u32[]{:S(2)}) collective-permute-start(bf16[16,64,512]{2,1,0:T(8,128)(2,1)S(1)} %bitcast.161), channel_id=1, source_target_pairs={{0,1},{1,0},{2,3},{3,2},{4,5},{5,4},{6,7},{7,6},{8,73},{9,72},{10,... | collective-permute-start | bytes 3145736 | tf_op jit(solution)/shard_map/ppermute | solution.py:48
  36.0 26.8 %collective-permute-start.11 = (bf16[16,64,512]{2,1,0:T(8,128)(2,1)S(1)}, bf16[16,64,512]{2,1,0:T(8,128)(2,1)}, u32[]{:S(2)}, u32[]{:S(2)}) collective-permute-start(bf16[16,64,512]{2,1,0:T(8,128)(2,1)S(1)} %bitcast.160), channel_id=1, source_target_pairs={{0,6},{1,7},{2,4},{3,5},{4,2},{5,3},{6,0},{7,1},{8,10},{9,11},{10,... | collective-permute-start | bytes 3145736 | tf_op jit(solution)/shard_map/ppermute | solution.py:48
  38.8 45.7 %copy-start.3 = (bf16[3,208,64]{2,1,0:T(8,128)(2,1)}, bf16[3,208,64]{2,1,0:T(8,128)(2,1)S(1)}, u32[]{:S(2)}) copy-start(bf16[3,208,64]{2,1,0:T(8,128)(2,1)S(1)} %copy.5.a_mine) | copy-start | bytes 239620
  44.8 1.4 collective-permute-start.5
  46.0 38.6 %copy-start.2 = (bf16[4,4,64,384]{3,2,1,0:T(8,128)(2,1)}, bf16[4,4,64,384]{3,2,1,0:T(8,128)(2,1)S(1)}, u32[]{:S(2)}) copy-start(bf16[4,4,64,384]{3,2,1,0:T(8,128)(2,1)S(1)} %pad_maximum_fusion.2) | copy-start | bytes 2359300
  46.2 18.9 %collective-permute-start.13 = (bf16[16,64,384]{2,1,0:T(8,128)(2,1)S(1)}, bf16[16,64,384]{2,1,0:T(8,128)(2,1)}, u32[]{:S(2)}, u32[]{:S(2)}) collective-permute-start(bf16[16,64,384]{2,1,0:T(8,128)(2,1)S(1)} %bitcast.163), channel_id=1, source_target_pairs={{0,16},{1,17},{2,18},{3,19},{4,20},{5,21},{6,22},{7,23},{8,56},{9,... | collective-permute-start | bytes 2359304 | tf_op jit(solution)/shard_map/ppermute | solution.py:48
  46.2 20.5 %collective-permute-start.21 = (bf16[16,64,512]{2,1,0:T(8,128)(2,1)S(1)}, bf16[16,64,512]{2,1,0:T(8,128)(2,1)}, u32[]{:S(2)}, u32[]{:S(2)}) collective-permute-start(bf16[16,64,512]{2,1,0:T(8,128)(2,1)S(1)} %bitcast.162), channel_id=1, source_target_pairs={{0,65},{1,64},{2,67},{3,66},{4,69},{5,68},{6,71},{7,70},{8,9},{9,8... | collective-permute-start | bytes 3145736 | tf_op jit(solution)/shard_map/ppermute | solution.py:48
  58.2 16.3 %collective-permute-start.12 = (bf16[16,64,512]{2,1,0:T(8,128)(2,1)}, bf16[16,64,512]{2,1,0:T(8,128)(2,1)}, u32[]{:S(2)}, u32[]{:S(2)}) collective-permute-start(bf16[16,64,512]{2,1,0:T(8,128)(2,1)} %collective-permute-done.10), channel_id=1, source_target_pairs={{0,6},{1,7},{2,4},{3,5},{4,2},{5,3},{6,0},{7,1},{8,10},{9,11},{10,... | collective-permute-start | bytes 3145736 | tf_op jit(solution)/shard_map/ppermute | solution.py:48
  60.9 15.1 %collective-permute-start.22 = (bf16[16,64,512]{2,1,0:T(8,128)(2,1)}, bf16[16,64,512]{2,1,0:T(8,128)(2,1)}, u32[]{:S(2)}, u32[]{:S(2)}) collective-permute-start(bf16[16,64,512]{2,1,0:T(8,128)(2,1)} %collective-permute-done.20), channel_id=1, source_target_pairs={{0,65},{1,64},{2,67},{3,66},{4,69},{5,68},{6,71},{7,70},{8,9},{9,8... | collective-permute-start | bytes 3145736 | tf_op jit(solution)/shard_map/ppermute | solution.py:48
  62.8 13.2 %collective-permute-start.14 = (bf16[16,64,384]{2,1,0:T(8,128)(2,1)S(1)}, bf16[16,64,384]{2,1,0:T(8,128)(2,1)S(1)}, u32[]{:S(2)}, u32[]{:S(2)}) collective-permute-start(bf16[16,64,384]{2,1,0:T(8,128)(2,1)S(1)} %bitcast.164), channel_id=1, source_target_pairs={{0,48},{1,49},{2,50},{3,51},{4,52},{5,53},{6,54},{7,55},{8,24},{9,... | collective-permute-start | bytes 2359304 | tf_op jit(solution)/shard_map/ppermute | solution.py:48
  65.2 19.4 %collective-permute-start.15 = (bf16[16,64,384]{2,1,0:T(8,128)(2,1)}, bf16[16,64,384]{2,1,0:T(8,128)(2,1)}, u32[]{:S(2)}, u32[]{:S(2)}) collective-permute-start(bf16[16,64,384]{2,1,0:T(8,128)(2,1)} %collective-permute-done.13), channel_id=1, source_target_pairs={{0,48},{1,49},{2,50},{3,51},{4,52},{5,53},{6,54},{7,55},{8,24},{9,... | collective-permute-start | bytes 2359304 | tf_op jit(solution)/shard_map/ppermute | solution.py:48
  100.0 2.7 %collective-permute-start.23 = (bf16[2,2,208,512]{3,2,1,0:T(8,128)(2,1)}, bf16[2,2,208,512]{3,2,1,0:T(8,128)(2,1)S(1)}, u32[]{:S(2)}, u32[]{:S(2)}) collective-permute-start(bf16[2,2,208,512]{3,2,1,0:T(8,128)(2,1)} %get-tuple-element.25.mine), channel_id=1, source_target_pairs={{0,8},{1,9},{2,10},{3,11},{4,12},{5,13},{6,14},{7,15},{8,0},{9,1},... | collective-permute-start | bytes 2555912 | tf_op jit(solution)/shard_map/ppermute | solution.py:48
  113.6 13.5 %collective-permute-start.25 = (bf16[16,64,384]{2,1,0:T(8,128)(2,1)}, bf16[16,64,384]{2,1,0:T(8,128)(2,1)S(1)}, u32[]{:S(2)}, u32[]{:S(2)}) collective-permute-start(bf16[16,64,384]{2,1,0:T(8,128)(2,1)} %bitcast.189), channel_id=1, source_target_pairs={{0,6},{1,7},{2,4},{3,5},{4,2},{5,3},{6,0},{7,1},{8,10},{9,11},{10,... | collective-permute-start | bytes 2359304 | tf_op jit(solution)/shard_map/ppermute | solution.py:48
  114.2 16.7 %collective-permute-start.32 = (bf16[16,64,384]{2,1,0:T(8,128)(2,1)}, bf16[16,64,384]{2,1,0:T(8,128)(2,1)S(1)}, u32[]{:S(2)}, u32[]{:S(2)}) collective-permute-start(bf16[16,64,384]{2,1,0:T(8,128)(2,1)} %bitcast.188), channel_id=1, source_target_pairs={{0,48},{1,49},{2,50},{3,51},{4,52},{5,53},{6,54},{7,55},{8,24},{9,... | collective-permute-start | bytes 2359304 | tf_op jit(solution)/shard_map/ppermute | solution.py:48
  116.5 14.7 %collective-permute-start.39 = (bf16[16,64,384]{2,1,0:T(8,128)(2,1)}, bf16[16,64,384]{2,1,0:T(8,128)(2,1)S(1)}, u32[]{:S(2)}, u32[]{:S(2)}) collective-permute-start(bf16[16,64,384]{2,1,0:T(8,128)(2,1)} %bitcast.187), channel_id=1, source_target_pairs={{0,65},{1,64},{2,67},{3,66},{4,69},{5,68},{6,71},{7,70},{8,9},{9,8... | collective-permute-start | bytes 2359304 | tf_op jit(solution)/shard_map/ppermute | solution.py:48
  116.7 24.0 %collective-permute-start.24 = (bf16[16,64,384]{2,1,0:T(8,128)(2,1)}, bf16[16,64,384]{2,1,0:T(8,128)(2,1)S(1)}, u32[]{:S(2)}, u32[]{:S(2)}) collective-permute-start(bf16[16,64,384]{2,1,0:T(8,128)(2,1)} %bitcast.186), channel_id=1, source_target_pairs={{0,6},{1,7},{2,4},{3,5},{4,2},{5,3},{6,0},{7,1},{8,10},{9,11},{10,... | collective-permute-start | bytes 2359304 | tf_op jit(solution)/shard_map/ppermute | solution.py:48
  128.3 16.2 %collective-permute-start.26 = (bf16[16,64,384]{2,1,0:T(8,128)(2,1)S(1)}, bf16[16,64,384]{2,1,0:T(8,128)(2,1)S(1)}, u32[]{:S(2)}, u32[]{:S(2)}) collective-permute-start(bf16[16,64,384]{2,1,0:T(8,128)(2,1)S(1)} %bitcast_add_fusion.2), channel_id=1, source_target_pairs={{0,2},{1,3},{2,0},{3,1},{4,6},{5,7},{6,4},{7,5},{8,14},{9,15},{10,... | collective-permute-start | bytes 2359304 | tf_op jit(solution)/shard_map/ppermute | solution.py:48
  128.4 20.6 %collective-permute-start.31 = (bf16[16,64,384]{2,1,0:T(8,128)(2,1)S(1)}, bf16[16,64,384]{2,1,0:T(8,128)(2,1)S(1)}, u32[]{:S(2)}, u32[]{:S(2)}) collective-permute-start(bf16[16,64,384]{2,1,0:T(8,128)(2,1)S(1)} %bitcast.185), channel_id=1, source_target_pairs={{0,48},{1,49},{2,50},{3,51},{4,52},{5,53},{6,54},{7,55},{8,24},{9,... | collective-permute-start | bytes 2359304 | tf_op jit(solution)/shard_map/ppermute | solution.py:48
  130.8 18.9 %collective-permute-start.38 = (bf16[16,64,384]{2,1,0:T(8,128)(2,1)S(1)}, bf16[16,64,384]{2,1,0:T(8,128)(2,1)S(1)}, u32[]{:S(2)}, u32[]{:S(2)}) collective-permute-start(bf16[16,64,384]{2,1,0:T(8,128)(2,1)S(1)} %bitcast.184), channel_id=1, source_target_pairs={{0,65},{1,64},{2,67},{3,66},{4,69},{5,68},{6,71},{7,70},{8,9},{9,8... | collective-permute-start | bytes 2359304 | tf_op jit(solution)/shard_map/ppermute | solution.py:48
  131.2 17.9 %collective-permute-start.33 = (bf16[16,64,384]{2,1,0:T(8,128)(2,1)S(1)}, bf16[16,64,384]{2,1,0:T(8,128)(2,1)S(1)}, u32[]{:S(2)}, u32[]{:S(2)}) collective-permute-start(bf16[16,64,384]{2,1,0:T(8,128)(2,1)S(1)} %bitcast_add_fusion.1), channel_id=1, source_target_pairs={{0,16},{1,17},{2,18},{3,19},{4,20},{5,21},{6,22},{7,23},{8,56},{9,... | collective-permute-start | bytes 2359304 | tf_op jit(solution)/shard_map/ppermute | solution.py:48
  140.7 18.0 %collective-permute-start.40 = (bf16[16,64,384]{2,1,0:T(8,128)(2,1)S(1)}, bf16[16,64,384]{2,1,0:T(8,128)(2,1)S(1)}, u32[]{:S(2)}, u32[]{:S(2)}) collective-permute-start(bf16[16,64,384]{2,1,0:T(8,128)(2,1)S(1)} %bitcast_add_fusion), channel_id=1, source_target_pairs={{0,1},{1,0},{2,3},{3,2},{4,5},{5,4},{6,7},{7,6},{8,73},{9,72},{10,... | collective-permute-start | bytes 2359304 | tf_op jit(solution)/shard_map/ppermute | solution.py:48
  145.1 16.2 %collective-permute-start.27 = (bf16[2,4,64,384]{3,2,1,0:T(8,128)(2,1)S(1)}, bf16[2,4,64,384]{3,2,1,0:T(8,128)(2,1)S(1)}, u32[]{:S(2)}, u32[]{:S(2)}) collective-permute-start(bf16[2,4,64,384]{3,2,1,0:T(8,128)(2,1)S(1)} %bitcast.175), channel_id=1, source_target_pairs={{0,65},{1,64},{2,67},{3,66},{4,69},{5,68},{6,71},{7,70},{8,9},{9,8... | collective-permute-start | bytes 1179656 | tf_op jit(solution)/shard_map/ppermute | solution.py:48
  149.6 13.9 %collective-permute-start.34 = (bf16[2,4,64,384]{3,2,1,0:T(8,128)(2,1)S(1)}, bf16[2,4,64,384]{3,2,1,0:T(8,128)(2,1)S(1)}, u32[]{:S(2)}, u32[]{:S(2)}) collective-permute-start(bf16[2,4,64,384]{3,2,1,0:T(8,128)(2,1)S(1)} %bitcast.176), channel_id=1, source_target_pairs={{0,6},{1,7},{2,4},{3,5},{4,2},{5,3},{6,0},{7,1},{8,10},{9,11},{10,... | collective-permute-start | bytes 1179656 | tf_op jit(solution)/shard_map/ppermute | solution.py:48
  159.3 11.2 %collective-permute-start.41 = (bf16[2,4,64,384]{3,2,1,0:T(8,128)(2,1)S(1)}, bf16[2,4,64,384]{3,2,1,0:T(8,128)(2,1)S(1)}, u32[]{:S(2)}, u32[]{:S(2)}) collective-permute-start(bf16[2,4,64,384]{3,2,1,0:T(8,128)(2,1)S(1)} %bitcast.177), channel_id=1, source_target_pairs={{0,48},{1,49},{2,50},{3,51},{4,52},{5,53},{6,54},{7,55},{8,24},{9,... | collective-permute-start | bytes 1179656 | tf_op jit(solution)/shard_map/ppermute | solution.py:48
  161.5 9.2 %collective-permute-start.28 = (bf16[4,64,384]{2,1,0:T(8,128)(2,1)S(1)}, bf16[4,64,384]{2,1,0:T(8,128)(2,1)S(1)}, u32[]{:S(2)}, u32[]{:S(2)}) collective-permute-start(bf16[4,64,384]{2,1,0:T(8,128)(2,1)S(1)} %slice_bitcast_fusion.4), channel_id=1, source_target_pairs={{0,1},{1,0},{2,3},{3,2},{4,5},{5,4},{6,7},{7,6},{8,73},{9,72},{10,... | collective-permute-start | bytes 589832 | tf_op jit(solution)/shard_map/ppermute | solution.py:48
  163.7 8.9 %collective-permute-start.35 = (bf16[4,64,384]{2,1,0:T(8,128)(2,1)S(1)}, bf16[4,64,384]{2,1,0:T(8,128)(2,1)S(1)}, u32[]{:S(2)}, u32[]{:S(2)}) collective-permute-start(bf16[4,64,384]{2,1,0:T(8,128)(2,1)S(1)} %slice_bitcast_fusion.2), channel_id=1, source_target_pairs={{0,2},{1,3},{2,0},{3,1},{4,6},{5,7},{6,4},{7,5},{8,14},{9,15},{10,... | collective-permute-start | bytes 589832 | tf_op jit(solution)/shard_map/ppermute | solution.py:48
  170.6 5.7 %collective-permute-start.42 = (bf16[4,64,384]{2,1,0:T(8,128)(2,1)S(1)}, bf16[4,64,384]{2,1,0:T(8,128)(2,1)S(1)}, u32[]{:S(2)}, u32[]{:S(2)}) collective-permute-start(bf16[4,64,384]{2,1,0:T(8,128)(2,1)S(1)} %slice_bitcast_fusion), channel_id=1, source_target_pairs={{0,16},{1,17},{2,18},{3,19},{4,20},{5,21},{6,22},{7,23},{8,56},{9,... | collective-permute-start | bytes 589832 | tf_op jit(solution)/shard_map/ppermute | solution.py:48
  170.7 5.9 %collective-permute-start.29 = (bf16[2,1,64,384]{3,2,1,0:T(8,128)(2,1)S(1)}, bf16[2,1,64,384]{3,2,1,0:T(8,128)(2,1)S(1)}, u32[]{:S(2)}, u32[]{:S(2)}) collective-permute-start(bf16[2,1,64,384]{3,2,1,0:T(8,128)(2,1)S(1)} %slice_bitcast_fusion.10), channel_id=1, source_target_pairs={{0,48},{1,49},{2,50},{3,51},{4,52},{5,53},{6,54},{7,55},{8,24},{9,... | collective-permute-start | bytes 294920 | tf_op jit(solution)/shard_map/ppermute | solution.py:48
  172.6 4.9 %collective-permute-start.36 = (bf16[2,1,64,384]{3,2,1,0:T(8,128)(2,1)S(1)}, bf16[2,1,64,384]{3,2,1,0:T(8,128)(2,1)S(1)}, u32[]{:S(2)}, u32[]{:S(2)}) collective-permute-start(bf16[2,1,64,384]{3,2,1,0:T(8,128)(2,1)S(1)} %slice_bitcast_fusion.8), channel_id=1, source_target_pairs={{0,65},{1,64},{2,67},{3,66},{4,69},{5,68},{6,71},{7,70},{8,9},{9,8... | collective-permute-start | bytes 294920 | tf_op jit(solution)/shard_map/ppermute | solution.py:48
  176.4 5.9 %collective-permute-start.43 = (bf16[2,1,64,384]{3,2,1,0:T(8,128)(2,1)S(1)}, bf16[2,1,64,384]{3,2,1,0:T(8,128)(2,1)S(1)}, u32[]{:S(2)}, u32[]{:S(2)}) collective-permute-start(bf16[2,1,64,384]{3,2,1,0:T(8,128)(2,1)S(1)} %slice_bitcast_fusion.6), channel_id=1, source_target_pairs={{0,6},{1,7},{2,4},{3,5},{4,2},{5,3},{6,0},{7,1},{8,10},{9,11},{10,... | collective-permute-start | bytes 294920 | tf_op jit(solution)/shard_map/ppermute | solution.py:48
  176.7 5.7 %collective-permute-start.30 = (bf16[1,64,384]{2,1,0:T(8,128)(2,1)S(1)}, bf16[1,64,384]{2,1,0:T(8,128)(2,1)S(1)}, u32[]{:S(2)}, u32[]{:S(2)}) collective-permute-start(bf16[1,64,384]{2,1,0:T(8,128)(2,1)S(1)} %slice_bitcast_fusion.16), channel_id=1, source_target_pairs={{0,16},{1,17},{2,18},{3,19},{4,20},{5,21},{6,22},{7,23},{8,56},{9,... | collective-permute-start | bytes 147464 | tf_op jit(solution)/shard_map/ppermute | solution.py:48
  177.6 8.9 %collective-permute-start.37 = (bf16[1,64,384]{2,1,0:T(8,128)(2,1)S(1)}, bf16[1,64,384]{2,1,0:T(8,128)(2,1)S(1)}, u32[]{:S(2)}, u32[]{:S(2)}) collective-permute-start(bf16[1,64,384]{2,1,0:T(8,128)(2,1)S(1)} %slice_bitcast_fusion.14), channel_id=1, source_target_pairs={{0,1},{1,0},{2,3},{3,2},{4,5},{5,4},{6,7},{7,6},{8,73},{9,72},{10,... | collective-permute-start | bytes 147464 | tf_op jit(solution)/shard_map/ppermute | solution.py:48
  182.3 4.2 %collective-permute-start.44 = (bf16[1,64,384]{2,1,0:T(8,128)(2,1)S(1)}, bf16[1,64,384]{2,1,0:T(8,128)(2,1)S(1)}, u32[]{:S(2)}, u32[]{:S(2)}) collective-permute-start(bf16[1,64,384]{2,1,0:T(8,128)(2,1)S(1)} %slice_bitcast_fusion.12), channel_id=1, source_target_pairs={{0,2},{1,3},{2,0},{3,1},{4,6},{5,7},{6,4},{7,5},{8,14},{9,15},{10,... | collective-permute-start | bytes 147464 | tf_op jit(solution)/shard_map/ppermute | solution.py:48
  (13 other events, 144.3 us)
